TPU v7x, 32 devices: a whole 2x2x4 slice. The times are simulated.
32 devices in a mesh: rep: 4 (over x, core), shard: 8 (over z, y).
Axes of the slice: x: 2, y: 2, z: 4, core: 2. Of those that a mesh axis runs over, the one named last changes fastest.
Arguments:
- tokens: bfloat16 [16384, 1024], P(('rep', 'shard')), may hold values from -6 to 6
- cotangent: bfloat16 [16384, 1024], P(('rep', 'shard')), may hold values from -6 to 6
- lengths: int32 [32, 4], P(('rep', 'shard')), may hold values from 0 to 512, as said below
- joint_weight: bfloat16 [1024, 3072], P('shard'), may hold values from -0.1875 to 0.1875
- query_bias: bfloat16 [1024], P('shard'), may hold values from -3 to 3
- value_bias: bfloat16 [1024], P('shard'), may hold values from -3 to 3
- output_weight: bfloat16 [1024, 1024], P('shard'), may hold values from -0.75 to 0.75
- output_bias: bfloat16 [1024], P('shard'), may hold values from -3 to 3
- norm_gain: bfloat16 [1024], P('shard'), may hold values from 0.5 to 1.5
- norm_shift: bfloat16 [1024], P('shard'), may hold values from -3 to 3
- expand_weight: bfloat16 [1024, 4096], P('shard'), may hold values from -0.1875 to 0.1875
- expand_bias: bfloat16 [4096], P('shard'), may hold values from -3 to 3
- reduce_weight: bfloat16 [4096, 1024], P('shard'), may hold values from -0.09375 to 0.09375
- reduce_bias: bfloat16 [1024], P('shard'), may hold values from -3 to 3
- final_gain: bfloat16 [1024], P('shard'), may hold values from 0.5 to 1.5
- final_shift: bfloat16 [1024], P('shard'), may hold values from -3 to 3
Outputs:
- output: bfloat16 [16384, 1024], P(('rep', 'shard'))
- grad_tokens: bfloat16 [16384, 1024], P(('rep', 'shard'))
- grad_joint_weight: float32 [1024, 3072], P('shard')
- grad_query_bias: float32 [1024], P('shard')
- grad_value_bias: float32 [1024], P('shard')
- grad_output_weight: float32 [1024, 1024], P('shard')
- grad_output_bias: float32 [1024], P('shard')
- grad_norm_gain: float32 [1024], P('shard')
- grad_norm_shift: float32 [1024], P('shard')
- grad_expand_weight: float32 [1024, 4096], P('shard')
- grad_expand_bias: float32 [4096], P('shard')
- grad_reduce_weight: float32 [4096, 1024], P('shard')
- grad_reduce_bias: float32 [1024], P('shard')
- grad_final_gain: float32 [1024], P('shard')
- grad_final_shift: float32 [1024], P('shard')
Inputs may be any that keep to these rules, and one draw needn't show every extreme that they name: `lengths`: each row sums to between 256 and 512; slots past the sum are padding; in every draw one row holds a single sequence of 512 tokens.
All inputs are finite; a program needn't handle non-finite values.
Results may differ from a plain program's by a relative error of at most 0.013.
Values may be sent and summed in bfloat16 or wider, within the bound.
A program may use at most 192 MiB of HBM per device.

v0:
```python
import jax
import jax.numpy as jnp
from jax import lax
from jax.sharding import PartitionSpec as P

HEADS = 16


epsilon = 1e-05
mask_fill = -1000000000.0


def layer_norm(inputs, gain_vector, shift_vector):
    centre = inputs - jnp.mean(inputs, axis=-1, keepdims=True)
    variance = jnp.mean(centre * centre, axis=-1, keepdims=True)
    return centre * lax.rsqrt(variance + epsilon) * gain_vector + shift_vector


def gelu_exact(inputs):
    return 0.5 * inputs * (1.0 + jax.scipy.special.erf(inputs * 0.7071067811865476))


def segment_of(length_row, row_count):
    seq_ends = jnp.cumsum(length_row)
    position = jnp.arange(row_count, dtype=jnp.int32)
    return jnp.sum((position[:, None] >= seq_ends[None, :]).astype(jnp.int32), axis=1)


def block_scores(query_block, key_heads, segment_block, segment, score_scale):
    scores = (
        jnp.einsum("qhd,khd->hqk", query_block, key_heads, preferred_element_type=jnp.float32)
        * score_scale
    )
    return jnp.where((segment_block[:, None] == segment[None, :])[None], scores, mask_fill)


def attend_forward(queries, key_rows, values, segment, head_count):
    row_count, model_width = queries.shape
    head_size = model_width // head_count
    block_size = min(512, row_count)
    score_scale = head_size ** (-0.5)
    key_heads = key_rows.reshape(row_count, head_count, head_size)
    value_heads = values.reshape(row_count, head_count, head_size)

    def one_block(state_carry, block_index):
        query_block = queries.reshape(block_size, head_count, head_size)
        scores = block_scores(query_block, key_heads, segment, segment, score_scale)
        row_max = jnp.max(scores, axis=-1, keepdims=True)
        powers = jnp.exp(scores - row_max)
        row_total = jnp.sum(powers, axis=-1, keepdims=True)
        attn_weights = (powers / row_total).astype(jnp.bfloat16)
        context = jnp.einsum(
            "hqk,khd->qhd", attn_weights, value_heads, preferred_element_type=jnp.float32
        )
        log_total = (row_max + jnp.log(row_total))[..., 0]
        return (
            state_carry,
            (context.reshape(block_size, model_width).astype(jnp.bfloat16), log_total),
        )

    _, (context, log_total) = lax.scan(one_block, 0, jnp.arange(row_count // block_size))
    return (context.reshape(row_count, model_width), log_total)


def attend_backward(queries, key_rows, values, segment, log_total, grad_context, head_count):
    row_count, model_width = queries.shape
    head_size = model_width // head_count
    block_size = min(512, row_count)
    score_scale = head_size ** (-0.5)
    key_heads = key_rows.reshape(row_count, head_count, head_size)
    value_heads = values.reshape(row_count, head_count, head_size)

    def one_block(state_carry, block_items):
        grad_keys, grad_values = state_carry
        block_index, block_total = block_items
        query_block = queries.reshape(block_size, head_count, head_size)
        grad_block = grad_context.reshape(block_size, head_count, head_size)
        scores = block_scores(query_block, key_heads, segment, segment, score_scale)
        attn_weights = jnp.exp(scores - block_total[..., None])
        grad_weights = jnp.einsum(
            "qhd,khd->hqk", grad_block, value_heads, preferred_element_type=jnp.float32
        )
        inner = jnp.sum(attn_weights * grad_weights, axis=-1, keepdims=True)
        grad_scores = (attn_weights * (grad_weights - inner)).astype(jnp.bfloat16)
        grad_query = (
            jnp.einsum("hqk,khd->qhd", grad_scores, key_heads, preferred_element_type=jnp.float32)
            * score_scale
        )
        grad_keys = (
            grad_keys
            + jnp.einsum(
                "hqk,qhd->khd", grad_scores, query_block, preferred_element_type=jnp.float32
            )
            * score_scale
        )
        grad_values = grad_values + jnp.einsum(
            "hqk,qhd->khd",
            attn_weights.astype(jnp.bfloat16),
            grad_block,
            preferred_element_type=jnp.float32,
        )
        return ((grad_keys, grad_values), grad_query.reshape(block_size, model_width))

    zero_heads = jnp.zeros((row_count, head_count, head_size), jnp.float32)
    (grad_keys, grad_values), grad_queries = lax.scan(
        one_block, (zero_heads, zero_heads), (jnp.arange(row_count // block_size), log_total)
    )
    return (
        grad_queries.reshape(row_count, model_width),
        grad_keys.reshape(row_count, model_width),
        grad_values.reshape(row_count, model_width),
    )


def on_device(
    tokens,
    cotangent,
    lengths,
    joint_weight,
    query_bias,
    value_bias,
    output_weight,
    output_bias,
    norm_gain,
    norm_shift,
    expand_weight,
    expand_bias,
    reduce_weight,
    reduce_bias,
    final_gain,
    final_shift,
):
    owned = (
        joint_weight,
        query_bias,
        value_bias,
        output_weight,
        output_bias,
        norm_gain,
        norm_shift,
        expand_weight,
        expand_bias,
        reduce_weight,
        reduce_bias,
        final_gain,
        final_shift,
    )
    full_params = (
        lax.all_gather(owned[0], "shard", axis=0, tiled=True),
        lax.all_gather(owned[1], "shard", axis=0, tiled=True),
        lax.all_gather(owned[2], "shard", axis=0, tiled=True),
        lax.all_gather(owned[3], "shard", axis=0, tiled=True),
        lax.all_gather(owned[4], "shard", axis=0, tiled=True),
        lax.all_gather(owned[5], "shard", axis=0, tiled=True),
        lax.all_gather(owned[6], "shard", axis=0, tiled=True),
        lax.all_gather(owned[7], "shard", axis=0, tiled=True),
        lax.all_gather(owned[8], "shard", axis=0, tiled=True),
        lax.all_gather(owned[9], "shard", axis=0, tiled=True),
        lax.all_gather(owned[10], "shard", axis=0, tiled=True),
        lax.all_gather(owned[11], "shard", axis=0, tiled=True),
        lax.all_gather(owned[12], "shard", axis=0, tiled=True),
    )
    row_count, model_width = tokens.shape
    segment = segment_of(lengths[0], row_count)
    live_rows = (segment < lengths.shape[1]).astype(jnp.float32)[:, None]
    joint = jnp.dot(tokens, full_params[0], preferred_element_type=jnp.float32)
    queries = (joint[:, :model_width] + full_params[1].astype(jnp.float32)).astype(jnp.bfloat16)
    key_rows = joint[:, model_width : 2 * model_width].astype(jnp.bfloat16)
    values = (joint[:, 2 * model_width :] + full_params[2].astype(jnp.float32)).astype(jnp.bfloat16)
    context, log_total = attend_forward(queries, key_rows, values, segment, HEADS)
    branch = jnp.dot(context, full_params[3], preferred_element_type=jnp.float32) + full_params[
        4
    ].astype(jnp.float32)
    middle, middle_pull = jax.vjp(
        layer_norm,
        tokens.astype(jnp.float32) + branch,
        full_params[5].astype(jnp.float32),
        full_params[6].astype(jnp.float32),
    )
    middle_low = middle.astype(jnp.bfloat16)
    hidden = jnp.dot(middle_low, full_params[7], preferred_element_type=jnp.float32) + full_params[
        8
    ].astype(jnp.float32)
    active_full, gelu_pull = jax.vjp(gelu_exact, hidden)
    active = active_full.astype(jnp.bfloat16)
    second = jnp.dot(active, full_params[9], preferred_element_type=jnp.float32) + full_params[
        10
    ].astype(jnp.float32)

    def final_norm(inputs, gain_vector, shift_vector):
        return layer_norm(inputs, gain_vector, shift_vector) * live_rows

    output, final_pull = jax.vjp(
        final_norm,
        middle + second,
        full_params[11].astype(jnp.float32),
        full_params[12].astype(jnp.float32),
    )
    back_params = (
        lax.all_gather(owned[0], "shard", axis=0, tiled=True),
        lax.all_gather(owned[1], "shard", axis=0, tiled=True),
        lax.all_gather(owned[2], "shard", axis=0, tiled=True),
        lax.all_gather(owned[3], "shard", axis=0, tiled=True),
        lax.all_gather(owned[4], "shard", axis=0, tiled=True),
        lax.all_gather(owned[5], "shard", axis=0, tiled=True),
        lax.all_gather(owned[6], "shard", axis=0, tiled=True),
        lax.all_gather(owned[7], "shard", axis=0, tiled=True),
        lax.all_gather(owned[8], "shard", axis=0, tiled=True),
        lax.all_gather(owned[9], "shard", axis=0, tiled=True),
        lax.all_gather(owned[10], "shard", axis=0, tiled=True),
        lax.all_gather(owned[11], "shard", axis=0, tiled=True),
        lax.all_gather(owned[12], "shard", axis=0, tiled=True),
    )
    grad_two, grad_final_gain, grad_final_shift = final_pull(cotangent.astype(jnp.float32))
    grad_second = grad_two.astype(jnp.bfloat16)
    grad_reduce_weight = jnp.einsum(
        "tf,td->fd", active, grad_second, preferred_element_type=jnp.float32
    )
    grad_reduce_bias = jnp.sum(grad_second.astype(jnp.float32), axis=0)
    grad_active = jnp.einsum(
        "td,fd->tf", grad_second, back_params[9], preferred_element_type=jnp.float32
    )
    grad_hidden = gelu_pull(grad_active)[0].astype(jnp.bfloat16)
    grad_expand_weight = jnp.einsum(
        "td,tf->df", middle_low, grad_hidden, preferred_element_type=jnp.float32
    )
    grad_expand_bias = jnp.sum(grad_hidden.astype(jnp.float32), axis=0)
    grad_middle = grad_two + jnp.einsum(
        "tf,df->td", grad_hidden, back_params[7], preferred_element_type=jnp.float32
    )
    ffn_grads = (
        grad_expand_weight,
        grad_expand_bias,
        grad_reduce_weight,
        grad_reduce_bias,
        grad_final_gain,
        grad_final_shift,
    )
    grad_one, grad_norm_gain, grad_norm_shift = middle_pull(grad_middle)
    grad_branch = grad_one.astype(jnp.bfloat16)
    grad_output_weight = jnp.einsum(
        "td,te->de", context, grad_branch, preferred_element_type=jnp.float32
    )
    grad_output_bias = jnp.sum(grad_branch.astype(jnp.float32), axis=0)
    grad_context = jnp.einsum(
        "te,de->td", grad_branch, back_params[3], preferred_element_type=jnp.float32
    ).astype(jnp.bfloat16)
    grad_queries, grad_keys, grad_values = attend_backward(
        queries, key_rows, values, segment, log_total, grad_context, HEADS
    )
    grad_joint = jnp.concatenate(
        [
            grad_queries.astype(jnp.bfloat16),
            grad_keys.astype(jnp.bfloat16),
            grad_values.astype(jnp.bfloat16),
        ],
        axis=1,
    )
    grad_query_bias = jnp.sum(grad_joint[:, :model_width].astype(jnp.float32), axis=0)
    grad_value_bias = jnp.sum(grad_joint[:, 2 * model_width :].astype(jnp.float32), axis=0)
    grad_joint_weight = jnp.einsum(
        "td,te->de", tokens, grad_joint, preferred_element_type=jnp.float32
    )
    grad_tokens = (
        grad_one
        + jnp.einsum("te,de->td", grad_joint, back_params[0], preferred_element_type=jnp.float32)
    ).astype(jnp.bfloat16)
    attn_grads = (
        grad_joint_weight,
        grad_query_bias,
        grad_value_bias,
        grad_output_weight,
        grad_output_bias,
        grad_norm_gain,
        grad_norm_shift,
    )
    every_part = lax.psum_scatter(attn_grads + ffn_grads, "shard", scatter_dimension=0, tiled=True)
    every_grad = lax.psum(every_part, "rep")
    attn_grads = every_grad[:7]
    ffn_grads = every_grad[7:]
    return (
        output.astype(jnp.bfloat16),
        grad_tokens,
        attn_grads[0],
        attn_grads[1],
        attn_grads[2],
        attn_grads[3],
        attn_grads[4],
        attn_grads[5],
        attn_grads[6],
        ffn_grads[0],
        ffn_grads[1],
        ffn_grads[2],
        ffn_grads[3],
        ffn_grads[4],
        ffn_grads[5],
    )


def solution(mesh):
    placed = (
        P(("rep", "shard"), None),
        P(("rep", "shard"), None),
        P(("rep", "shard"), None),
        P("shard", None),
        P("shard"),
        P("shard"),
        P("shard", None),
        P("shard"),
        P("shard"),
        P("shard"),
        P("shard", None),
        P("shard"),
        P("shard", None),
        P("shard"),
        P("shard"),
        P("shard"),
    )
    return jax.shard_map(
        on_device,
        mesh=mesh,
        in_specs=placed,
        out_specs=(
            P(("rep", "shard"), None),
            P(("rep", "shard"), None),
            P("shard", None),
            P("shard"),
            P("shard"),
            P("shard", None),
            P("shard"),
            P("shard"),
            P("shard"),
            P("shard", None),
            P("shard"),
            P("shard", None),
            P("shard"),
            P("shard"),
            P("shard"),
        ),
        check_vma=False,
    )
```

profile of v0, /device:TPU:0, one launch (start us, length us, event | category | flops | bytes accessed | tf_op | source)
XLA Modules:
  0.0 1461.9 jit_solution(7140990105467277821)
XLA Ops:
  10.2 22.3 %all-gather.1 = bf16[8,1,128]{2,1,0:T(2,128)(2,1)S(1)} all-gather(bf16[1,1,128]{2,1,0:T(2,128)(2,1)S(1)} %bitcast.103), channel_id=1, replica_groups=mesh['rep'=4,'shard'=8] {'shard'}, dimensions={0}, use_global_device_ids=true | all-gather | bytes 2304 | tf_op jit(solution)/shard_map/all_gather | solution.py:150
  32.5 16.5 %all-gather = bf16[8,1,128]{2,1,0:T(2,128)(2,1)S(1)} all-gather(bf16[1,1,128]{2,1,0:T(2,128)(2,1)S(1)} %bitcast.104), channel_id=1, replica_groups=mesh['rep'=4,'shard'=8] {'shard'}, dimensions={0}, use_global_device_ids=true | all-gather | bytes 2304 | tf_op jit(solution)/shard_map/all_gather | solution.py:151
  49.0 18.3 %all-gather.2 = bf16[8,1,128]{2,1,0:T(2,128)(2,1)S(1)} all-gather(bf16[1,1,128]{2,1,0:T(2,128)(2,1)S(1)} %bitcast.105), channel_id=1, replica_groups=mesh['rep'=4,'shard'=8] {'shard'}, dimensions={0}, use_global_device_ids=true | all-gather | bytes 2304 | tf_op jit(solution)/shard_map/all_gather | solution.py:153
  67.2 16.5 %all-gather.3 = bf16[8,1,128]{2,1,0:T(2,128)(2,1)S(1)} all-gather(bf16[1,1,128]{2,1,0:T(2,128)(2,1)S(1)} %bitcast.106), channel_id=1, replica_groups=mesh['rep'=4,'shard'=8] {'shard'}, dimensions={0}, use_global_device_ids=true | all-gather | bytes 2304 | tf_op jit(solution)/shard_map/all_gather | solution.py:154
  84.4 18.1 %all-gather.4 = bf16[8,1,128]{2,1,0:T(2,128)(2,1)S(1)} all-gather(bf16[1,1,128]{2,1,0:T(2,128)(2,1)S(1)} %bitcast.107), channel_id=1, replica_groups=mesh['rep'=4,'shard'=8] {'shard'}, dimensions={0}, use_global_device_ids=true | all-gather | bytes 2304 | tf_op jit(solution)/shard_map/all_gather | solution.py:155
  103.1 16.4 %all-gather.6 = bf16[8,1,128]{2,1,0:T(2,128)(2,1)S(1)} all-gather(bf16[1,1,128]{2,1,0:T(2,128)(2,1)S(1)} %bitcast.108), channel_id=1, replica_groups=mesh['rep'=4,'shard'=8] {'shard'}, dimensions={0}, use_global_device_ids=true | all-gather | bytes 2304 | tf_op jit(solution)/shard_map/all_gather | solution.py:159
  120.1 17.9 %all-gather.7 = bf16[8,1,128]{2,1,0:T(2,128)(2,1)S(1)} all-gather(bf16[1,1,128]{2,1,0:T(2,128)(2,1)S(1)} %bitcast.109), channel_id=1, replica_groups=mesh['rep'=4,'shard'=8] {'shard'}, dimensions={0}, use_global_device_ids=true | all-gather | bytes 2304 | tf_op jit(solution)/shard_map/all_gather | solution.py:160
  138.1 16.6 %all-gather.8 = bf16[8,1,128]{2,1,0:T(2,128)(2,1)S(1)} all-gather(bf16[1,1,128]{2,1,0:T(2,128)(2,1)S(1)} %bitcast.110), channel_id=1, replica_groups=mesh['rep'=4,'shard'=8] {'shard'}, dimensions={0}, use_global_device_ids=true | all-gather | bytes 2304 | tf_op jit(solution)/shard_map/all_gather | solution.py:161
  155.2 26.2 %all-gather.5 = bf16[8,1,512]{2,1,0:T(2,128)(2,1)S(1)} all-gather(bf16[1,1,512]{2,1,0:T(2,128)(2,1)S(1)} %reshape.221), channel_id=1, replica_groups=mesh['rep'=4,'shard'=8] {'shard'}, dimensions={0}, use_global_device_ids=true | all-gather | bytes 9216 | tf_op jit(solution)/shard_map/all_gather | solution.py:157
  183.3 5.5 fusion.28
  188.9 1.6 fusion.6
  191.6 1.5 copy.62
  193.2 7.5 fusion.25
  200.7 8.3 fusion
  208.9 9.0 fusion.11
  217.9 3.5 fusion.26
  221.9 65.8 %all-gather.18.cloned.1.call-done = bf16[1024,4096]{1,0:T(8,128)(2,1)} async-done(((bf16[128,4096]{1,0:T(8,128)(2,1)}), bf16[1024,4096]{1,0:T(8,128)(2,1)}) %all-gather.18.cloned.1.call-update) | async-done | bytes 8388624 | tf_op jit(solution)/shard_map/all_gather | solution.py:156
  287.7 10.6 multiply_convert_fusion.1
  298.3 114.5 %all-gather.20.cloned.1.call-done = bf16[4096,1024]{1,0:T(8,128)(2,1)} async-done(((bf16[512,1024]{1,0:T(8,128)(2,1)}), bf16[4096,1024]{1,0:T(8,128)(2,1)}) %all-gather.20.cloned.1.call-update) | async-done | bytes 8388624 | tf_op jit(solution)/shard_map/all_gather | solution.py:158
  412.8 8.8 fusion.27
  422.8 1.5 multiply_reduce_fusion.1
  424.3 2.0 fusion.24
  426.6 13.9 convert_reduce_fusion
  440.6 8.2 multiply_reduce_fusion.2
  449.5 1.3 copy-done.5
  452.6 3.3 fusion.29
  457.5 3.5 convolution_convert_fusion
  461.0 2.5 copy.66
  463.5 16.9 %multiply_reduce_fusion = (f32[16,512]{1,0:T(8,128)}, f32[16,512,512]{1,2,0:T(8,128)}) fusion(f32[16,512,512]{1,2,0:T(8,128)} %get-tuple-element.168, f32[16,512]{1,0:T(8,128)} %log_add_fusion, bf16[512,16,64]{0,2,1:T(8,128)(2,1)} %bitcast.74, bf16[512,16,64]{0,2,1:T(8,128)(2,1)} %bitcast.77), kind=kOutput, calls=%fused_computation.1 | convolution fusion | flops 549445632 | bytes 35717120 | tf_op jit(solution)/shard_map/while/body/eval_jaxpr/qhd,khd->hqk/dot_general | solution.py:80
  480.4 10.8 multiply_convert_fusion
  491.1 6.6 multiply_convert_fusion.2
  497.7 1.5 convert_reduce_fusion.4
  499.4 9.1 convert_reduce_fusion.3
  509.5 10.0 convolution_bitcast_fusion
  519.5 1.5 copy-done.2
  521.0 11.1 fusion.19
  532.2 1.2 copy-done.18
  533.3 10.5 fusion.30
  544.0 209.8 %reduce-scatter.5.cloned.1.call-done = f32[128,3072]{0,1:T(8,128)} async-done(((f32[1024,3072]{0,1:T(8,128)}), f32[128,3072]{0,1:T(8,128)}) %reduce-scatter.5.cloned.1.call-update) | async-done | bytes 1572880 | tf_op jit(solution)/shard_map/reduce_scatter | solution.py:277
  753.7 286.0 %reduce-scatter.9.cloned.1.call-done = f32[128,4096]{1,0:T(8,128)} async-done(((f32[1024,4096]{1,0:T(8,128)}), f32[128,4096]{1,0:T(8,128)}) %reduce-scatter.9.cloned.1.call-update) | async-done | bytes 2097168 | tf_op jit(solution)/shard_map/reduce_scatter | solution.py:277
  1039.7 285.5 %reduce-scatter.11.cloned.1.call-done = f32[512,1024]{1,0:T(8,128)} async-done(((f32[4096,1024]{1,0:T(8,128)}), f32[512,1024]{1,0:T(8,128)}) %reduce-scatter.11.cloned.1.call-update) | async-done | bytes 2097168 | tf_op jit(solution)/shard_map/reduce_scatter | solution.py:277
  1327.9 35.7 %all-reduce.9 = (f32[1024]{0:T(1024)S(1)}, f32[1024]{0:T(1024)S(1)}, f32[1024]{0:T(1024)S(1)}, f32[1024]{0:T(1024)S(1)}, f32[1024]{0:T(1024)S(1)}, /*index=5*/f3...) all-reduce(f32[1024]{0:T(1024)S(1)} %reduce_sum.230, ...), channel_id=3, replica_groups=mesh['rep'=4,'shard'=8] {'shard'}, use_global_device_ids=true, to_apply=%region_16.17.clone | all-reduce | flops 12288 | bytes 98304
  1364.3 7.4 all-reduce.10
  1371.7 8.1 add_convert_fusion.1
  1379.7 67.7 %all-reduce.14.cloned.1.call-done = (f32[128,3072]{0,1:T(8,128)}, f32[128,1024]{1,0:T(8,128)}, f32[128,4096]{1,0:T(8,128)}, f32[512,1024]{1,0:T(8,128)}) async-done(((f32[128,3072]{0,1:T(8,128)}, f32[128,1024]{1,0:T(8,128)}, f32[128,4096]{1,0:T(8,128)}, f32[512,1024]{1,0:T(8,128)}), (f32[128,3072]{0,1:T(8,128)}, f32[128,1024]{1,0:T(8,128)}, f32[128,4096]{1,0:T(8,128)}, ...) | async-done | bytes 6291472 | tf_op jit(solution)/shard_map/psum | solution.py:278
  1447.5 3.2 copy.70
  1451.4 1.3 copy.80
  1453.8 1.3 copy.81
  (186 shorter events, 19.5 us)
Async XLA Ops:
  7.2 3.0 copy-start.44
  7.2 3.0 copy-start.45
  7.2 25.2 %copy-start.46 = (bf16[128]{0:T(256)(128)(2,1)S(1)}, bf16[128]{0:T(256)(128)(2,1)}, u32[]{:S(2)}) copy-start(bf16[128]{0:T(256)(128)(2,1)} %param.21) | copy-start | bytes 772
  7.2 41.7 %copy-start.47 = (bf16[128]{0:T(256)(128)(2,1)S(1)}, bf16[128]{0:T(256)(128)(2,1)}, u32[]{:S(2)}) copy-start(bf16[128]{0:T(256)(128)(2,1)} %param.23) | copy-start | bytes 772
  7.2 60.0 %copy-start.48 = (bf16[128]{0:T(256)(128)(2,1)S(1)}, bf16[128]{0:T(256)(128)(2,1)}, u32[]{:S(2)}) copy-start(bf16[128]{0:T(256)(128)(2,1)} %param.24) | copy-start | bytes 772
  7.2 77.2 %copy-start.49 = (bf16[128]{0:T(256)(128)(2,1)S(1)}, bf16[128]{0:T(256)(128)(2,1)}, u32[]{:S(2)}) copy-start(bf16[128]{0:T(256)(128)(2,1)} %param.25) | copy-start | bytes 772
  7.2 95.9 %copy-start.50 = (bf16[128]{0:T(256)(128)(2,1)S(1)}, bf16[128]{0:T(256)(128)(2,1)}, u32[]{:S(2)}) copy-start(bf16[128]{0:T(256)(128)(2,1)} %param.29) | copy-start | bytes 772
  7.3 112.9 %copy-start.51 = (bf16[128]{0:T(256)(128)(2,1)S(1)}, bf16[128]{0:T(256)(128)(2,1)}, u32[]{:S(2)}) copy-start(bf16[128]{0:T(256)(128)(2,1)} %param.30) | copy-start | bytes 772
  7.3 130.8 %copy-start.52 = (bf16[128]{0:T(256)(128)(2,1)S(1)}, bf16[128]{0:T(256)(128)(2,1)}, u32[]{:S(2)}) copy-start(bf16[128]{0:T(256)(128)(2,1)} %param.31) | copy-start | bytes 772
  7.3 174.8 %copy-start.53 = (s32[1,4]{1,0:T(1,128)S(1)}, s32[1,4]{1,0:T(1,128)}, u32[]{:S(2)}) copy-start(s32[1,4]{1,0:T(1,128)} %param.18) | copy-start | bytes 52
  7.3 176.0 %copy-start.20 = (bf16[512,1024]{1,0:T(8,128)(2,1)S(1)}, bf16[512,1024]{1,0:T(8,128)(2,1)}, u32[]{:S(2)}) copy-start(bf16[512,1024]{1,0:T(8,128)(2,1)} %param.16) | copy-start | bytes 3145732
  7.3 176.0 %all-gather.14.cloned.1.call-start = ((), (), s32[]{:S(2)}) async-start(), calls=%async_computation.4 | async-start | bytes 7077888 | tf_op jit(solution)/shard_map/all_gather | solution.py:149
  8.0 209.9 %all-gather.16.cloned.1.call-start = ((), (), s32[]{:S(2)}) async-start(), calls=%async_computation.5 | async-start | bytes 2359296 | tf_op jit(solution)/shard_map/all_gather | solution.py:152
  8.8 278.9 %all-gather.18.cloned.1.call-start = ((), (), s32[]{:S(2)}) async-start(), calls=%async_computation.6 | async-start | bytes 9437184 | tf_op jit(solution)/shard_map/all_gather | solution.py:156
  9.5 403.3 %all-gather.20.cloned.1.call-start = ((), (), s32[]{:S(2)}) async-start(), calls=%async_computation.7 | async-start | bytes 9437184 | tf_op jit(solution)/shard_map/all_gather | solution.py:158
  10.1 533.9 %reduce-scatter.7.cloned.1.call-start = ((), (), s32[]{:S(2)}) async-start(), calls=%async_computation.9 | async-start | bytes 4718592 | tf_op jit(solution)/shard_map/reduce_scatter | solution.py:277
  191.1 9.6 copy-start.3
  193.2 15.8 %copy-start.7 = (bf16[512,1024]{0,1:T(8,128)(2,1)}, bf16[512,1024]{0,1:T(8,128)(2,1)S(1)}, u32[]{:S(2)}) copy-start(bf16[512,1024]{0,1:T(8,128)(2,1)S(1)} %copy.62) | copy-start | bytes 3145732
  221.5 227.3 %copy-start.1 = (f32[512,1024]{1,0:T(8,128)}, f32[512,1024]{1,0:T(8,128)S(1)}, u32[]{:S(2)}) copy-start(f32[512,1024]{1,0:T(8,128)S(1)} %get-tuple-element.170) | copy-start | bytes 6291460
  221.5 66.2 %copy-start.31 = (f32[8,1,512]{2,1,0:T(1,128)S(1)}, f32[8,1,512]{2,1,0:T(1,128)}, u32[]{:S(2)}) copy-start(f32[8,1,512]{2,1,0:T(1,128)} %convert_element_type.194) | copy-start | bytes 49156
  221.5 66.2 %copy-start.32 = (f32[8,1,128]{2,1,0:T(1,128)S(1)}, f32[8,1,128]{2,1,0:T(1,128)}, u32[]{:S(2)}) copy-start(f32[8,1,128]{2,1,0:T(1,128)} %convert_element_type.192) | copy-start | bytes 12292
  221.5 66.2 %copy-start.41 = (f32[8,1,128]{2,1,0:T(1,128)S(1)}, f32[8,1,128]{2,1,0:T(1,128)}, u32[]{:S(2)}) copy-start(f32[8,1,128]{2,1,0:T(1,128)} %convert_element_type.193) | copy-start | bytes 12292
  221.5 227.2 %copy-start.25 = (f32[512]{0:T(512)}, f32[512]{0:T(512)S(1)}, u32[]{:S(2)}) copy-start(f32[512]{0:T(512)S(1)} %broadcast_multiply_fusion.1) | copy-start | bytes 6148
  221.9 226.9 %copy-start.35 = (f32[512]{0:T(512)}, f32[512]{0:T(512)S(1)}, u32[]{:S(2)}) copy-start(f32[512]{0:T(512)S(1)} %fusion.15) | copy-start | bytes 6148
  287.7 125.1 %copy-start.43 = (f32[8,1,128]{2,1,0:T(1,128)S(1)}, f32[8,1,128]{2,1,0:T(1,128)}, u32[]{:S(2)}) copy-start(f32[8,1,128]{2,1,0:T(1,128)} %convert_element_type.195) | copy-start | bytes 12292
  426.4 14.2 slice-start.4
  426.6 13.9 copy-start.17
  426.6 13.9 slice-start.5
  449.5 3.1 copy-start.22
  449.5 6.4 copy-start.37
  456.0 297.8 %reduce-scatter.5.cloned.1.call-start = ((), (), s32[]{:S(2)}) async-start(), calls=%async_computation.8 | async-start | bytes 14155776 | tf_op jit(solution)/shard_map/reduce_scatter | solution.py:277
  463.5 16.9 %slice-start = ((s8[16777216]{0:T(1024)(128)(4,1)}), s8[4194304]{0:T(1024)(128)(4,1)S(1)}, s32[]{:S(2)}) async-start(s8[16777216]{0:T(1024)(128)(4,1)} %bitcast.68), calls=%async_computation.13 | async-start | bytes 8388608
  463.5 16.9 %slice-start.1 = ((s8[16777216]{0:T(1024)(128)(4,1)}), s8[4194304]{0:T(1024)(128)(4,1)S(1)}, s32[]{:S(2)}) async-start(s8[16777216]{0:T(1024)(128)(4,1)} %bitcast.68), calls=%async_computation.14 | async-start | bytes 8388608
  463.5 16.9 %slice-start.2 = ((s8[16777216]{0:T(1024)(128)(4,1)}), s8[4194304]{0:T(1024)(128)(4,1)S(1)}, s32[]{:S(2)}) async-start(s8[16777216]{0:T(1024)(128)(4,1)} %bitcast.68), calls=%async_computation.15 | async-start | bytes 8388608
  463.5 16.9 %slice-start.3 = ((s8[16777216]{0:T(1024)(128)(4,1)}), s8[4194304]{0:T(1024)(128)(4,1)S(1)}, s32[]{:S(2)}) async-start(s8[16777216]{0:T(1024)(128)(4,1)} %bitcast.68), calls=%async_computation.16 | async-start | bytes 8388608
  491.1 6.6 copy-start
  497.7 10.8 copy-start.15
  499.4 9.1 copy-start.9
  499.4 10.1 copy-start.21
  519.5 520.2 %reduce-scatter.9.cloned.1.call-start = ((), (), s32[]{:S(2)}) async-start(), calls=%async_computation.10 | async-start | bytes 18874368 | tf_op jit(solution)/shard_map/reduce_scatter | solution.py:277
  532.1 793.1 %reduce-scatter.11.cloned.1.call-start = ((), (), s32[]{:S(2)}) async-start(), calls=%async_computation.11 | async-start | bytes 18874368 | tf_op jit(solution)/shard_map/reduce_scatter | solution.py:277
  543.9 903.6 %all-reduce.14.cloned.1.call-start = ((), (), s32[]{:S(2)}) async-start(), calls=%async_computation.12 | async-start | bytes 12582912 | tf_op jit(solution)/shard_map/psum | solution.py:278
  1325.2 2.7 copy-start.39
  1325.3 46.4 %copy-start.6 = (f32[512,1024]{1,0:T(8,128)S(1)}, f32[512,1024]{1,0:T(8,128)}, u32[]{:S(2)}) copy-start(f32[512,1024]{1,0:T(8,128)} %copy-done.5) | copy-start | bytes 6291460
  1325.3 46.4 %copy-start.10 = (bf16[16,64,512]{2,1,0:T(8,128)(2,1)S(1)}, bf16[16,64,512]{2,1,0:T(8,128)(2,1)}, u32[]{:S(2)}) copy-start(bf16[16,64,512]{2,1,0:T(8,128)(2,1)} %copy-done.9) | copy-start | bytes 3145732
  1325.3 46.4 %copy-start.38 = (f32[512]{0:T(512)S(1)}, f32[512]{0:T(512)}, u32[]{:S(2)}) copy-start(f32[512]{0:T(512)} %copy-done.37) | copy-start | bytes 6148
  1447.5 3.2 copy-start.23
  1447.5 4.0 copy-start.13
  (22 other events, 39.4 us)
Sparse Core Ops, SparseCore 0:
  10.3 101.9 all-gather.13
  114.5 47.5 all-gather.15
  164.2 123.4 all-gather.17
  289.7 123.1 all-gather.19
  456.1 86.2 reduce-scatter.6
  546.3 207.4 reduce-scatter.4
  758.0 281.6 reduce-scatter.8
  1043.5 281.6 reduce-scatter.10
  1328.0 119.4 all-reduce.13
where the time goes:
time: 1470 us; the launch traced here: 1460 us
  waiting for transfers between devices  1030 us (70%)
  blocking collectives  212 us (14%)
  matrix products  147 us (10%)
  other arithmetic  31.5 us (2%)
  local copies, waits for them, and re-layouts  22.7 us (2%)
  between operations  16 us (1%)
    reduce_scatter x4, waiting for transfers between devices, on_device(): lax.psum_scatter(attn_grads + ffn_grads, 'shard', scatter_dimension=0, ti...  781 us
    all_gather x1, waiting for transfers between devices, on_device(): lax.all_gather(owned[9], 'shard', axis=0, tiled=True)  115 us
    psum x1, waiting for transfers between devices, on_device(): every_grad = lax.psum(every_part, 'rep')  67.7 us
    all_gather x1, waiting for transfers between devices, on_device(): lax.all_gather(owned[7], 'shard', axis=0, tiled=True)  65.8 us
    unnamed x1, blocking collectives  35.7 us
  transfers between devices with their start and end apart: 9, of which 6 were waited for; matrix products, arithmetic and copies ran while one was open for 10% of the time, Pallas kernels for 0%

commit v1 on v0

--- a/solution.py
+++ b/solution.py
@@ -1,3 +1,5 @@
+import functools
+
 import jax
 import jax.numpy as jnp
 from jax import lax
@@ -112,7 +114,181 @@
     )
 
 
+def flip_pairs(rep_count, shard_count, rep_bit, shard_bit):
+    pairs = []
+    for rep in range(rep_count):
+        for shard in range(shard_count):
+            to_rep = rep ^ rep_bit[rep % 2]
+            to_shard = shard ^ shard_bit[rep % 2]
+            pairs.append((rep * shard_count + shard, to_rep * shard_count + to_shard))
+    return pairs
+
+
+class Links:
+    def __init__(self, mesh):
+        rep_count, shard_count = mesh.shape["rep"], mesh.shape["shard"]
+        self.rep_count, self.shard_count = rep_count, shard_count
+        self.shard_bits = shard_count.bit_length() - 1
+
+        def pairs(rep_bit, shard_bit):
+            return flip_pairs(rep_count, shard_count, rep_bit, shard_bit)
+
+        self.core = pairs((1, 1), (0, 0))
+        self.x = pairs((2, 2), (0, 0))
+        self.first = pairs((2, 0), (0, 1))
+        self.second = pairs((0, 2), (1, 0))
+        self.bits = [pairs((0, 0), (1 << b, 1 << b)) for b in range(self.shard_bits)]
+
+    def send(self, array, pairs):
+        return lax.ppermute(array, ("rep", "shard"), pairs)
+
+
+def after(array, marker):
+    if marker is None:
+        return array
+    return lax.optimization_barrier((array, marker))[0]
+
+
+def take(array, index, axis):
+    return lax.dynamic_index_in_dim(array, index, axis, keepdims=False)
+
+
+def put_pair(mine, other, bit, axis):
+    return jnp.where(bit == 0, jnp.stack([mine, other], axis), jnp.stack([other, mine], axis))
+
+
+def place():
+    rep, shard = lax.axis_index("rep"), lax.axis_index("shard")
+    return rep % 2, rep // 2, shard
+
+
+def gather_weight(links, own, marks):
+    core, x, shard = place()
+    rows, width = own.shape
+    quarter = rows // 4
+    piece = take(take(own.reshape(2, 2, quarter, width), x, 0), core, 0)
+    new_marks = []
+    high = links.shard_bits - 1
+    step = 0
+
+    def mark_of(i):
+        return marks[i] if marks else None
+
+    part = piece[None]
+    for b in range(high, 0, -1):
+        got = links.send(after(part, mark_of(step)), links.bits[b])
+        new_marks.append(got)
+        bit = (shard >> b) % 2
+        part = put_pair(part, got, bit, 1)
+        part = part.reshape(-1, quarter, width)
+        step += 1
+    y = shard % 2
+    final_q = y * 2 + x
+    final = part
+    mid = links.send(after(final, mark_of(step)), links.second)
+    new_marks.append(mid)
+    step += 1
+    other_final = links.send(after(final, mark_of(step)), links.first)
+    other_mid = links.send(mid, links.first)
+    new_marks.append(other_mid)
+    step += 1
+    mid_q = jnp.where(core == 0, final_q ^ 2, final_q ^ 1)
+    of_q = jnp.where(core == 0, final_q ^ 1, final_q ^ 2)
+    om_q = 3 - final_q
+    pieces = [final, mid, other_final, other_mid]
+    far = [links.send(piece, links.core) for piece in pieces]
+    whole = jnp.zeros((part.shape[0], 4, 2, quarter, width), own.dtype)
+    zero = jnp.int32(0)
+    for block, q in zip(pieces, (final_q, mid_q, of_q, om_q)):
+        whole = lax.dynamic_update_slice(
+            whole, block[:, None, None], (zero, q, core, zero, zero)
+        )
+    for block, q in zip(far, (final_q, of_q, mid_q, om_q)):
+        whole = lax.dynamic_update_slice(
+            whole, block[:, None, None], (zero, q, 1 - core, zero, zero)
+        )
+    return whole.reshape(rows * links.shard_count, width), new_marks
+
+
+def add_low(mine, got):
+    return (mine.astype(jnp.float32) + got.astype(jnp.float32)).astype(jnp.bfloat16)
+
+
+def reduce_weight_grad(links, grad, marks):
+    core, x, shard = place()
+    total_rows, width = grad.shape
+    rows = total_rows // links.shard_count
+    quarter = rows // 4
+    lead = links.shard_count // 2
+    y = shard % 2
+    view = grad.reshape(lead, 4, 2, quarter, width)
+    final_q = y * 2 + x
+    new_marks = []
+
+    def mark_of(i):
+        return marks[i] if marks else None
+
+    mid_q = jnp.where(core == 0, final_q ^ 2, final_q ^ 1)
+    of_q = jnp.where(core == 0, final_q ^ 1, final_q ^ 2)
+    om_q = 3 - final_q
+    order = (om_q, mid_q, of_q, final_q)
+    far_order = (om_q, of_q, mid_q, final_q)
+
+    def piece_of(q, c):
+        zero = jnp.int32(0)
+        block = lax.dynamic_slice(view, (zero, q, c, zero, zero), (lead, 1, 1, quarter, width))
+        return block.reshape(lead, quarter, width)
+
+    sums = []
+    for q, far_q in zip(order, far_order):
+        got = links.send(after(piece_of(far_q, 1 - core), mark_of(0)), links.core)
+        sums.append(add_low(piece_of(q, core), got))
+    new_marks.append(got)
+    send_mid, mid, send_final, final = sums
+    got_mid = links.send(after(send_mid, mark_of(1)), links.first)
+    mid = add_low(mid, got_mid)
+    got_final = links.send(after(send_final, got_mid), links.first)
+    new_marks.append(got_final)
+    got = links.send(after(mid, mark_of(2)), links.second)
+    new_marks.append(got)
+    total = (final.astype(jnp.float32) + got_final.astype(jnp.float32) + got.astype(jnp.float32)).astype(
+        jnp.bfloat16
+    )
+    step = 3
+    for b in range(1, links.shard_bits):
+        bit = (shard >> b) % 2
+        pairs = total.reshape(-1, 2, quarter, width)
+        got = links.send(after(take(pairs, 1 - bit, 1), mark_of(step)), links.bits[b])
+        new_marks.append(got)
+        total = add_low(take(pairs, bit, 1), got)
+        step += 1
+    total = total.reshape(quarter, width)
+    both_x = put_pair(total, links.send(after(total, mark_of(step)), links.x), x, 0)
+    new_marks.append(both_x)
+    both = put_pair(both_x, links.send(both_x, links.core), core, 1)
+    return both.reshape(rows, width).astype(jnp.float32), new_marks
+
+
+def gather_small(links, own):
+    _, _, shard = place()
+    part = own[None]
+    for b in range(links.shard_bits):
+        got = links.send(part, links.bits[b])
+        bit = (shard >> b) % 2
+        part = jnp.where(
+            bit == 0, jnp.concatenate([part, got], 0), jnp.concatenate([got, part], 0)
+        )
+    return part
+
+
+def sum_small(links, vector):
+    for pairs in [links.core, links.x] + links.bits:
+        vector = vector + links.send(vector, pairs)
+    return vector
+
+
 def on_device(
+    links,
     tokens,
     cotangent,
     lengths,
@@ -145,21 +321,18 @@
         final_gain,
         final_shift,
     )
-    full_params = (
-        lax.all_gather(owned[0], "shard", axis=0, tiled=True),
-        lax.all_gather(owned[1], "shard", axis=0, tiled=True),
-        lax.all_gather(owned[2], "shard", axis=0, tiled=True),
-        lax.all_gather(owned[3], "shard", axis=0, tiled=True),
-        lax.all_gather(owned[4], "shard", axis=0, tiled=True),
-        lax.all_gather(owned[5], "shard", axis=0, tiled=True),
-        lax.all_gather(owned[6], "shard", axis=0, tiled=True),
-        lax.all_gather(owned[7], "shard", axis=0, tiled=True),
-        lax.all_gather(owned[8], "shard", axis=0, tiled=True),
-        lax.all_gather(owned[9], "shard", axis=0, tiled=True),
-        lax.all_gather(owned[10], "shard", axis=0, tiled=True),
-        lax.all_gather(owned[11], "shard", axis=0, tiled=True),
-        lax.all_gather(owned[12], "shard", axis=0, tiled=True),
-    )
+    small = gather_small(links, jnp.concatenate([param for param in owned if param.ndim == 1]))
+    marks = None
+    full = []
+    start = 0
+    for param in owned:
+        if param.ndim == 1:
+            full.append(small[:, start : start + param.shape[0]].reshape(-1))
+            start += param.shape[0]
+        else:
+            whole, marks = gather_weight(links, param, marks)
+            full.append(whole)
+    full_params = tuple(full)
     row_count, model_width = tokens.shape
     segment = segment_of(lengths[0], row_count)
     live_rows = (segment < lengths.shape[1]).astype(jnp.float32)[:, None]
@@ -196,37 +369,25 @@
         full_params[11].astype(jnp.float32),
         full_params[12].astype(jnp.float32),
     )
-    back_params = (
-        lax.all_gather(owned[0], "shard", axis=0, tiled=True),
-        lax.all_gather(owned[1], "shard", axis=0, tiled=True),
-        lax.all_gather(owned[2], "shard", axis=0, tiled=True),
-        lax.all_gather(owned[3], "shard", axis=0, tiled=True),
-        lax.all_gather(owned[4], "shard", axis=0, tiled=True),
-        lax.all_gather(owned[5], "shard", axis=0, tiled=True),
-        lax.all_gather(owned[6], "shard", axis=0, tiled=True),
-        lax.all_gather(owned[7], "shard", axis=0, tiled=True),
-        lax.all_gather(owned[8], "shard", axis=0, tiled=True),
-        lax.all_gather(owned[9], "shard", axis=0, tiled=True),
-        lax.all_gather(owned[10], "shard", axis=0, tiled=True),
-        lax.all_gather(owned[11], "shard", axis=0, tiled=True),
-        lax.all_gather(owned[12], "shard", axis=0, tiled=True),
-    )
+    back_params = full_params
     grad_two, grad_final_gain, grad_final_shift = final_pull(cotangent.astype(jnp.float32))
     grad_second = grad_two.astype(jnp.bfloat16)
     grad_reduce_weight = jnp.einsum(
         "tf,td->fd", active, grad_second, preferred_element_type=jnp.float32
-    )
+    ).astype(jnp.bfloat16)
     grad_reduce_bias = jnp.sum(grad_second.astype(jnp.float32), axis=0)
+    sum_reduce, marks = reduce_weight_grad(links, grad_reduce_weight, None)
     grad_active = jnp.einsum(
-        "td,fd->tf", grad_second, back_params[9], preferred_element_type=jnp.float32
+        "td,fd->tf", after(grad_second, grad_reduce_weight), back_params[9], preferred_element_type=jnp.float32
     )
     grad_hidden = gelu_pull(grad_active)[0].astype(jnp.bfloat16)
     grad_expand_weight = jnp.einsum(
         "td,tf->df", middle_low, grad_hidden, preferred_element_type=jnp.float32
-    )
+    ).astype(jnp.bfloat16)
     grad_expand_bias = jnp.sum(grad_hidden.astype(jnp.float32), axis=0)
+    sum_expand, marks = reduce_weight_grad(links, grad_expand_weight, marks)
     grad_middle = grad_two + jnp.einsum(
-        "tf,df->td", grad_hidden, back_params[7], preferred_element_type=jnp.float32
+        "tf,df->td", after(grad_hidden, grad_expand_weight), back_params[7], preferred_element_type=jnp.float32
     )
     ffn_grads = (
         grad_expand_weight,
@@ -240,10 +401,11 @@
     grad_branch = grad_one.astype(jnp.bfloat16)
     grad_output_weight = jnp.einsum(
         "td,te->de", context, grad_branch, preferred_element_type=jnp.float32
-    )
+    ).astype(jnp.bfloat16)
     grad_output_bias = jnp.sum(grad_branch.astype(jnp.float32), axis=0)
+    sum_output, marks = reduce_weight_grad(links, grad_output_weight, marks)
     grad_context = jnp.einsum(
-        "te,de->td", grad_branch, back_params[3], preferred_element_type=jnp.float32
+        "te,de->td", after(grad_branch, grad_output_weight), back_params[3], preferred_element_type=jnp.float32
     ).astype(jnp.bfloat16)
     grad_queries, grad_keys, grad_values = attend_backward(
         queries, key_rows, values, segment, log_total, grad_context, HEADS
@@ -260,10 +422,11 @@
     grad_value_bias = jnp.sum(grad_joint[:, 2 * model_width :].astype(jnp.float32), axis=0)
     grad_joint_weight = jnp.einsum(
         "td,te->de", tokens, grad_joint, preferred_element_type=jnp.float32
-    )
+    ).astype(jnp.bfloat16)
+    sum_joint, marks = reduce_weight_grad(links, grad_joint_weight, marks)
     grad_tokens = (
         grad_one
-        + jnp.einsum("te,de->td", grad_joint, back_params[0], preferred_element_type=jnp.float32)
+        + jnp.einsum("te,de->td", after(grad_joint, grad_joint_weight), back_params[0], preferred_element_type=jnp.float32)
     ).astype(jnp.bfloat16)
     attn_grads = (
         grad_joint_weight,
@@ -274,8 +437,19 @@
         grad_norm_gain,
         grad_norm_shift,
     )
-    every_part = lax.psum_scatter(attn_grads + ffn_grads, "shard", scatter_dimension=0, tiled=True)
-    every_grad = lax.psum(every_part, "rep")
+    every = attn_grads + ffn_grads
+    vectors = [grad for grad in every if grad.ndim == 1]
+    summed = sum_small(links, jnp.concatenate(vectors))
+    shard = lax.axis_index("shard")
+    small_sums = []
+    start = 0
+    for vector in vectors:
+        size = vector.shape[0] // links.shard_count
+        small_sums.append(lax.dynamic_slice(summed, (start + shard * size,), (size,)))
+        start += vector.shape[0]
+    small_sums = iter(small_sums)
+    large_sums = iter([sum_joint, sum_output, sum_expand, sum_reduce])
+    every_grad = [next(small_sums) if grad.ndim == 1 else next(large_sums) for grad in every]
     attn_grads = every_grad[:7]
     ffn_grads = every_grad[7:]
     return (
@@ -317,7 +491,7 @@
         P("shard"),
     )
     return jax.shard_map(
-        on_device,
+        functools.partial(on_device, Links(mesh)),
         mesh=mesh,
         in_specs=placed,
         out_specs=(

time: 1470 us -> 524 us (0.36)
  waiting for transfers between devices: 1030 us -> 213 us
  blocking collectives: 212 us -> 0 us
  starting transfers between devices: 0.36 us -> 68.6 us
  local copies, waits for them, and re-layouts: 22.7 us -> 49.1 us
  other arithmetic: 31.5 us -> 51.9 us
  matrix products: 147 us -> 129 us
    reduce_scatter x4 -> x0, waiting for transfers between devices: 781 us -> none  [on_device(): lax.psum_scatter(attn_grads + ffn_grads, 'shard', scatter_dimension=0, ti...]
    ppermute x0 -> x88, waiting for transfers between devices: none -> 213 us  [send(): return lax.ppermute(array, ('rep', 'shard'), pairs)]
    all_gather x4 -> x0, waiting for transfers between devices: 180 us -> none  [the longest x1 115 us: on_device(): lax.all_gather(owned[9], 'shard', axis=0, tiled=True)]
    all_gather x9 -> x0, blocking collectives: 169 us -> none  [the longest x1 26.2 us: on_device(): lax.all_gather(owned[8], 'shard', axis=0, tiled=True)]
    ppermute x0 -> x88, starting transfers between devices: none -> 68.6 us  [send(): return lax.ppermute(array, ('rep', 'shard'), pairs)]
    psum x1 -> x0, waiting for transfers between devices: 67.7 us -> none  [on_device(): every_grad = lax.psum(every_part, 'rep')]
    unnamed x1 -> x0, blocking collectives: 35.7 us -> none
    dynamic_update_slice x0 -> x32, local copies, waits for them, and re-layouts: none -> 24.7 us  [the longest x16 12.5 us: gather_weight(): lax.dynamic_update_slice(whole, block[:, None, None], (zero, q, 1 - core,...]
  transfers between devices with their start and end apart: 9 -> 88, of which waited for: 6 -> 31; matrix products, arithmetic and copies ran while one was open for 10% -> 23% of each run, Pallas kernels for 0% -> 0%
where the time goes in v1:
time: 524 us; the launch traced here: 514 us
  waiting for transfers between devices  213 us (41%)
  matrix products  129 us (25%)
  starting transfers between devices  68.6 us (13%)
  other arithmetic  51.9 us (10%)
  local copies, waits for them, and re-layouts  49.1 us (9%)
    ppermute x88, waiting for transfers between devices, send(): return lax.ppermute(array, ('rep', 'shard'), pairs)  213 us
    ppermute x88, starting transfers between devices, send(): return lax.ppermute(array, ('rep', 'shard'), pairs)  68.6 us
    dot_general x1, matrix products, one_block(): jnp.einsum('qhd,khd->hqk', grad_block, value_heads, preferred_element_typ...  15 us
    dynamic_update_slice x16, local copies, waits for them, and re-layouts, gather_weight(): lax.dynamic_update_slice(whole, block[:, None, None], (zero, q, 1 - core,...  12.5 us
    dynamic_update_slice x16, local copies, waits for them, and re-layouts, gather_weight(): lax.dynamic_update_slice(whole, block[:, None, None], (zero, q, core, zer...  12.2 us
    dot_general x1, matrix products, on_device(): jnp.einsum('td,fd->tf', after(grad_second, grad_reduce_weight), back_para...  11.7 us
    dot_general x1, matrix products, on_device(): jnp.dot(middle_low, full_params[7], preferred_element_type=jnp.float32)  10.7 us
    convert_element_type x1, other arithmetic, one_block(): grad_scores = (attn_weights * (grad_weights - inner)).astype(jnp.bfloat16)  10.5 us
  transfers between devices with their start and end apart: 88, of which 31 were waited for; matrix products, arithmetic and copies ran while one was open for 23% of the time, Pallas kernels for 0%

profile of v1, /device:TPU:0, one launch (start us, length us, event | category | flops | bytes accessed | tf_op | source)
XLA Modules:
  0.0 513.6 jit_solution(12173618920727553291)
XLA Ops:
  8.3 3.0 collective-permute-start.9
  12.3 2.7 collective-permute-start
  20.8 3.2 collective-permute-done.10
  24.2 4.5 collective-permute-done.11
  30.3 4.8 collective-permute-done.12
  35.3 14.5 %collective-permute-done.21 = bf16[1,32,4096]{2,1,0:T(8,128)(2,1)S(1)} collective-permute-done((bf16[1,32,4096]{2,1,0:T(8,128)(2,1)S(1)}, bf16[1,32,4096]{2,1,0:T(8,128)(2,1)S(1)}, u32[]{:S(2)}, u32[]{:S(2)}) %collective-permute-start.21) | collective-permute-done | bytes 262176 | tf_op jit(solution)/shard_map/ppermute | solution.py:143
  52.2 7.8 %collective-permute-done.13 = bf16[2,32,1024]{2,1,0:T(8,128)(2,1)S(1)} collective-permute-done((bf16[2,32,1024]{2,1,0:T(8,128)(2,1)S(1)}, bf16[2,32,1024]{2,1,0:T(8,128)(2,1)S(1)}, u32[]{:S(2)}, u32[]{:S(2)}) %collective-permute-start.13) | collective-permute-done | bytes 131104 | tf_op jit(solution)/shard_map/ppermute | solution.py:143
  61.5 10.5 %collective-permute-done.22 = bf16[2,32,4096]{2,1,0:T(8,128)(2,1)S(1)} collective-permute-done((bf16[2,32,4096]{2,1,0:T(8,128)(2,1)S(1)}, bf16[2,32,4096]{2,1,0:T(8,128)(2,1)S(1)}, u32[]{:S(2)}, u32[]{:S(2)}) %collective-permute-start.22) | collective-permute-done | bytes 524320 | tf_op jit(solution)/shard_map/ppermute | solution.py:143
  79.0 5.9 %collective-permute-done.14 = bf16[4,32,1024]{2,1,0:T(8,128)(2,1)S(1)} collective-permute-done((bf16[4,32,1024]{2,1,0:T(8,128)(2,1)S(1)}, bf16[4,32,1024]{2,1,0:T(8,128)(2,1)S(1)}, u32[]{:S(2)}, u32[]{:S(2)}) %collective-permute-start.14) | collective-permute-done | bytes 262176 | tf_op jit(solution)/shard_map/ppermute | solution.py:143
  87.9 4.7 collective-permute-done.16
  102.3 6.7 %collective-permute-done.15 = bf16[4,32,1024]{2,1,0:T(8,128)(2,1)S(1)} collective-permute-done((bf16[4,32,1024]{2,1,0:T(8,128)(2,1)S(1)}, bf16[4,32,1024]{2,1,0:T(8,128)(2,1)S(1)}, u32[]{:S(2)}, u32[]{:S(2)}) %collective-permute-start.15) | collective-permute-done | bytes 262176 | tf_op jit(solution)/shard_map/ppermute | solution.py:143
  115.9 21.5 %collective-permute-done.24 = bf16[4,32,4096]{2,1,0:T(8,128)(2,1)S(1)} collective-permute-done((bf16[4,32,4096]{2,1,0:T(8,128)(2,1)}, bf16[4,32,4096]{2,1,0:T(8,128)(2,1)S(1)}, u32[]{:S(2)}, u32[]{:S(2)}) %collective-permute-start.24) | collective-permute-done | bytes 1048608 | tf_op jit(solution)/shard_map/ppermute | solution.py:143
  137.6 2.4 collective-permute-start.25
  140.1 3.7 convolution_bitcast_fusion
  145.3 7.6 %fusion.51 = (f32[16,512]{1,0:T(8,128)S(1)}, f32[16,512,512]{1,2,0:T(8,128)}) fusion(bf16[512,16,64]{0,2,1:T(8,128)(2,1)S(1)} %bitcast.412, bf16[512,16,64]{0,2,1:T(8,128)(2,1)S(1)} %bitcast.408, pred[512,512]{0,1:T(8,128)(4,1)S(1)} %broadcast_compare_fusion), kind=kOutput, calls=%fused_computation.243 | convolution fusion | flops 549445632 | bytes 19169280 | tf_op jit(solution)/shard_map/while/body/eval_jaxpr/qhd,khd->hqk/dot_general | solution.py:33
  152.9 8.3 %fusion = f32[16,512]{1,0:T(8,128)S(1)} fusion(f32[16,512,512]{1,2,0:T(8,128)} %get-tuple-element.220, f32[16,512]{1,0:T(8,128)S(1)} %get-tuple-element.219), kind=kLoop, calls=%fused_computation.6 | loop fusion | flops 8380416 | bytes 16842752 | tf_op jit(solution)/shard_map/while/body/eval_jaxpr/reduce_sum | solution.py:52
  161.2 9.2 %fusion.23 = bf16[16,64,512]{2,1,0:T(8,128)(2,1)S(1)} fusion(bf16[512,16,64]{0,2,1:T(8,128)(2,1)} %bitcast.450, f32[16,512,512]{1,2,0:T(8,128)} %get-tuple-element.220, f32[16,512]{1,0:T(8,128)S(1)} %fusion, f32[16,512]{1,0:T(8,128)S(1)} %get-tuple-element.219), kind=kOutput, calls=%fused_computation.82 | convolution fusion | flops 549978112 | bytes 18939904 | tf_op jit(solution)/shard_map/while/body/eval_jaxpr/hqk,khd->qhd/dot_general | solution.py:54
  186.8 10.7 %multiply_convert_fusion.1 = (bf16[512,4096]{1,0:T(8,128)(2,1)S(1)}, f32[512,4096]{1,0:T(8,128)}) fusion(f32[4096]{0:T(1024)S(1)} %bitcast.512, bf16[1024,4096]{1,0:T(8,128)(2,1)} %bitcast.432, f32[512,1024]{1,0:T(8,128)S(1)} %get-tuple-element.222, f32[1024]{0:T(1024)S(1)} %get-tuple-element.214, f32[1024]{0:T(1024)S(1)} %get-tuple-element.215, ...), kind=kOutput, calls=%fused_computation.12 | convolution fusion | flops 4310171648 | bytes 23097344 | tf_op jit(solution)/shard_map/dot_general | solution.py:354
  197.5 3.7 collective-permute-done.34
  205.6 4.8 fusion.53
  215.2 6.8 %convolution_convert_fusion.1 = bf16[4096,1024]{1,0:T(8,128)(2,1)} fusion(bf16[512,4096]{1,0:T(8,128)(2,1)S(1)} %get-tuple-element.223, bf16[512,1024]{1,0:T(8,128)(2,1)S(1)} %get-tuple-element.125), kind=kOutput, calls=%fused_computation.16 | convolution fusion | flops 4299161600 | bytes 13631488 | tf_op jit(solution)/shard_map/tf,td->fd/dot_general | solution.py:375
  222.0 11.7 %convert_reduce_fusion = (f32[4096]{0:T(1024)}, bf16[512,4096]{1,0:T(8,128)(2,1)}) fusion(f32[512,4096]{1,0:T(8,128)} %get-tuple-element.224, f32[4096]{0:T(1024)S(1)} %bitcast.513, bf16[512,1024]{1,0:T(8,128)(2,1)S(1)} %get-tuple-element.125, bf16[4096,1024]{1,0:T(8,128)(2,1)S(1)} %bitcast.431), kind=kOutput, calls=%fused_computation.9 | convolution fusion | flops 4328517632 | bytes 22052864 | tf_op jit(solution)/shard_map/td,fd->tf/dot_general | solution.py:380
  233.8 9.5 %convolution_convert_fusion = bf16[1024,4096]{1,0:T(8,128)(2,1)} fusion(bf16[512,4096]{1,0:T(8,128)(2,1)} %get-tuple-element.126, f32[512,1024]{1,0:T(8,128)S(1)} %get-tuple-element.222, f32[1024]{0:T(1024)S(1)} %get-tuple-element.214, f32[1024]{0:T(1024)S(1)} %get-tuple-element.215, f32[512]{0:T(512)S(1)} %fusion.43, f32[512]{0:T(512)S(1)} %broadcast_multiply_fusion.1), kind=kOutput, calls=%fused_computation.15 | convolution fusion | flops 4301783040 | bytes 14692352 | tf_op jit(solution)/shard_map/td,tf->df/dot_general | solution.py:384
  243.2 8.3 %multiply_reduce_fusion.2 = (f32[1024]{0:T(1024)}, f32[512]{0:T(512)S(1)}, f32[1024]{0:T(1024)}, f32[512,1024]{1,0:T(8,128)S(1)}) fusion(f32[512,1024]{1,0:T(8,128)S(1)} %get-tuple-element.222, f32[512]{0:T(512)S(1)} %fusion.43, f32[512]{0:T(512)S(1)} %broadcast_multiply_fusion.1, f32[1024]{0:T(1024)S(1)} %get-tuple-element.215, ...), kind=kOutput, calls=%fused_computation.45 | convolution fusion | flops 4300207616 | bytes 18894848 | tf_op jit(solution)/shard_map/tf,df->td/dot_general | solution.py:389
  254.2 2.6 convolution_convert_fusion.3
  259.5 9.9 %convert_reduce_fusion.3 = (f32[16,64]{1,0:T(8,128)S(1)}, bf16[16,64,512]{2,1,0:T(8,128)(2,1)}) fusion(bf16[512,16,64]{0,2,1:T(8,128)(2,1)} %bitcast.410, f32[16,512,512]{1,2,0:T(8,128)} %get-tuple-element.220, f32[16,512]{1,0:T(8,128)} %log_add_fusion), kind=kOutput, calls=%fused_computation.47 | convolution fusion | flops 546831360 | bytes 18911232 | tf_op jit(solution)/shard_map/while/body/eval_jaxpr/hqk,qhd->khd/dot_general | solution.py:98
  269.4 15.0 %multiply_reduce_fusion = (f32[16,512]{1,0:T(8,128)}, f32[16,512,512]{1,2,0:T(8,128)}) fusion(f32[16,512,512]{1,2,0:T(8,128)} %get-tuple-element.220, f32[16,512]{1,0:T(8,128)} %log_add_fusion, bf16[512,16,64]{0,2,1:T(8,128)(2,1)} %bitcast.411, bf16[512,16,64]{0,2,1:T(8,128)(2,1)} %bitcast.451), kind=kOutput, calls=%fused_computation.1 | convolution fusion | flops 549445632 | bytes 35717120 | tf_op jit(solution)/shard_map/while/body/eval_jaxpr/qhd,khd->hqk/dot_general | solution.py:82
  284.4 10.5 %multiply_convert_fusion = bf16[16,512,512]{1,2,0:T(8,128)(2,1)} fusion(f32[16,512,512]{1,2,0:T(8,128)} %get-tuple-element.229, f32[16,512,512]{1,2,0:T(8,128)S(1)} %bitcast.407, f32[16,512]{1,0:T(8,128)} %get-tuple-element.228, f32[16,512]{1,0:T(8,128)} %log_add_fusion), kind=kLoop, calls=%fused_computation | loop fusion | flops 16777216 | bytes 42008576 | tf_op jit(solution)/shard_map/while/body/eval_jaxpr/convert_element_type | solution.py:86
  294.9 6.5 %multiply_convert_fusion.2 = bf16[16,64,512]{2,1,0:T(8,128)(2,1)S(1)} fusion(bf16[512,16,64]{0,2,1:T(8,128)(2,1)} %bitcast.413, bf16[16,512,512]{1,2,0:T(8,128)(2,1)} %multiply_convert_fusion), kind=kOutput, calls=%fused_computation.54 | convolution fusion | flops 537919488 | bytes 10485760 | tf_op jit(solution)/shard_map/while/body/eval_jaxpr/hqk,qhd->khd/dot_general | solution.py:93
  310.8 8.2 %add_convert_fusion.5 = bf16[512,1024]{1,0:T(8,128)(2,1)} fusion(f32[512,1024]{1,0:T(8,128)S(1)} %copy-done.7, bf16[512,3072]{0,1:T(8,128)(2,1)S(1)} %pad_maximum_fusion, bf16[1024,3072]{1,0:T(8,128)(2,1)} %bitcast.445, f32[512]{0:T(512)S(1)} %copy-done.27), kind=kOutput, calls=%fused_computation.53 | convolution fusion | flops 3222798336 | bytes 12584960 | tf_op jit(solution)/shard_map/te,de->td/dot_general | solution.py:429
  319.2 2.6 fusion.12
  325.1 10.1 %convolution_convert_fusion.2 = bf16[3072,1024]{0,1:T(8,128)(2,1)} fusion(bf16[512,1024]{1,0:T(8,128)(2,1)} %param.16, bf16[512,1024]{0,1:T(8,128)(2,1)S(1)} %bitcast.453, bf16[512,1024]{0,1:T(8,128)(2,1)S(1)} %bitcast.455, bf16[512,1024]{0,1:T(8,128)(2,1)S(1)} %bitcast.437), kind=kOutput, calls=%fused_computation.17 | convolution fusion | flops 3233808384 | bytes 10485760 | tf_op jit(solution)/shard_map/td,te->de/dot_general | solution.py:423
  337.3 3.2 add_convert_fusion.3
  345.7 20.6 %collective-permute-done.52 = bf16[4,128,1024]{2,1,0:T(8,128)(2,1)S(1)} collective-permute-done((bf16[4,128,1024]{2,1,0:T(8,128)(2,1)S(1)}, bf16[4,128,1024]{2,1,0:T(8,128)(2,1)S(1)}, u32[]{:S(2)}, u32[]{:S(2)}) %collective-permute-start.52) | collective-permute-done | bytes 1048608 | tf_op jit(solution)/shard_map/ppermute | solution.py:143
  372.9 10.0 %collective-permute-done.67 = bf16[2,128,1024]{2,1,0:T(8,128)(2,1)S(1)} collective-permute-done((bf16[2,128,1024]{2,1,0:T(8,128)(2,1)S(1)}, bf16[2,128,1024]{2,1,0:T(8,128)(2,1)S(1)}, u32[]{:S(2)}, u32[]{:S(2)}) %collective-permute-start.67) | collective-permute-done | bytes 524320 | tf_op jit(solution)/shard_map/ppermute | solution.py:143
  386.9 11.6 %collective-permute-done.71 = bf16[1,128,1024]{2,1,0:T(8,128)(2,1)S(1)} collective-permute-done((bf16[1,128,1024]{2,1,0:T(8,128)(2,1)S(1)}, bf16[1,128,1024]{2,1,0:T(8,128)(2,1)S(1)}, u32[]{:S(2)}, u32[]{:S(2)}) %collective-permute-start.71) | collective-permute-done | bytes 262176 | tf_op jit(solution)/shard_map/ppermute | solution.py:143
  400.7 8.1 %collective-permute-done.75 = bf16[128,1024]{1,0:T(8,128)(2,1)S(1)} collective-permute-done((bf16[128,1024]{1,0:T(8,128)(2,1)S(1)}, bf16[128,1024]{1,0:T(8,128)(2,1)S(1)}, u32[]{:S(2)}, u32[]{:S(2)}) %collective-permute-start.75) | collective-permute-done | bytes 262176 | tf_op jit(solution)/shard_map/ppermute | solution.py:143
  408.8 8.8 %collective-permute-start.59 = (bf16[4,32,3072]{2,1,0:T(8,128)(2,1)S(1)}, bf16[4,32,3072]{2,1,0:T(8,128)(2,1)S(1)}, u32[]{:S(2)}, u32[]{:S(2)}) collective-permute-start(bf16[4,32,3072]{2,1,0:T(8,128)(2,1)S(1)} %get-tuple-element.145), channel_id=1, source_target_pairs={{0,8},{1,9},{2,10},{3,11},{4,12},{5,13},{6,14},{7,15},{8,0},{9,1},... | collective-permute-start | bytes 2359304 | tf_op jit(solution)/shard_map/ppermute | solution.py:143
  421.7 2.6 collective-permute-done.55
  426.9 6.0 %collective-permute-done.56 = bf16[4,32,1024]{2,1,0:T(8,128)(2,1)S(1)} collective-permute-done((bf16[4,32,1024]{2,1,0:T(8,128)(2,1)S(1)}, bf16[4,32,1024]{2,1,0:T(8,128)(2,1)S(1)}, u32[]{:S(2)}, u32[]{:S(2)}) %collective-permute-start.56) | collective-permute-done | bytes 262176 | tf_op jit(solution)/shard_map/ppermute | solution.py:143
  437.2 4.6 collective-permute-done.69
  442.8 6.5 %collective-permute-done.72 = bf16[1,32,4096]{2,1,0:T(8,128)(2,1)S(1)} collective-permute-done((bf16[1,32,4096]{2,1,0:T(8,128)(2,1)S(1)}, bf16[1,32,4096]{2,1,0:T(8,128)(2,1)S(1)}, u32[]{:S(2)}, u32[]{:S(2)}) %collective-permute-start.72) | collective-permute-done | bytes 262176 | tf_op jit(solution)/shard_map/ppermute | solution.py:143
  449.4 5.1 collective-permute-done.73
  458.9 4.9 collective-permute-done.76
  467.0 12.2 %collective-permute-done.77 = bf16[32,1024]{1,0:T(8,128)(2,1)S(1)} collective-permute-done((bf16[32,1024]{1,0:T(8,128)(2,1)S(1)}, bf16[32,1024]{1,0:T(8,128)(2,1)S(1)}, u32[]{:S(2)}, u32[]{:S(2)}) %collective-permute-start.77) | collective-permute-done | bytes 65568 | tf_op jit(solution)/shard_map/ppermute | solution.py:143
  480.6 10.8 %collective-permute-done.70 = bf16[2,32,3072]{2,1,0:T(8,128)(2,1)S(1)} collective-permute-done((bf16[2,32,3072]{2,1,0:T(8,128)(2,1)S(1)}, bf16[2,32,3072]{2,1,0:T(8,128)(2,1)S(1)}, u32[]{:S(2)}, u32[]{:S(2)}) %collective-permute-start.70) | collective-permute-done | bytes 393248 | tf_op jit(solution)/shard_map/ppermute | solution.py:143
  494.0 9.2 %collective-permute-done.74 = bf16[1,32,3072]{2,1,0:T(8,128)(2,1)S(1)} collective-permute-done((bf16[1,32,3072]{2,1,0:T(8,128)(2,1)S(1)}, bf16[1,32,3072]{2,1,0:T(8,128)(2,1)S(1)}, u32[]{:S(2)}, u32[]{:S(2)}) %collective-permute-start.74) | collective-permute-done | bytes 196640 | tf_op jit(solution)/shard_map/ppermute | solution.py:143
  505.1 5.0 collective-permute-done.78
  (407 shorter events, 140.1 us)
Async XLA Ops:
  12.3 16.4 %collective-permute-start = (bf16[1,32,3072]{2,1,0:T(8,128)(2,1)S(1)}, bf16[1,32,3072]{2,1,0:T(8,128)(2,1)S(1)}, u32[]{:S(2)}, u32[]{:S(2)}) collective-permute-start(bf16[1,32,3072]{2,1,0:T(8,128)(2,1)S(1)} %fusion.86), channel_id=1, source_target_pairs={{0,4},{1,5},{2,6},{3,7},{4,0},{5,1},{6,2},{7,3},{8,12},{9,13},{10,... | collective-permute-start | bytes 589832 | tf_op jit(solution)/shard_map/ppermute | solution.py:143
  28.9 21.0 %collective-permute-start.1 = (bf16[2,32,3072]{2,1,0:T(8,128)(2,1)S(1)}, bf16[2,32,3072]{2,1,0:T(8,128)(2,1)S(1)}, u32[]{:S(2)}, u32[]{:S(2)}) collective-permute-start(bf16[2,32,3072]{2,1,0:T(8,128)(2,1)S(1)} %maximum_select_fusion.15), channel_id=1, source_target_pairs={{0,2},{1,3},{2,0},{3,1},{4,6},{5,7},{6,4},{7,5},{8,10},{9,11},{10,... | collective-permute-start | bytes 1179656 | tf_op jit(solution)/shard_map/ppermute | solution.py:143
  35.2 14.6 %collective-permute-start.21 = (bf16[1,32,4096]{2,1,0:T(8,128)(2,1)S(1)}, bf16[1,32,4096]{2,1,0:T(8,128)(2,1)S(1)}, u32[]{:S(2)}, u32[]{:S(2)}) collective-permute-start(bf16[1,32,4096]{2,1,0:T(8,128)(2,1)S(1)} %fusion.88), channel_id=1, source_target_pairs={{0,4},{1,5},{2,6},{3,7},{4,0},{5,1},{6,2},{7,3},{8,12},{9,13},{10,... | collective-permute-start | bytes 786440 | tf_op jit(solution)/shard_map/ppermute | solution.py:143
  50.1 45.0 %collective-permute-start.5 = (bf16[4,32,3072]{2,1,0:T(8,128)(2,1)S(1)}, bf16[4,32,3072]{2,1,0:T(8,128)(2,1)}, u32[]{:S(2)}, u32[]{:S(2)}) collective-permute-start(bf16[4,32,3072]{2,1,0:T(8,128)(2,1)S(1)} %bitcast.460), channel_id=1, source_target_pairs={{0,8},{1,9},{2,10},{3,11},{4,12},{5,13},{6,14},{7,15},{8,0},{9,1},... | collective-permute-start | bytes 2359304 | tf_op jit(solution)/shard_map/ppermute | solution.py:143
  50.2 27.2 %collective-permute-start.3 = (bf16[4,32,3072]{2,1,0:T(8,128)(2,1)S(1)}, bf16[4,32,3072]{2,1,0:T(8,128)(2,1)S(1)}, u32[]{:S(2)}, u32[]{:S(2)}) collective-permute-start(bf16[4,32,3072]{2,1,0:T(8,128)(2,1)S(1)} %bitcast.461), channel_id=1, source_target_pairs={{0,16},{1,17},{2,18},{3,19},{4,20},{5,21},{6,22},{7,23},{8,9},{9,8... | collective-permute-start | bytes 2359304 | tf_op jit(solution)/shard_map/ppermute | solution.py:143
  51.7 23.8 %collective-permute-start.2 = (bf16[4,32,3072]{2,1,0:T(8,128)(2,1)S(1)}, bf16[4,32,3072]{2,1,0:T(8,128)(2,1)}, u32[]{:S(2)}, u32[]{:S(2)}) collective-permute-start(bf16[4,32,3072]{2,1,0:T(8,128)(2,1)S(1)} %bitcast.462), channel_id=1, source_target_pairs={{0,1},{1,0},{2,3},{3,2},{4,5},{5,4},{6,7},{7,6},{8,24},{9,25},{10,... | collective-permute-start | bytes 2359304 | tf_op jit(solution)/shard_map/ppermute | solution.py:143
  61.2 48.8 %collective-permute-start.17 = (bf16[4,32,1024]{2,1,0:T(8,128)(2,1)S(1)}, bf16[4,32,1024]{2,1,0:T(8,128)(2,1)S(1)}, u32[]{:S(2)}, u32[]{:S(2)}) collective-permute-start(bf16[4,32,1024]{2,1,0:T(8,128)(2,1)S(1)} %bitcast.477), channel_id=1, source_target_pairs={{0,8},{1,9},{2,10},{3,11},{4,12},{5,13},{6,14},{7,15},{8,0},{9,1},... | collective-permute-start | bytes 786440 | tf_op jit(solution)/shard_map/ppermute | solution.py:143
  77.4 15.2 %collective-permute-start.4 = (bf16[4,32,3072]{2,1,0:T(8,128)(2,1)}, bf16[4,32,3072]{2,1,0:T(8,128)(2,1)}, u32[]{:S(2)}, u32[]{:S(2)}) collective-permute-start(bf16[4,32,3072]{2,1,0:T(8,128)(2,1)} %collective-permute-done.2), channel_id=1, source_target_pairs={{0,16},{1,17},{2,18},{3,19},{4,20},{5,21},{6,22},{7,23},{8,9},{9,8... | collective-permute-start | bytes 2359304 | tf_op jit(solution)/shard_map/ppermute | solution.py:143
  84.8 90.4 %collective-permute-start.26 = (bf16[4,32,4096]{2,1,0:T(8,128)(2,1)}, bf16[4,32,4096]{2,1,0:T(8,128)(2,1)}, u32[]{:S(2)}, u32[]{:S(2)}) collective-permute-start(bf16[4,32,4096]{2,1,0:T(8,128)(2,1)} %bitcast.58), channel_id=1, source_target_pairs={{0,8},{1,9},{2,10},{3,11},{4,12},{5,13},{6,14},{7,15},{8,0},{9,1},... | collective-permute-start | bytes 3145736 | tf_op jit(solution)/shard_map/ppermute | solution.py:143
  95.1 18.6 %collective-permute-start.23 = (bf16[4,32,4096]{2,1,0:T(8,128)(2,1)}, bf16[4,32,4096]{2,1,0:T(8,128)(2,1)}, u32[]{:S(2)}, u32[]{:S(2)}) collective-permute-start(bf16[4,32,4096]{2,1,0:T(8,128)(2,1)} %bitcast.58), channel_id=1, source_target_pairs={{0,1},{1,0},{2,3},{3,2},{4,5},{5,4},{6,7},{7,6},{8,24},{9,25},{10,... | collective-permute-start | bytes 3145736 | tf_op jit(solution)/shard_map/ppermute | solution.py:143
  109.0 93.0 %collective-permute-start.35 = (bf16[4,128,1024]{2,1,0:T(8,128)(2,1)S(1)}, bf16[4,128,1024]{2,1,0:T(8,128)(2,1)}, u32[]{:S(2)}, u32[]{:S(2)}) collective-permute-start(bf16[4,128,1024]{2,1,0:T(8,128)(2,1)S(1)} %bitcast.447), channel_id=1, source_target_pairs={{0,8},{1,9},{2,10},{3,11},{4,12},{5,13},{6,14},{7,15},{8,0},{9,1},... | collective-permute-start | bytes 3145736 | tf_op jit(solution)/shard_map/ppermute | solution.py:143
  112.0 25.4 %collective-permute-start.24 = (bf16[4,32,4096]{2,1,0:T(8,128)(2,1)}, bf16[4,32,4096]{2,1,0:T(8,128)(2,1)S(1)}, u32[]{:S(2)}, u32[]{:S(2)}) collective-permute-start(bf16[4,32,4096]{2,1,0:T(8,128)(2,1)} %bitcast.58), channel_id=1, source_target_pairs={{0,16},{1,17},{2,18},{3,19},{4,20},{5,21},{6,22},{7,23},{8,9},{9,8... | collective-permute-start | bytes 3145736 | tf_op jit(solution)/shard_map/ppermute | solution.py:143
  113.6 23.9 %collective-permute-start.8 = (bf16[4,32,3072]{2,1,0:T(8,128)(2,1)}, bf16[4,32,3072]{2,1,0:T(8,128)(2,1)S(1)}, u32[]{:S(2)}, u32[]{:S(2)}) collective-permute-start(bf16[4,32,3072]{2,1,0:T(8,128)(2,1)} %collective-permute-done.4), channel_id=1, source_target_pairs={{0,8},{1,9},{2,10},{3,11},{4,12},{5,13},{6,14},{7,15},{8,0},{9,1},... | collective-permute-start | bytes 2359304 | tf_op jit(solution)/shard_map/ppermute | solution.py:143
  113.8 65.4 %collective-permute-start.32 = (bf16[4,128,1024]{2,1,0:T(8,128)(2,1)S(1)}, bf16[4,128,1024]{2,1,0:T(8,128)(2,1)}, u32[]{:S(2)}, u32[]{:S(2)}) collective-permute-start(bf16[4,128,1024]{2,1,0:T(8,128)(2,1)S(1)} %bitcast.448), channel_id=1, source_target_pairs={{0,1},{1,0},{2,3},{3,2},{4,5},{5,4},{6,7},{7,6},{8,24},{9,25},{10,... | collective-permute-start | bytes 3145736 | tf_op jit(solution)/shard_map/ppermute | solution.py:143
  137.4 41.8 %collective-permute-start.27 = (bf16[4,32,4096]{2,1,0:T(8,128)(2,1)}, bf16[4,32,4096]{2,1,0:T(8,128)(2,1)}, u32[]{:S(2)}, u32[]{:S(2)}) collective-permute-start(bf16[4,32,4096]{2,1,0:T(8,128)(2,1)} %collective-permute-done.23), channel_id=1, source_target_pairs={{0,8},{1,9},{2,10},{3,11},{4,12},{5,13},{6,14},{7,15},{8,0},{9,1},... | collective-permute-start | bytes 3145736 | tf_op jit(solution)/shard_map/ppermute | solution.py:143
  137.6 35.2 %collective-permute-start.25 = (bf16[4,32,4096]{2,1,0:T(8,128)(2,1)}, bf16[4,32,4096]{2,1,0:T(8,128)(2,1)}, u32[]{:S(2)}, u32[]{:S(2)}) collective-permute-start(bf16[4,32,4096]{2,1,0:T(8,128)(2,1)} %collective-permute-done.23), channel_id=1, source_target_pairs={{0,16},{1,17},{2,18},{3,19},{4,20},{5,21},{6,22},{7,23},{8,9},{9,8... | collective-permute-start | bytes 3145736 | tf_op jit(solution)/shard_map/ppermute | solution.py:143
  175.2 26.0 %collective-permute-start.33 = (bf16[4,128,1024]{2,1,0:T(8,128)(2,1)S(1)}, bf16[4,128,1024]{2,1,0:T(8,128)(2,1)S(1)}, u32[]{:S(2)}, u32[]{:S(2)}) collective-permute-start(bf16[4,128,1024]{2,1,0:T(8,128)(2,1)S(1)} %bitcast.449), channel_id=1, source_target_pairs={{0,16},{1,17},{2,18},{3,19},{4,20},{5,21},{6,22},{7,23},{8,9},{9,8... | collective-permute-start | bytes 3145736 | tf_op jit(solution)/shard_map/ppermute | solution.py:143
  179.2 24.1 %collective-permute-start.36 = (bf16[4,128,1024]{2,1,0:T(8,128)(2,1)}, bf16[4,128,1024]{2,1,0:T(8,128)(2,1)S(1)}, u32[]{:S(2)}, u32[]{:S(2)}) collective-permute-start(bf16[4,128,1024]{2,1,0:T(8,128)(2,1)} %collective-permute-done.32), channel_id=1, source_target_pairs={{0,8},{1,9},{2,10},{3,11},{4,12},{5,13},{6,14},{7,15},{8,0},{9,1},... | collective-permute-start | bytes 3145736 | tf_op jit(solution)/shard_map/ppermute | solution.py:143
  184.3 17.0 %collective-permute-start.34 = (bf16[4,128,1024]{2,1,0:T(8,128)(2,1)}, bf16[4,128,1024]{2,1,0:T(8,128)(2,1)S(1)}, u32[]{:S(2)}, u32[]{:S(2)}) collective-permute-start(bf16[4,128,1024]{2,1,0:T(8,128)(2,1)} %collective-permute-done.32), channel_id=1, source_target_pairs={{0,16},{1,17},{2,18},{3,19},{4,20},{5,21},{6,22},{7,23},{8,9},{9,8... | collective-permute-start | bytes 3145736 | tf_op jit(solution)/shard_map/ppermute | solution.py:143
  306.1 29.0 %collective-permute-start.62 = (bf16[4,128,1024]{2,1,0:T(8,128)(2,1)}, bf16[4,128,1024]{2,1,0:T(8,128)(2,1)}, u32[]{:S(2)}, u32[]{:S(2)}) collective-permute-start(bf16[4,128,1024]{2,1,0:T(8,128)(2,1)} %get-tuple-element.178), channel_id=1, source_target_pairs={{0,8},{1,9},{2,10},{3,11},{4,12},{5,13},{6,14},{7,15},{8,0},{9,1},... | collective-permute-start | bytes 3145736 | tf_op jit(solution)/shard_map/ppermute | solution.py:143
  306.7 30.6 %collective-permute-start.49 = (bf16[4,128,1024]{2,1,0:T(8,128)(2,1)}, bf16[4,128,1024]{2,1,0:T(8,128)(2,1)}, u32[]{:S(2)}, u32[]{:S(2)}) collective-permute-start(bf16[4,128,1024]{2,1,0:T(8,128)(2,1)} %get-tuple-element.180), channel_id=1, source_target_pairs={{0,8},{1,9},{2,10},{3,11},{4,12},{5,13},{6,14},{7,15},{8,0},{9,1},... | collective-permute-start | bytes 3145736 | tf_op jit(solution)/shard_map/ppermute | solution.py:143
  306.8 17.8 %collective-permute-start.39 = (bf16[4,128,1024]{2,1,0:T(8,128)(2,1)}, bf16[4,128,1024]{2,1,0:T(8,128)(2,1)}, u32[]{:S(2)}, u32[]{:S(2)}) collective-permute-start(bf16[4,128,1024]{2,1,0:T(8,128)(2,1)} %get-tuple-element.181), channel_id=1, source_target_pairs={{0,8},{1,9},{2,10},{3,11},{4,12},{5,13},{6,14},{7,15},{8,0},{9,1},... | collective-permute-start | bytes 3145736 | tf_op jit(solution)/shard_map/ppermute | solution.py:143
  321.9 15.4 %collective-permute-start.51 = (bf16[4,128,1024]{2,1,0:T(8,128)(2,1)}, bf16[4,128,1024]{2,1,0:T(8,128)(2,1)}, u32[]{:S(2)}, u32[]{:S(2)}) collective-permute-start(bf16[4,128,1024]{2,1,0:T(8,128)(2,1)} %fusion.12), channel_id=1, source_target_pairs={{0,16},{1,17},{2,18},{3,19},{4,20},{5,21},{6,22},{7,23},{8,9},{9,8... | collective-permute-start | bytes 3145736 | tf_op jit(solution)/shard_map/ppermute | solution.py:143
  324.6 19.1 %collective-permute-start.40 = (bf16[4,32,4096]{2,1,0:T(8,128)(2,1)}, bf16[4,32,4096]{2,1,0:T(8,128)(2,1)}, u32[]{:S(2)}, u32[]{:S(2)}) collective-permute-start(bf16[4,32,4096]{2,1,0:T(8,128)(2,1)} %get-tuple-element.129), channel_id=1, source_target_pairs={{0,8},{1,9},{2,10},{3,11},{4,12},{5,13},{6,14},{7,15},{8,0},{9,1},... | collective-permute-start | bytes 3145736 | tf_op jit(solution)/shard_map/ppermute | solution.py:143
  324.6 19.1 %collective-permute-start.48 = (bf16[4,32,4096]{2,1,0:T(8,128)(2,1)}, bf16[4,32,4096]{2,1,0:T(8,128)(2,1)}, u32[]{:S(2)}, u32[]{:S(2)}) collective-permute-start(bf16[4,32,4096]{2,1,0:T(8,128)(2,1)} %get-tuple-element.137), channel_id=1, source_target_pairs={{0,8},{1,9},{2,10},{3,11},{4,12},{5,13},{6,14},{7,15},{8,0},{9,1},... | collective-permute-start | bytes 3145736 | tf_op jit(solution)/shard_map/ppermute | solution.py:143
  340.5 25.8 %collective-permute-start.52 = (bf16[4,128,1024]{2,1,0:T(8,128)(2,1)S(1)}, bf16[4,128,1024]{2,1,0:T(8,128)(2,1)S(1)}, u32[]{:S(2)}, u32[]{:S(2)}) collective-permute-start(bf16[4,128,1024]{2,1,0:T(8,128)(2,1)S(1)} %get-tuple-element.138), channel_id=1, source_target_pairs={{0,16},{1,17},{2,18},{3,19},{4,20},{5,21},{6,22},{7,23},{8,9},{9,8... | collective-permute-start | bytes 3145736 | tf_op jit(solution)/shard_map/ppermute | solution.py:143
  341.6 24.7 %collective-permute-start.63 = (bf16[4,128,1024]{2,1,0:T(8,128)(2,1)S(1)}, bf16[4,128,1024]{2,1,0:T(8,128)(2,1)S(1)}, u32[]{:S(2)}, u32[]{:S(2)}) collective-permute-start(bf16[4,128,1024]{2,1,0:T(8,128)(2,1)S(1)} %get-tuple-element.176), channel_id=1, source_target_pairs={{0,1},{1,0},{2,3},{3,2},{4,5},{5,4},{6,7},{7,6},{8,24},{9,25},{10,... | collective-permute-start | bytes 3145736 | tf_op jit(solution)/shard_map/ppermute | solution.py:143
  343.6 25.4 %collective-permute-start.84 = (f32[12288]{0:T(1024)S(1)}, f32[12288]{0:T(1024)S(1)}, u32[]{:S(2)}, u32[]{:S(2)}) collective-permute-start(f32[12288]{0:T(1024)S(1)} %add.633), channel_id=1, source_target_pairs={{0,4},{1,5},{2,6},{3,7},{4,0},{5,1},{6,2},{7,3},{8,12},{9,13},{10,... | collective-permute-start | bytes 147464 | tf_op jit(solution)/shard_map/ppermute | solution.py:143
  343.7 39.5 %collective-permute-start.47 = (bf16[4,32,4096]{2,1,0:T(8,128)(2,1)S(1)}, bf16[4,32,4096]{2,1,0:T(8,128)(2,1)S(1)}, u32[]{:S(2)}, u32[]{:S(2)}) collective-permute-start(bf16[4,32,4096]{2,1,0:T(8,128)(2,1)S(1)} %get-tuple-element.136), channel_id=1, source_target_pairs={{0,8},{1,9},{2,10},{3,11},{4,12},{5,13},{6,14},{7,15},{8,0},{9,1},... | collective-permute-start | bytes 3145736 | tf_op jit(solution)/shard_map/ppermute | solution.py:143
  343.7 40.0 %collective-permute-start.61 = (bf16[4,32,4096]{2,1,0:T(8,128)(2,1)S(1)}, bf16[4,32,4096]{2,1,0:T(8,128)(2,1)S(1)}, u32[]{:S(2)}, u32[]{:S(2)}) collective-permute-start(bf16[4,32,4096]{2,1,0:T(8,128)(2,1)S(1)} %get-tuple-element.147), channel_id=1, source_target_pairs={{0,8},{1,9},{2,10},{3,11},{4,12},{5,13},{6,14},{7,15},{8,0},{9,1},... | collective-permute-start | bytes 3145736 | tf_op jit(solution)/shard_map/ppermute | solution.py:143
  369.0 13.9 %collective-permute-start.67 = (bf16[2,128,1024]{2,1,0:T(8,128)(2,1)S(1)}, bf16[2,128,1024]{2,1,0:T(8,128)(2,1)S(1)}, u32[]{:S(2)}, u32[]{:S(2)}) collective-permute-start(bf16[2,128,1024]{2,1,0:T(8,128)(2,1)S(1)} %dynamic-slice_bitcast_fusion.12), channel_id=1, source_target_pairs={{0,2},{1,3},{2,0},{3,1},{4,6},{5,7},{6,4},{7,5},{8,10},{9,11},{10,... | collective-permute-start | bytes 1572872 | tf_op jit(solution)/shard_map/ppermute | solution.py:143
  370.3 14.8 %collective-permute-start.53 = (bf16[4,32,4096]{2,1,0:T(8,128)(2,1)S(1)}, bf16[4,32,4096]{2,1,0:T(8,128)(2,1)S(1)}, u32[]{:S(2)}, u32[]{:S(2)}) collective-permute-start(bf16[4,32,4096]{2,1,0:T(8,128)(2,1)S(1)} %fusion.14), channel_id=1, source_target_pairs={{0,16},{1,17},{2,18},{3,19},{4,20},{5,21},{6,22},{7,23},{8,9},{9,8... | collective-permute-start | bytes 3145736 | tf_op jit(solution)/shard_map/ppermute | solution.py:143
  372.7 47.9 %collective-permute-start.45 = (bf16[4,32,1024]{2,1,0:T(8,128)(2,1)S(1)}, bf16[4,32,1024]{2,1,0:T(8,128)(2,1)S(1)}, u32[]{:S(2)}, u32[]{:S(2)}) collective-permute-start(bf16[4,32,1024]{2,1,0:T(8,128)(2,1)S(1)} %get-tuple-element.134), channel_id=1, source_target_pairs={{0,8},{1,9},{2,10},{3,11},{4,12},{5,13},{6,14},{7,15},{8,0},{9,1},... | collective-permute-start | bytes 786440 | tf_op jit(solution)/shard_map/ppermute | solution.py:143
  382.9 38.8 %collective-permute-start.60 = (bf16[4,32,1024]{2,1,0:T(8,128)(2,1)S(1)}, bf16[4,32,1024]{2,1,0:T(8,128)(2,1)S(1)}, u32[]{:S(2)}, u32[]{:S(2)}) collective-permute-start(bf16[4,32,1024]{2,1,0:T(8,128)(2,1)S(1)} %get-tuple-element.146), channel_id=1, source_target_pairs={{0,8},{1,9},{2,10},{3,11},{4,12},{5,13},{6,14},{7,15},{8,0},{9,1},... | collective-permute-start | bytes 786440 | tf_op jit(solution)/shard_map/ppermute | solution.py:143
  383.1 16.4 %collective-permute-start.44 = (bf16[4,32,3072]{2,1,0:T(8,128)(2,1)S(1)}, bf16[4,32,3072]{2,1,0:T(8,128)(2,1)S(1)}, u32[]{:S(2)}, u32[]{:S(2)}) collective-permute-start(bf16[4,32,3072]{2,1,0:T(8,128)(2,1)S(1)} %get-tuple-element.133), channel_id=1, source_target_pairs={{0,8},{1,9},{2,10},{3,11},{4,12},{5,13},{6,14},{7,15},{8,0},{9,1},... | collective-permute-start | bytes 2359304 | tf_op jit(solution)/shard_map/ppermute | solution.py:143
  383.7 14.8 %collective-permute-start.71 = (bf16[1,128,1024]{2,1,0:T(8,128)(2,1)S(1)}, bf16[1,128,1024]{2,1,0:T(8,128)(2,1)S(1)}, u32[]{:S(2)}, u32[]{:S(2)}) collective-permute-start(bf16[1,128,1024]{2,1,0:T(8,128)(2,1)S(1)} %constant_dynamic-slice_fusion), channel_id=1, source_target_pairs={{0,4},{1,5},{2,6},{3,7},{4,0},{5,1},{6,2},{7,3},{8,12},{9,13},{10,... | collective-permute-start | bytes 786440 | tf_op jit(solution)/shard_map/ppermute | solution.py:143
  386.1 31.6 %collective-permute-start.54 = (bf16[4,32,4096]{2,1,0:T(8,128)(2,1)S(1)}, bf16[4,32,4096]{2,1,0:T(8,128)(2,1)S(1)}, u32[]{:S(2)}, u32[]{:S(2)}) collective-permute-start(bf16[4,32,4096]{2,1,0:T(8,128)(2,1)S(1)} %get-tuple-element.140), channel_id=1, source_target_pairs={{0,16},{1,17},{2,18},{3,19},{4,20},{5,21},{6,22},{7,23},{8,9},{9,8... | collective-permute-start | bytes 3145736 | tf_op jit(solution)/shard_map/ppermute | solution.py:143
  398.5 19.3 %collective-permute-start.64 = (bf16[4,32,4096]{2,1,0:T(8,128)(2,1)S(1)}, bf16[4,32,4096]{2,1,0:T(8,128)(2,1)S(1)}, u32[]{:S(2)}, u32[]{:S(2)}) collective-permute-start(bf16[4,32,4096]{2,1,0:T(8,128)(2,1)S(1)} %get-tuple-element.148), channel_id=1, source_target_pairs={{0,1},{1,0},{2,3},{3,2},{4,5},{5,4},{6,7},{7,6},{8,24},{9,25},{10,... | collective-permute-start | bytes 3145736 | tf_op jit(solution)/shard_map/ppermute | solution.py:143
  408.8 47.2 %collective-permute-start.59 = (bf16[4,32,3072]{2,1,0:T(8,128)(2,1)S(1)}, bf16[4,32,3072]{2,1,0:T(8,128)(2,1)S(1)}, u32[]{:S(2)}, u32[]{:S(2)}) collective-permute-start(bf16[4,32,3072]{2,1,0:T(8,128)(2,1)S(1)} %get-tuple-element.145), channel_id=1, source_target_pairs={{0,8},{1,9},{2,10},{3,11},{4,12},{5,13},{6,14},{7,15},{8,0},{9,1},... | collective-permute-start | bytes 2359304 | tf_op jit(solution)/shard_map/ppermute | solution.py:143
  420.6 14.1 %collective-permute-start.68 = (bf16[2,32,4096]{2,1,0:T(8,128)(2,1)S(1)}, bf16[2,32,4096]{2,1,0:T(8,128)(2,1)S(1)}, u32[]{:S(2)}, u32[]{:S(2)}) collective-permute-start(bf16[2,32,4096]{2,1,0:T(8,128)(2,1)S(1)} %dynamic-slice_bitcast_fusion.13), channel_id=1, source_target_pairs={{0,2},{1,3},{2,0},{3,1},{4,6},{5,7},{6,4},{7,5},{8,10},{9,11},{10,... | collective-permute-start | bytes 1572872 | tf_op jit(solution)/shard_map/ppermute | solution.py:143
  426.7 29.3 %collective-permute-start.43 = (bf16[4,32,3072]{2,1,0:T(8,128)(2,1)S(1)}, bf16[4,32,3072]{2,1,0:T(8,128)(2,1)S(1)}, u32[]{:S(2)}, u32[]{:S(2)}) collective-permute-start(bf16[4,32,3072]{2,1,0:T(8,128)(2,1)S(1)} %get-tuple-element.132), channel_id=1, source_target_pairs={{0,8},{1,9},{2,10},{3,11},{4,12},{5,13},{6,14},{7,15},{8,0},{9,1},... | collective-permute-start | bytes 2359304 | tf_op jit(solution)/shard_map/ppermute | solution.py:143
  433.0 46.3 %collective-permute-start.42 = (bf16[4,32,3072]{2,1,0:T(8,128)(2,1)S(1)}, bf16[4,32,3072]{2,1,0:T(8,128)(2,1)S(1)}, u32[]{:S(2)}, u32[]{:S(2)}) collective-permute-start(bf16[4,32,3072]{2,1,0:T(8,128)(2,1)S(1)} %get-tuple-element.131), channel_id=1, source_target_pairs={{0,8},{1,9},{2,10},{3,11},{4,12},{5,13},{6,14},{7,15},{8,0},{9,1},... | collective-permute-start | bytes 2359304 | tf_op jit(solution)/shard_map/ppermute | solution.py:143
  435.7 13.7 %collective-permute-start.72 = (bf16[1,32,4096]{2,1,0:T(8,128)(2,1)S(1)}, bf16[1,32,4096]{2,1,0:T(8,128)(2,1)S(1)}, u32[]{:S(2)}, u32[]{:S(2)}) collective-permute-start(bf16[1,32,4096]{2,1,0:T(8,128)(2,1)S(1)} %constant_dynamic-slice_fusion.1), channel_id=1, source_target_pairs={{0,4},{1,5},{2,6},{3,7},{4,0},{5,1},{6,2},{7,3},{8,12},{9,13},{10,... | collective-permute-start | bytes 786440 | tf_op jit(solution)/shard_map/ppermute | solution.py:143
  441.9 14.1 %collective-permute-start.57 = (bf16[4,32,3072]{2,1,0:T(8,128)(2,1)S(1)}, bf16[4,32,3072]{2,1,0:T(8,128)(2,1)S(1)}, u32[]{:S(2)}, u32[]{:S(2)}) collective-permute-start(bf16[4,32,3072]{2,1,0:T(8,128)(2,1)S(1)} %fusion.20), channel_id=1, source_target_pairs={{0,16},{1,17},{2,18},{3,19},{4,20},{5,21},{6,22},{7,23},{8,9},{9,8... | collective-permute-start | bytes 2359304 | tf_op jit(solution)/shard_map/ppermute | solution.py:143
  456.7 22.6 %collective-permute-start.66 = (bf16[4,32,3072]{2,1,0:T(8,128)(2,1)S(1)}, bf16[4,32,3072]{2,1,0:T(8,128)(2,1)S(1)}, u32[]{:S(2)}, u32[]{:S(2)}) collective-permute-start(bf16[4,32,3072]{2,1,0:T(8,128)(2,1)S(1)} %get-tuple-element.150), channel_id=1, source_target_pairs={{0,1},{1,0},{2,3},{3,2},{4,5},{5,4},{6,7},{7,6},{8,24},{9,25},{10,... | collective-permute-start | bytes 2359304 | tf_op jit(solution)/shard_map/ppermute | solution.py:143
  457.8 21.5 %collective-permute-start.58 = (bf16[4,32,3072]{2,1,0:T(8,128)(2,1)S(1)}, bf16[4,32,3072]{2,1,0:T(8,128)(2,1)S(1)}, u32[]{:S(2)}, u32[]{:S(2)}) collective-permute-start(bf16[4,32,3072]{2,1,0:T(8,128)(2,1)S(1)} %get-tuple-element.144), channel_id=1, source_target_pairs={{0,16},{1,17},{2,18},{3,19},{4,20},{5,21},{6,22},{7,23},{8,9},{9,8... | collective-permute-start | bytes 2359304 | tf_op jit(solution)/shard_map/ppermute | solution.py:143
  463.9 15.3 %collective-permute-start.77 = (bf16[32,1024]{1,0:T(8,128)(2,1)S(1)}, bf16[32,1024]{1,0:T(8,128)(2,1)S(1)}, u32[]{:S(2)}, u32[]{:S(2)}) collective-permute-start(bf16[32,1024]{1,0:T(8,128)(2,1)S(1)} %bitcast.493), channel_id=1, source_target_pairs={{0,16},{1,17},{2,18},{3,19},{4,20},{5,21},{6,22},{7,23},{8,24},{9,... | collective-permute-start | bytes 196616 | tf_op jit(solution)/shard_map/ppermute | solution.py:143
  467.0 37.9 %collective-permute-start.86 = (bf16[2,32,4096]{2,1,0:T(8,128)(2,1)S(1)}, bf16[2,32,4096]{2,1,0:T(8,128)(2,1)S(1)}, u32[]{:S(2)}, u32[]{:S(2)}) collective-permute-start(bf16[2,32,4096]{2,1,0:T(8,128)(2,1)S(1)} %maximum_select_fusion.11), channel_id=1, source_target_pairs={{0,8},{1,9},{2,10},{3,11},{4,12},{5,13},{6,14},{7,15},{8,0},{9,1},... | collective-permute-start | bytes 1572872 | tf_op jit(solution)/shard_map/ppermute | solution.py:143
  (85 other events, 802.3 us)

commit v2 on v1

v2 whole, which is shorter than its diff:
```python
import functools

import jax
import jax.numpy as jnp
from jax import lax
from jax.sharding import PartitionSpec as P

HEADS = 16


epsilon = 1e-05
mask_fill = -1000000000.0


def layer_norm(inputs, gain_vector, shift_vector):
    centre = inputs - jnp.mean(inputs, axis=-1, keepdims=True)
    variance = jnp.mean(centre * centre, axis=-1, keepdims=True)
    return centre * lax.rsqrt(variance + epsilon) * gain_vector + shift_vector


def gelu_exact(inputs):
    return 0.5 * inputs * (1.0 + jax.scipy.special.erf(inputs * 0.7071067811865476))


def segment_of(length_row, row_count):
    seq_ends = jnp.cumsum(length_row)
    position = jnp.arange(row_count, dtype=jnp.int32)
    return jnp.sum((position[:, None] >= seq_ends[None, :]).astype(jnp.int32), axis=1)


def block_scores(query_block, key_heads, segment_block, segment, score_scale):
    scores = (
        jnp.einsum("qhd,khd->hqk", query_block, key_heads, preferred_element_type=jnp.float32)
        * score_scale
    )
    return jnp.where((segment_block[:, None] == segment[None, :])[None], scores, mask_fill)


def attend_forward(queries, key_rows, values, segment, head_count):
    row_count, model_width = queries.shape
    head_size = model_width // head_count
    block_size = min(512, row_count)
    score_scale = head_size ** (-0.5)
    key_heads = key_rows.reshape(row_count, head_count, head_size)
    value_heads = values.reshape(row_count, head_count, head_size)

    def one_block(state_carry, block_index):
        query_block = queries.reshape(block_size, head_count, head_size)
        scores = block_scores(query_block, key_heads, segment, segment, score_scale)
        row_max = jnp.max(scores, axis=-1, keepdims=True)
        powers = jnp.exp(scores - row_max)
        row_total = jnp.sum(powers, axis=-1, keepdims=True)
        attn_weights = (powers / row_total).astype(jnp.bfloat16)
        context = jnp.einsum(
            "hqk,khd->qhd", attn_weights, value_heads, preferred_element_type=jnp.float32
        )
        log_total = (row_max + jnp.log(row_total))[..., 0]
        return (
            state_carry,
            (context.reshape(block_size, model_width).astype(jnp.bfloat16), log_total),
        )

    _, (context, log_total) = lax.scan(one_block, 0, jnp.arange(row_count // block_size))
    return (context.reshape(row_count, model_width), log_total)


def attend_backward(queries, key_rows, values, segment, log_total, grad_context, head_count):
    row_count, model_width = queries.shape
    head_size = model_width // head_count
    block_size = min(512, row_count)
    score_scale = head_size ** (-0.5)
    key_heads = key_rows.reshape(row_count, head_count, head_size)
    value_heads = values.reshape(row_count, head_count, head_size)

    def one_block(state_carry, block_items):
        grad_keys, grad_values = state_carry
        block_index, block_total = block_items
        query_block = queries.reshape(block_size, head_count, head_size)
        grad_block = grad_context.reshape(block_size, head_count, head_size)
        scores = block_scores(query_block, key_heads, segment, segment, score_scale)
        attn_weights = jnp.exp(scores - block_total[..., None])
        grad_weights = jnp.einsum(
            "qhd,khd->hqk", grad_block, value_heads, preferred_element_type=jnp.float32
        )
        inner = jnp.sum(attn_weights * grad_weights, axis=-1, keepdims=True)
        grad_scores = (attn_weights * (grad_weights - inner)).astype(jnp.bfloat16)
        grad_query = (
            jnp.einsum("hqk,khd->qhd", grad_scores, key_heads, preferred_element_type=jnp.float32)
            * score_scale
        )
        grad_keys = (
            grad_keys
            + jnp.einsum(
                "hqk,qhd->khd", grad_scores, query_block, preferred_element_type=jnp.float32
            )
            * score_scale
        )
        grad_values = grad_values + jnp.einsum(
            "hqk,qhd->khd",
            attn_weights.astype(jnp.bfloat16),
            grad_block,
            preferred_element_type=jnp.float32,
        )
        return ((grad_keys, grad_values), grad_query.reshape(block_size, model_width))

    zero_heads = jnp.zeros((row_count, head_count, head_size), jnp.float32)
    (grad_keys, grad_values), grad_queries = lax.scan(
        one_block, (zero_heads, zero_heads), (jnp.arange(row_count // block_size), log_total)
    )
    return (
        grad_queries.reshape(row_count, model_width),
        grad_keys.reshape(row_count, model_width),
        grad_values.reshape(row_count, model_width),
    )


def flip_pairs(rep_count, shard_count, rep_bit, shard_bit):
    pairs = []
    for rep in range(rep_count):
        for shard in range(shard_count):
            to_rep = rep ^ rep_bit[rep % 2]
            to_shard = shard ^ shard_bit[rep % 2]
            pairs.append((rep * shard_count + shard, to_rep * shard_count + to_shard))
    return pairs


class Links:
    def __init__(self, mesh):
        rep_count, shard_count = mesh.shape["rep"], mesh.shape["shard"]
        self.rep_count, self.shard_count = rep_count, shard_count
        self.shard_bits = shard_count.bit_length() - 1

        def pairs(rep_bit, shard_bit):
            return flip_pairs(rep_count, shard_count, rep_bit, shard_bit)

        self.core = pairs((1, 1), (0, 0))
        self.x = pairs((2, 2), (0, 0))
        self.first = pairs((2, 0), (0, 1))
        self.second = pairs((0, 2), (1, 0))
        self.bits = [pairs((0, 0), (1 << b, 1 << b)) for b in range(self.shard_bits)]

    def send(self, array, pairs):
        return lax.ppermute(array, ("rep", "shard"), pairs)


def after(array, marker):
    if marker is None:
        return array
    return lax.optimization_barrier((array, marker))[0]


def take(array, index, axis):
    return lax.dynamic_index_in_dim(array, index, axis, keepdims=False)


def put_pair(mine, other, bit, axis):
    return jnp.where(bit == 0, jnp.stack([mine, other], axis), jnp.stack([other, mine], axis))


def place():
    rep, shard = lax.axis_index("rep"), lax.axis_index("shard")
    return rep % 2, rep // 2, shard


def add_low(mine, got):
    return (mine.astype(jnp.float32) + got.astype(jnp.float32)).astype(jnp.bfloat16)


def gather_chunk(links, owns):
    core, x, shard = place()
    rows = owns[0].shape[0]
    quarter = rows // 4
    widths = [own.shape[1] for own in owns]
    width = sum(widths)

    def quarter_of(own):
        return take(take(own.reshape(2, 2, quarter, own.shape[1]), x, 0), core, 0)

    part = jnp.concatenate([quarter_of(own) for own in owns], axis=1)[None]
    for b in range(links.shard_bits - 1, 0, -1):
        got = yield (part, links.bits[b])
        part = put_pair(part, got, (shard >> b) % 2, 1).reshape(-1, quarter, width)
    lead = part.shape[0]
    mine_q = (shard % 2) * 2 + x
    got = yield (part, links.second)
    pair = jnp.stack([part, got], axis=1)
    got = yield (pair, links.first)
    four = jnp.concatenate([pair, got], axis=1)
    blocks = []
    for q in range(4):
        apart = q ^ mine_q
        swapped = (apart % 2) * 2 + apart // 2
        blocks.append(take(four, jnp.where(core == 0, swapped, apart), 1))
    near = jnp.stack(blocks, axis=1)
    far = yield (near, links.core)
    zero = jnp.int32(0)
    wholes = []
    start = 0
    for size in widths:
        whole = jnp.zeros((lead, 4, 2, quarter, size), part.dtype)
        for block, side in ((near, core), (far, 1 - core)):
            block = block[:, :, None, :, start : start + size]
            whole = lax.dynamic_update_slice(whole, block, (zero, zero, side, zero, zero))
        wholes.append(whole.reshape(rows * links.shard_count, size))
        start += size
    return wholes


def reduce_chunk(links, grads):
    core, x, shard = place()
    rows = grads[0].shape[0] // links.shard_count
    quarter = rows // 4
    lead = links.shard_count // 2
    widths = [grad.shape[1] for grad in grads]
    width = sum(widths)

    def side_of(side):
        views = [grad.reshape(lead, 4, 2, quarter, grad.shape[1]) for grad in grads]
        return jnp.concatenate([take(view, side, 2) for view in views], axis=-1)

    got = yield (side_of(1 - core), links.core)
    four = add_low(side_of(core), got)
    final_q = (shard % 2) * 2 + x
    mid_q = jnp.where(core == 0, final_q ^ 2, final_q ^ 1)
    away_final = jnp.where(core == 0, final_q ^ 1, final_q ^ 2)
    away = jnp.stack([take(four, away_final, 1), take(four, 3 - final_q, 1)], axis=1)
    got = yield (away, links.first)
    mid = add_low(take(four, mid_q, 1), got[:, 1])
    final = take(four, final_q, 1).astype(jnp.float32) + got[:, 0].astype(jnp.float32)
    got = yield (mid, links.second)
    total = (final + got.astype(jnp.float32)).astype(jnp.bfloat16)
    for b in range(1, links.shard_bits):
        bit = (shard >> b) % 2
        pairs = total.reshape(-1, 2, quarter, width)
        got = yield (take(pairs, 1 - bit, 1), links.bits[b])
        total = add_low(take(pairs, bit, 1), got)
    total = total.reshape(quarter, width)
    got = yield (total, links.x)
    both_x = put_pair(total, got, x, 0)
    got = yield (both_x, links.core)
    both = put_pair(both_x, got, core, 1).reshape(rows, width).astype(jnp.float32)
    sums = []
    start = 0
    for size in widths:
        sums.append(both[:, start : start + size])
        start += size
    return sums


def gather_small(links, own):
    _, _, shard = place()
    part = own[None]
    for b in range(links.shard_bits):
        got = yield (part, links.bits[b])
        bit = (shard >> b) % 2
        part = jnp.where(
            bit == 0, jnp.concatenate([part, got], 0), jnp.concatenate([got, part], 0)
        )
    return part


def sum_small(links, vector):
    for pairs in [links.core, links.x] + links.bits:
        got = yield (vector, pairs)
        vector = vector + got
    return vector


class Ticks:
    def __init__(self, links):
        self.links = links
        self.waiting = {}
        self.done = {}

    def begin(self, name, stages):
        self.waiting[name] = (stages, next(stages))

    def tick(self, compute=None, inputs=()):
        names = list(self.waiting)
        operands = [self.waiting[name][1][0] for name in names]
        operands, inputs = lax.optimization_barrier((operands, tuple(inputs)))
        gots = [
            self.links.send(operand, self.waiting[name][1][1])
            for operand, name in zip(operands, names)
        ]
        outs = compute(*inputs) if compute is not None else ()
        gots, outs = lax.optimization_barrier((gots, outs))
        for name, got in zip(names, gots):
            stages = self.waiting[name][0]
            try:
                self.waiting[name] = (stages, stages.send(got))
            except StopIteration as finished:
                self.done[name] = finished.value
                del self.waiting[name]
        return outs

    def finish(self, *names):
        while any(name not in self.done for name in names):
            self.tick()
        return [self.done[name] for name in names]


def on_device(
    links,
    tokens,
    cotangent,
    lengths,
    joint_weight,
    query_bias,
    value_bias,
    output_weight,
    output_bias,
    norm_gain,
    norm_shift,
    expand_weight,
    expand_bias,
    reduce_weight,
    reduce_bias,
    final_gain,
    final_shift,
):
    owned = (
        joint_weight,
        query_bias,
        value_bias,
        output_weight,
        output_bias,
        norm_gain,
        norm_shift,
        expand_weight,
        expand_bias,
        reduce_weight,
        reduce_bias,
        final_gain,
        final_shift,
    )
    ticks = Ticks(links)
    ticks.begin("joint", gather_chunk(links, [joint_weight]))
    ticks.begin("small", gather_small(links, jnp.concatenate([p for p in owned if p.ndim == 1])))
    ticks.tick()
    ticks.begin("wide", gather_chunk(links, [expand_weight, output_weight]))
    ticks.tick()
    ticks.begin("reduce", gather_chunk(links, [reduce_weight]))
    (joint_full,), small = ticks.finish("joint", "small")
    vectors = []
    start = 0
    for param in owned:
        if param.ndim == 1:
            whole = small[:, start : start + param.shape[0]].reshape(-1)
            vectors.append(whole.astype(jnp.float32))
            start += param.shape[0]
    query_add, value_add, output_add, gain_one, shift_one, expand_add, reduce_add, gain_two, shift_two = (
        vectors
    )

    row_count, model_width = tokens.shape
    segment = segment_of(lengths[0], row_count)
    live_rows = (segment < lengths.shape[1]).astype(jnp.float32)[:, None]

    def attend(tokens, weight):
        joint = jnp.dot(tokens, weight, preferred_element_type=jnp.float32)
        queries = (joint[:, :model_width] + query_add).astype(jnp.bfloat16)
        key_rows = joint[:, model_width : 2 * model_width].astype(jnp.bfloat16)
        values = (joint[:, 2 * model_width :] + value_add).astype(jnp.bfloat16)
        context, log_total = attend_forward(queries, key_rows, values, segment, HEADS)
        return queries, key_rows, values, context, log_total

    queries, key_rows, values, context, log_total = ticks.tick(attend, (tokens, joint_full))
    ((expand_full, output_full),) = ticks.finish("wide")

    def to_active(context, expand_full, output_full):
        branch = jnp.dot(context, output_full, preferred_element_type=jnp.float32) + output_add
        normed = tokens.astype(jnp.float32) + branch
        middle = layer_norm(normed, gain_one, shift_one)
        middle_low = middle.astype(jnp.bfloat16)
        hidden = jnp.dot(middle_low, expand_full, preferred_element_type=jnp.float32) + expand_add
        return normed, middle, middle_low, hidden, gelu_exact(hidden).astype(jnp.bfloat16)

    normed, middle, middle_low, hidden, active = ticks.tick(
        to_active, (context, expand_full, output_full)
    )
    ((reduce_full,),) = ticks.finish("reduce")
    second = jnp.dot(active, reduce_full, preferred_element_type=jnp.float32) + reduce_add

    def final_norm(inputs, gain_vector, shift_vector):
        return layer_norm(inputs, gain_vector, shift_vector) * live_rows

    output, final_pull = jax.vjp(final_norm, middle + second, gain_two, shift_two)
    grad_two, grad_final_gain, grad_final_shift = final_pull(cotangent.astype(jnp.float32))
    grad_second = grad_two.astype(jnp.bfloat16)
    grad_reduce_weight = jnp.einsum(
        "tf,td->fd", active, grad_second, preferred_element_type=jnp.float32
    ).astype(jnp.bfloat16)
    grad_reduce_bias = jnp.sum(grad_second.astype(jnp.float32), axis=0)
    ticks.begin("grad_reduce", reduce_chunk(links, [grad_reduce_weight]))

    def hidden_back(grad_second, hidden, middle_low):
        grad_active = jnp.einsum(
            "td,fd->tf", grad_second, reduce_full, preferred_element_type=jnp.float32
        )
        _, gelu_pull = jax.vjp(gelu_exact, hidden)
        grad_hidden = gelu_pull(grad_active)[0].astype(jnp.bfloat16)
        grad_expand_weight = jnp.einsum(
            "td,tf->df", middle_low, grad_hidden, preferred_element_type=jnp.float32
        ).astype(jnp.bfloat16)
        return grad_hidden, grad_expand_weight

    grad_hidden, grad_expand_weight = ticks.tick(hidden_back, (grad_second, hidden, middle_low))
    grad_expand_bias = jnp.sum(grad_hidden.astype(jnp.float32), axis=0)

    def middle_back(grad_hidden, grad_two, normed, context):
        grad_middle = grad_two + jnp.einsum(
            "tf,df->td", grad_hidden, expand_full, preferred_element_type=jnp.float32
        )
        _, middle_pull = jax.vjp(layer_norm, normed, gain_one, shift_one)
        grad_one, grad_norm_gain, grad_norm_shift = middle_pull(grad_middle)
        grad_branch = grad_one.astype(jnp.bfloat16)
        grad_output_weight = jnp.einsum(
            "td,te->de", context, grad_branch, preferred_element_type=jnp.float32
        ).astype(jnp.bfloat16)
        return grad_one, grad_norm_gain, grad_norm_shift, grad_branch, grad_output_weight

    grad_one, grad_norm_gain, grad_norm_shift, grad_branch, grad_output_weight = ticks.tick(
        middle_back, (grad_hidden, grad_two, normed, context)
    )
    ticks.begin("grad_wide", reduce_chunk(links, [grad_expand_weight, grad_output_weight]))
    grad_output_bias = jnp.sum(grad_branch.astype(jnp.float32), axis=0)
    grad_context = jnp.einsum(
        "te,de->td", grad_branch, output_full, preferred_element_type=jnp.float32
    ).astype(jnp.bfloat16)
    parts = []
    groups = 2
    group_width = model_width // groups
    group_heads = HEADS // groups
    for group in range(groups):
        columns = slice(group * group_width, (group + 1) * group_width)

        def heads_back(queries, key_rows, values, grad_context, log_total):
            grads = attend_backward(
                queries, key_rows, values, segment, log_total, grad_context, group_heads
            )
            return tuple(grad.astype(jnp.bfloat16) for grad in grads)

        if parts:
            grad_context = after(grad_context, parts[-1])
        parts.append(
            ticks.tick(
                heads_back,
                (
                    queries[:, columns],
                    key_rows[:, columns],
                    values[:, columns],
                    grad_context[:, columns],
                    log_total[:, group * group_heads : (group + 1) * group_heads],
                ),
            )
        )
    grad_joint = jnp.concatenate(
        [parts[group][which] for which in range(3) for group in range(groups)], axis=1
    )
    grad_query_bias = jnp.sum(grad_joint[:, :model_width].astype(jnp.float32), axis=0)
    grad_value_bias = jnp.sum(grad_joint[:, 2 * model_width :].astype(jnp.float32), axis=0)

    def joint_back(tokens, grad_joint):
        return jnp.einsum(
            "td,te->de", tokens, grad_joint, preferred_element_type=jnp.float32
        ).astype(jnp.bfloat16)

    grad_joint_weight = ticks.tick(joint_back, (tokens, grad_joint))
    ticks.begin("grad_joint", reduce_chunk(links, [grad_joint_weight]))
    vectors = [
        grad_query_bias,
        grad_value_bias,
        grad_output_bias,
        grad_norm_gain,
        grad_norm_shift,
        grad_expand_bias,
        grad_reduce_bias,
        grad_final_gain,
        grad_final_shift,
    ]
    ticks.begin("grad_small", sum_small(links, jnp.concatenate(vectors)))

    def tokens_back(grad_one, grad_joint):
        return (
            grad_one
            + jnp.einsum("te,de->td", grad_joint, joint_full, preferred_element_type=jnp.float32)
        ).astype(jnp.bfloat16)

    grad_tokens = ticks.tick(tokens_back, (grad_one, grad_joint))
    (sum_joint,), (sum_expand, sum_output), (sum_reduce,), summed = ticks.finish(
        "grad_joint", "grad_wide", "grad_reduce", "grad_small"
    )
    shard = lax.axis_index("shard")
    small_sums = []
    start = 0
    for vector in vectors:
        size = vector.shape[0] // links.shard_count
        small_sums.append(lax.dynamic_slice(summed, (start + shard * size,), (size,)))
        start += vector.shape[0]
    attn_grads = (sum_joint, *small_sums[:2], sum_output, *small_sums[2:5])
    ffn_grads = (sum_expand, small_sums[5], sum_reduce, *small_sums[6:])
    return (
        output.astype(jnp.bfloat16),
        grad_tokens,
        attn_grads[0],
        attn_grads[1],
        attn_grads[2],
        attn_grads[3],
        attn_grads[4],
        attn_grads[5],
        attn_grads[6],
        ffn_grads[0],
        ffn_grads[1],
        ffn_grads[2],
        ffn_grads[3],
        ffn_grads[4],
        ffn_grads[5],
    )


def solution(mesh):
    placed = (
        P(("rep", "shard"), None),
        P(("rep", "shard"), None),
        P(("rep", "shard"), None),
        P("shard", None),
        P("shard"),
        P("shard"),
        P("shard", None),
        P("shard"),
        P("shard"),
        P("shard"),
        P("shard", None),
        P("shard"),
        P("shard", None),
        P("shard"),
        P("shard"),
        P("shard"),
    )
    return jax.shard_map(
        functools.partial(on_device, Links(mesh)),
        mesh=mesh,
        in_specs=placed,
        out_specs=(
            P(("rep", "shard"), None),
            P(("rep", "shard"), None),
            P("shard", None),
            P("shard"),
            P("shard"),
            P("shard", None),
            P("shard"),
            P("shard"),
            P("shard"),
            P("shard", None),
            P("shard"),
            P("shard", None),
            P("shard"),
            P("shard"),
            P("shard"),
        ),
        check_vma=False,
    )
```

time: 524 us -> 538 us (1.027)
  other arithmetic: 51.9 us -> 90 us
  local copies, waits for them, and re-layouts: 49.1 us -> 84.9 us
  waiting for transfers between devices: 213 us -> 190 us
  matrix products: 129 us -> 109 us
  starting transfers between devices: 68.6 us -> 52 us
    ppermute x88 -> x44, waiting for transfers between devices: 213 us -> 190 us  [send(): return lax.ppermute(array, ('rep', 'shard'), pairs)]
    ppermute x88 -> x44, starting transfers between devices: 68.6 us -> 52 us  [send(): return lax.ppermute(array, ('rep', 'shard'), pairs)]
    another operation x1 -> x11, other arithmetic: 0.83 us -> 17.2 us  [the longest x3 7.54 us: gather_chunk(): near = jnp.stack(blocks, axis=1)]
    unnamed x107 -> x163, local copies, waits for them, and re-layouts: 9.04 us -> 22.9 us
    squeeze x8 -> x12, local copies, waits for them, and re-layouts: 0.23 us -> 12 us  [take(): return lax.dynamic_index_in_dim(array, index, axis, keepdims=False)]
    slice x1 -> x10, local copies, waits for them, and re-layouts: 0.13 us -> 10.2 us  [the longest x1 3.01 us: on_device(): values[:, columns]]
    dot_general x1 -> x2, matrix products: 15 us -> 5.84 us  [one_block(): jnp.einsum('qhd,khd->hqk', grad_block, value_heads, preferred_element_typ...]
    concatenate x1 -> x4, other arithmetic: 0.23 us -> 9.23 us  [the longest x3 6.45 us: gather_chunk(): four = jnp.concatenate([pair, got], axis=1)]
  transfers between devices with their start and end apart: 88 -> 44, of which waited for: 31 -> 21; matrix products, arithmetic and copies ran while one was open for 23% -> 29% of each run, Pallas kernels for 0% -> 0%
where the time goes in v2:
time: 538 us; the launch traced here: 529 us
  waiting for transfers between devices  190 us (35%)
  matrix products  109 us (20%)
  other arithmetic  90 us (17%)
  local copies, waits for them, and re-layouts  84.9 us (16%)
  starting transfers between devices  52 us (10%)
    ppermute x44, waiting for transfers between devices, send(): return lax.ppermute(array, ('rep', 'shard'), pairs)  190 us
    ppermute x44, starting transfers between devices, send(): return lax.ppermute(array, ('rep', 'shard'), pairs)  52 us
    unnamed x163, local copies, waits for them, and re-layouts  22.9 us
    convert_element_type x12, other arithmetic, add_low(): (mine.astype(jnp.float32) + got.astype(jnp.float32)).astype(jnp.bfloat16)  18.5 us
    dynamic_update_slice x6, local copies, waits for them, and re-layouts, gather_chunk(): lax.dynamic_update_slice(whole, block, (zero, zero, side, zero, zero))  18.4 us
    dot_general x3, matrix products, block_scores(): jnp.einsum('qhd,khd->hqk', query_block, key_heads, preferred_element_type...  12.5 us
    squeeze x12, local copies, waits for them, and re-layouts, take(): return lax.dynamic_index_in_dim(array, index, axis, keepdims=False)  12 us
    dot_general x1, matrix products, hidden_back(): jnp.einsum('td,fd->tf', grad_second, reduce_full, preferred_element_type=...  11.3 us
  transfers between devices with their start and end apart: 44, of which 21 were waited for; matrix products, arithmetic and copies ran while one was open for 29% of the time, Pallas kernels for 0%

profile of v2, /device:TPU:0, one launch (start us, length us, event | category | flops | bytes accessed | tf_op | source)
XLA Modules:
  0.0 528.5 jit_solution(15495325964627895000)
XLA Ops:
  9.3 4.1 collective-permute-start
  17.8 4.7 collective-permute-done
  23.4 3.4 collective-permute-start.4
  27.0 13.2 %collective-permute-done.3 = bf16[2,1536]{1,0:T(2,128)(2,1)S(1)} collective-permute-done((bf16[2,1536]{1,0:T(2,128)(2,1)S(1)}, bf16[2,1536]{1,0:T(2,128)(2,1)S(1)}, u32[]{:S(2)}, u32[]{:S(2)}) %collective-permute-start.3) | collective-permute-done | bytes 6176 | tf_op jit(solution)/shard_map/ppermute | solution.py:143
  41.7 3.3 collective-permute-start.7
  48.0 16.1 %collective-permute-done.6 = bf16[4,1536]{1,0:T(4,128)(2,1)S(1)} collective-permute-done((bf16[4,1536]{1,0:T(4,128)(2,1)S(1)}, bf16[4,1536]{1,0:T(4,128)(2,1)S(1)}, u32[]{:S(2)}, u32[]{:S(2)}) %collective-permute-start.6) | collective-permute-done | bytes 12320 | tf_op jit(solution)/shard_map/ppermute | solution.py:143
  71.3 11.1 %collective-permute-done.11 = bf16[2,128,1024]{2,1,0:T(8,128)(2,1)} collective-permute-done((bf16[2,128,1024]{2,1,0:T(8,128)(2,1)}, bf16[2,128,1024]{2,1,0:T(8,128)(2,1)}, u32[]{:S(2)}, u32[]{:S(2)}) %collective-permute-start.11) | collective-permute-done | bytes 524320 | tf_op jit(solution)/shard_map/ppermute | solution.py:143
  82.3 17.4 %collective-permute-done.10 = bf16[4,32,5120]{2,1,0:T(8,128)(2,1)} collective-permute-done((bf16[4,32,5120]{2,1,0:T(8,128)(2,1)S(1)}, bf16[4,32,5120]{2,1,0:T(8,128)(2,1)}, u32[]{:S(2)}, u32[]{:S(2)}) %collective-permute-start.10) | collective-permute-done | bytes 1310752 | tf_op jit(solution)/shard_map/ppermute | solution.py:143
  103.7 3.1 pad_maximum_fusion.7
  113.8 24.1 %collective-permute-done.14 = bf16[4,128,1024]{2,1,0:T(8,128)(2,1)S(1)} collective-permute-done((bf16[4,128,1024]{2,1,0:T(8,128)(2,1)S(1)}, bf16[4,128,1024]{2,1,0:T(8,128)(2,1)S(1)}, u32[]{:S(2)}, u32[]{:S(2)}) %collective-permute-start.14) | collective-permute-done | bytes 1048608 | tf_op jit(solution)/shard_map/ppermute | solution.py:143
  137.9 16.2 %collective-permute-done.13 = bf16[4,2,32,5120]{3,2,1,0:T(8,128)(2,1)} collective-permute-done((bf16[4,2,32,5120]{3,2,1,0:T(8,128)(2,1)}, bf16[4,2,32,5120]{3,2,1,0:T(8,128)(2,1)}, u32[]{:S(2)}, u32[]{:S(2)}) %collective-permute-start.13) | collective-permute-done | bytes 2621472 | tf_op jit(solution)/shard_map/ppermute | solution.py:143
  161.8 3.0 pad_maximum_fusion.1
  165.9 3.5 fusion.72
  175.9 10.0 %fusion = (f32[16,512]{1,0:T(8,128)S(1)}, f32[16,512,512]{1,2,0:T(8,128)}) fusion(pred[512,512]{0,1:T(8,128)(4,1)S(1)} %broadcast_compare_fusion, bf16[512,16,64]{0,2,1:T(8,128)(2,1)} %bitcast.364, bf16[512,16,64]{0,2,1:T(8,128)(2,1)} %bitcast.365), kind=kOutput, calls=%fused_computation.3 | convolution fusion | flops 549445632 | bytes 19169280 | tf_op jit(solution)/shard_map/while/body/eval_jaxpr/qhd,khd->hqk/dot_general | solution.py:33
  185.9 9.2 %fusion.1 = f32[16,512]{1,0:T(8,128)S(1)} fusion(f32[16,512,512]{1,2,0:T(8,128)} %get-tuple-element.439, f32[16,512]{1,0:T(8,128)S(1)} %get-tuple-element.438, pred[512,512]{0,1:T(8,128)(4,1)S(1)} %broadcast_compare_fusion), kind=kLoop, calls=%fused_computation.4 | loop fusion | flops 16769024 | bytes 17104896 | tf_op jit(solution)/shard_map/while/body/eval_jaxpr/reduce_sum | solution.py:52
  196.7 5.3 %broadcast_in_dim.165 = bf16[4,4,2,32,4096]{4,3,2,1,0:T(8,128)(2,1)} broadcast(bf16[]{:T(256)} %constant.506.clone.1), dimensions={} | broadcast | bytes 8388610 | tf_op jit(solution)/shard_map/broadcast_in_dim | solution.py:200
  202.0 5.4 %fusion.7 = bf16[4,4,2,32,4096]{4,3,2,1,0:T(8,128)(2,1)} fusion(bf16[4,4,2,32,4096]{4,3,2,1,0:T(8,128)(2,1)} %broadcast_in_dim.165, s32[]{:T(128)S(6)} %select_n.559, bf16[4,4,32,5120]{3,2,1,0:T(8,128)(2,1)} %pad_maximum_fusion.1), kind=kLoop, calls=%fused_computation.30 | loop fusion | bytes 8388612 | tf_op jit(solution)/shard_map/dynamic_update_slice | solution.py:203
  207.5 5.5 %fusion.25 = bf16[16,64,512]{2,1,0:T(8,128)(2,1)} fusion(bf16[512,16,64]{0,2,1:T(8,128)(2,1)S(1)} %bitcast.394, f32[16,512,512]{1,2,0:T(8,128)S(1)} %copy-done.2, f32[16,512]{1,0:T(8,128)S(1)} %fusion.1, f32[16,512]{1,0:T(8,128)S(1)} %get-tuple-element.438, pred[512,512]{0,1:T(8,128)(4,1)S(1)} %broadcast_compare_fusion), kind=kOutput, calls=%fused_computation.95 | convolution fusion | flops 558366720 | bytes 19202048 | tf_op jit(solution)/shard_map/while/body/eval_jaxpr/hqk,khd->qhd/dot_general | solution.py:54
  217.7 3.5 bitcast_dynamic-update-slice_fusion.2
  230.8 9.7 %multiply_convert_fusion.2 = (bf16[512,4096]{1,0:T(8,128)(2,1)S(1)}, f32[512,4096]{1,0:T(8,128)}) fusion(f32[4096]{0:T(1024)S(1)} %bitcast.418, bf16[512,1024]{1,0:T(8,128)(2,1)S(1)} %get-tuple-element.281, bf16[1024,4096]{1,0:T(8,128)(2,1)} %bitcast.335), kind=kOutput, calls=%fused_computation.16 | convolution fusion | flops 4307550208 | bytes 22036480 | tf_op jit(solution)/shard_map/dot_general | solution.py:376
  240.5 4.3 bitcast_dynamic-update-slice_fusion.1
  244.8 4.6 fusion.73
  257.0 5.0 convolution_convert_fusion.1
  262.0 3.1 dynamic-slice_bitcast_fusion.2
  268.9 3.0 fusion.66
  271.9 11.3 %add_convert_fusion.1 = bf16[512,4096]{1,0:T(8,128)(2,1)S(1)} fusion(f32[512,4096]{1,0:T(8,128)} %get-tuple-element.279, bf16[512,1024]{1,0:T(8,128)(2,1)} %copy-done.52, bf16[4096,1024]{1,0:T(8,128)(2,1)} %bitcast.332), kind=kOutput, calls=%fused_computation.15 | convolution fusion | flops 4322230272 | bytes 22020096 | tf_op jit(solution)/shard_map/td,fd->tf/dot_general | solution.py:398
  283.3 7.3 %convolution_convert_fusion = bf16[1024,4096]{1,0:T(8,128)(2,1)} fusion(bf16[512,1024]{1,0:T(8,128)(2,1)S(1)} %copy-done.51, bf16[512,4096]{1,0:T(8,128)(2,1)S(1)} %add_convert_fusion.1), kind=kOutput, calls=%fused_computation.18 | convolution fusion | flops 4299161600 | bytes 13631488 | tf_op jit(solution)/shard_map/td,tf->df/dot_general | solution.py:403
  290.6 4.3 fusion.2
  299.7 10.2 %multiply_reduce_fusion.3 = (f32[1024]{0:T(1024)S(1)}, f32[512]{0:T(512)S(1)}, f32[1024]{0:T(1024)S(1)}, f32[512,1024]{1,0:T(8,128)S(1)}) fusion(f32[512,1024]{1,0:T(8,128)S(1)} %get-tuple-element.288, f32[512]{0:T(512)S(1)} %fusion.54, f32[512]{0:T(512)S(1)} %broadcast_multiply_fusion, f32[1024]{0:T(1024)S(1)} %get-tuple-element.434, ...), kind=kOutput, calls=%fused_computation.74 | convolution fusion | flops 4299683328 | bytes 18892800 | tf_op jit(solution)/shard_map/tf,df->td/dot_general | solution.py:412
  318.4 6.1 %collective-permute-done.19 = bf16[4,2,128,1024]{3,2,0,1:T(8,128)(2,1)} collective-permute-done((bf16[4,2,128,1024]{3,2,0,1:T(8,128)(2,1)}, bf16[4,2,128,1024]{3,2,0,1:T(8,128)(2,1)}, u32[]{:S(2)}, u32[]{:S(2)}) %collective-permute-start.19) | collective-permute-done | bytes 2097184 | tf_op jit(solution)/shard_map/ppermute | solution.py:143
  324.5 3.3 convolution_convert_fusion.4
  332.0 3.0 fusion.38
  335.2 3.2 convert_reduce_fusion
  342.9 3.0 multiply_reduce_fusion.1
  352.5 3.1 fusion.28
  356.8 6.0 %add_convert_fusion = bf16[4,4,32,5120]{3,2,1,0:T(8,128)(2,1)S(1)} fusion(bf16[4,4,32,5120]{3,2,1,0:T(8,128)(2,1)} %collective-permute-done.21, bf16[4,4,32,1024]{3,2,1,0:T(8,128)(2,1)} %get-tuple-element.410, bf16[4,4,32,4096]{3,2,1,0:T(8,128)(2,1)} %get-tuple-element.387), kind=kLoop, calls=%fused_computation.5 | loop fusion | flops 18350080 | bytes 15728640 | tf_op jit(solution)/shard_map/convert_element_type | solution.py:166
  388.5 16.7 %collective-permute-done.23 = bf16[4,2,32,5120]{3,2,0,1:T(8,128)(2,1)S(1)} collective-permute-done((bf16[4,2,32,5120]{3,2,0,1:T(8,128)(2,1)}, bf16[4,2,32,5120]{3,2,0,1:T(8,128)(2,1)S(1)}, u32[]{:S(2)}, u32[]{:S(2)}) %collective-permute-start.23) | collective-permute-done | bytes 2621472 | tf_op jit(solution)/shard_map/ppermute | solution.py:143
  410.7 5.9 %convolution_convert_fusion.2 = bf16[1024,3072]{1,0:T(8,128)(2,1)S(1)} fusion(bf16[512,1024]{1,0:T(8,128)(2,1)S(1)} %copy-done.47, bf16[512,3072]{0,1:T(8,128)(2,1)} %copy-done.55), kind=kOutput, calls=%fused_computation.23 | convolution fusion | flops 3224371200 | bytes 10485760 | tf_op jit(solution)/shard_map/td,te->de/dot_general | solution.py:465
  416.7 5.3 %collective-permute-done.24 = bf16[1,128,1024]{2,1,0:T(8,128)(2,1)S(1)} collective-permute-done((bf16[1,128,1024]{2,1,0:T(8,128)(2,1)S(1)}, bf16[1,128,1024]{2,1,0:T(8,128)(2,1)S(1)}, u32[]{:S(2)}, u32[]{:S(2)}) %collective-permute-start.24) | collective-permute-done | bytes 262176 | tf_op jit(solution)/shard_map/ppermute | solution.py:143
  422.0 3.0 collective-permute-done.25
  431.3 8.7 %add_convert_fusion.3 = bf16[512,1024]{1,0:T(8,128)(2,1)} fusion(f32[512,1024]{1,0:T(8,128)} %get-tuple-element.337, bf16[512,3072]{0,1:T(8,128)(2,1)} %copy-done.55, bf16[1024,3072]{1,0:T(8,128)(2,1)} %bitcast.343), kind=kOutput, calls=%fused_computation.68 | convolution fusion | flops 3222274048 | bytes 12582912 | tf_op jit(solution)/shard_map/te,de->td/dot_general | solution.py:487
  440.0 5.8 %collective-permute-done.27 = bf16[2,32,5120]{2,1,0:T(8,128)(2,1)S(1)} collective-permute-done((bf16[2,32,5120]{2,1,0:T(8,128)(2,1)S(1)}, bf16[2,32,5120]{2,1,0:T(8,128)(2,1)S(1)}, u32[]{:S(2)}, u32[]{:S(2)}) %collective-permute-start.27) | collective-permute-done | bytes 655392 | tf_op jit(solution)/shard_map/ppermute | solution.py:143
  445.8 3.1 fusion.4
  454.0 17.1 %collective-permute-done.33 = f32[12288]{0:T(1024)S(1)} collective-permute-done((f32[12288]{0:T(1024)S(1)}, f32[12288]{0:T(1024)S(1)}, u32[]{:S(2)}, u32[]{:S(2)}) %collective-permute-start.33) | collective-permute-done | bytes 49184 | tf_op jit(solution)/shard_map/ppermute | solution.py:143
  477.9 7.8 %collective-permute-done.36 = f32[12288]{0:T(1024)S(1)} collective-permute-done((f32[12288]{0:T(1024)}, f32[12288]{0:T(1024)S(1)}, u32[]{:S(2)}, u32[]{:S(2)}) %collective-permute-start.36) | collective-permute-done | bytes 49184 | tf_op jit(solution)/shard_map/ppermute | solution.py:143
  488.4 3.1 collective-permute-start.37
  495.3 10.0 %collective-permute-done.39 = f32[12288]{0:T(1024)S(1)} collective-permute-done((f32[12288]{0:T(1024)S(1)}, f32[12288]{0:T(1024)S(1)}, u32[]{:S(2)}, u32[]{:S(2)}) %collective-permute-start.39) | collective-permute-done | bytes 49184 | tf_op jit(solution)/shard_map/ppermute | solution.py:143
  508.6 10.1 %collective-permute-done.41 = f32[12288]{0:T(1024)S(1)} collective-permute-done((f32[12288]{0:T(1024)S(1)}, f32[12288]{0:T(1024)S(1)}, u32[]{:S(2)}, u32[]{:S(2)}) %collective-permute-start.41) | collective-permute-done | bytes 49184 | tf_op jit(solution)/shard_map/ppermute | solution.py:143
  (384 shorter events, 176.6 us)
Async XLA Ops:
  0.6 22.7 %copy-start = (bf16[512,1024]{1,0:T(8,128)(2,1)S(1)}, bf16[512,1024]{1,0:T(8,128)(2,1)}, u32[]{:S(2)}) copy-start(bf16[512,1024]{1,0:T(8,128)(2,1)} %param.28) | copy-start | bytes 3145732
  9.3 13.2 %collective-permute-start = (bf16[1,32,3072]{2,1,0:T(8,128)(2,1)S(1)}, bf16[1,32,3072]{2,1,0:T(8,128)(2,1)S(1)}, u32[]{:S(2)}, u32[]{:S(2)}) collective-permute-start(bf16[1,32,3072]{2,1,0:T(8,128)(2,1)S(1)} %fusion.122), channel_id=1, source_target_pairs={{0,4},{1,5},{2,6},{3,7},{4,0},{5,1},{6,2},{7,3},{8,12},{9,13},{10,... | collective-permute-start | bytes 589832 | tf_op jit(solution)/shard_map/ppermute | solution.py:143
  13.4 4.4 collective-permute-start.1
  22.6 17.5 %collective-permute-start.2 = (bf16[2,32,3072]{2,1,0:T(8,128)(2,1)S(1)}, bf16[2,32,3072]{2,1,0:T(8,128)(2,1)S(1)}, u32[]{:S(2)}, u32[]{:S(2)}) collective-permute-start(bf16[2,32,3072]{2,1,0:T(8,128)(2,1)S(1)} %maximum_select_fusion.15), channel_id=1, source_target_pairs={{0,2},{1,3},{2,0},{3,1},{4,6},{5,7},{6,4},{7,5},{8,10},{9,11},{10,... | collective-permute-start | bytes 1179656 | tf_op jit(solution)/shard_map/ppermute | solution.py:143
  23.4 16.7 %collective-permute-start.4 = (bf16[1,32,5120]{2,1,0:T(8,128)(2,1)S(1)}, bf16[1,32,5120]{2,1,0:T(8,128)(2,1)S(1)}, u32[]{:S(2)}, u32[]{:S(2)}) collective-permute-start(bf16[1,32,5120]{2,1,0:T(8,128)(2,1)S(1)} %get-tuple-element.238), channel_id=1, source_target_pairs={{0,4},{1,5},{2,6},{3,7},{4,0},{5,1},{6,2},{7,3},{8,12},{9,13},{10,... | collective-permute-start | bytes 983048 | tf_op jit(solution)/shard_map/ppermute | solution.py:143
  26.9 13.2 %collective-permute-start.3 = (bf16[2,1536]{1,0:T(2,128)(2,1)S(1)}, bf16[2,1536]{1,0:T(2,128)(2,1)S(1)}, u32[]{:S(2)}, u32[]{:S(2)}) collective-permute-start(bf16[2,1536]{1,0:T(2,128)(2,1)S(1)} %broadcast_select_fusion), channel_id=1, source_target_pairs={{0,2},{1,3},{2,0},{3,1},{4,6},{5,7},{6,4},{7,5},{8,10},{9,11},{10,... | collective-permute-start | bytes 18440 | tf_op jit(solution)/shard_map/ppermute | solution.py:143
  40.4 24.5 %collective-permute-start.5 = (bf16[4,32,3072]{2,1,0:T(8,128)(2,1)S(1)}, bf16[4,32,3072]{2,1,0:T(8,128)(2,1)S(1)}, u32[]{:S(2)}, u32[]{:S(2)}) collective-permute-start(bf16[4,32,3072]{2,1,0:T(8,128)(2,1)S(1)} %bitcast.339), channel_id=1, source_target_pairs={{0,1},{1,0},{2,3},{3,2},{4,5},{5,4},{6,7},{7,6},{8,24},{9,25},{10,... | collective-permute-start | bytes 2359304 | tf_op jit(solution)/shard_map/ppermute | solution.py:143
  41.7 23.2 %collective-permute-start.7 = (bf16[2,32,5120]{2,1,0:T(8,128)(2,1)S(1)}, bf16[2,32,5120]{2,1,0:T(8,128)(2,1)S(1)}, u32[]{:S(2)}, u32[]{:S(2)}) collective-permute-start(bf16[2,32,5120]{2,1,0:T(8,128)(2,1)S(1)} %maximum_select_fusion.6), channel_id=1, source_target_pairs={{0,2},{1,3},{2,0},{3,1},{4,6},{5,7},{6,4},{7,5},{8,10},{9,11},{10,... | collective-permute-start | bytes 1966088 | tf_op jit(solution)/shard_map/ppermute | solution.py:143
  45.0 19.2 %collective-permute-start.8 = (bf16[1,128,1024]{2,1,0:T(8,128)(2,1)S(1)}, bf16[1,128,1024]{2,1,0:T(8,128)(2,1)S(1)}, u32[]{:S(2)}, u32[]{:S(2)}) collective-permute-start(bf16[1,128,1024]{2,1,0:T(8,128)(2,1)S(1)} %fusion.121), channel_id=1, source_target_pairs={{0,4},{1,5},{2,6},{3,7},{4,0},{5,1},{6,2},{7,3},{8,12},{9,13},{10,... | collective-permute-start | bytes 786440 | tf_op jit(solution)/shard_map/ppermute | solution.py:143
  46.8 17.3 %collective-permute-start.6 = (bf16[4,1536]{1,0:T(4,128)(2,1)S(1)}, bf16[4,1536]{1,0:T(4,128)(2,1)S(1)}, u32[]{:S(2)}, u32[]{:S(2)}) collective-permute-start(bf16[4,1536]{1,0:T(4,128)(2,1)S(1)} %maximum_select_fusion.19), channel_id=1, source_target_pairs={{0,4},{1,5},{2,6},{3,7},{4,0},{5,1},{6,2},{7,3},{8,12},{9,13},{10,... | collective-permute-start | bytes 36872 | tf_op jit(solution)/shard_map/ppermute | solution.py:143
  67.3 34.5 %collective-permute-start.9 = (bf16[4,2,32,3072]{3,2,1,0:T(8,128)(2,1)}, bf16[4,2,32,3072]{3,2,1,0:T(8,128)(2,1)}, u32[]{:S(2)}, u32[]{:S(2)}) collective-permute-start(bf16[4,2,32,3072]{3,2,1,0:T(8,128)(2,1)} %pad_maximum_fusion.11), channel_id=1, source_target_pairs={{0,16},{1,17},{2,18},{3,19},{4,20},{5,21},{6,22},{7,23},{8,9},{9,8... | collective-permute-start | bytes 4718600 | tf_op jit(solution)/shard_map/ppermute | solution.py:143
  67.9 31.8 %collective-permute-start.10 = (bf16[4,32,5120]{2,1,0:T(8,128)(2,1)S(1)}, bf16[4,32,5120]{2,1,0:T(8,128)(2,1)}, u32[]{:S(2)}, u32[]{:S(2)}) collective-permute-start(bf16[4,32,5120]{2,1,0:T(8,128)(2,1)S(1)} %bitcast.318), channel_id=1, source_target_pairs={{0,1},{1,0},{2,3},{3,2},{4,5},{5,4},{6,7},{7,6},{8,24},{9,25},{10,... | collective-permute-start | bytes 3932168 | tf_op jit(solution)/shard_map/ppermute | solution.py:143
  69.4 12.9 %collective-permute-start.11 = (bf16[2,128,1024]{2,1,0:T(8,128)(2,1)}, bf16[2,128,1024]{2,1,0:T(8,128)(2,1)}, u32[]{:S(2)}, u32[]{:S(2)}) collective-permute-start(bf16[2,128,1024]{2,1,0:T(8,128)(2,1)} %maximum_select_fusion.11), channel_id=1, source_target_pairs={{0,2},{1,3},{2,0},{3,1},{4,6},{5,7},{6,4},{7,5},{8,10},{9,11},{10,... | collective-permute-start | bytes 1572872 | tf_op jit(solution)/shard_map/ppermute | solution.py:143
  108.1 49.1 %copy-start.8 = (bf16[2,2,128,1024]{3,2,1,0:T(8,128)(2,1)}, bf16[2,2,128,1024]{3,2,1,0:T(8,128)(2,1)S(1)}, u32[]{:S(2)}) copy-start(bf16[2,2,128,1024]{3,2,1,0:T(8,128)(2,1)S(1)} %maximum_select_fusion.2) | copy-start | bytes 3145732
  111.3 42.8 %collective-permute-start.12 = (bf16[4,4,32,3072]{3,2,1,0:T(8,128)(2,1)}, bf16[4,4,32,3072]{3,2,1,0:T(8,128)(2,1)}, u32[]{:S(2)}, u32[]{:S(2)}) collective-permute-start(bf16[4,4,32,3072]{3,2,1,0:T(8,128)(2,1)} %pad_maximum_fusion.6), channel_id=1, source_target_pairs={{0,8},{1,9},{2,10},{3,11},{4,12},{5,13},{6,14},{7,15},{8,0},{9,1},... | collective-permute-start | bytes 9437192 | tf_op jit(solution)/shard_map/ppermute | solution.py:143
  111.3 42.8 %collective-permute-start.13 = (bf16[4,2,32,5120]{3,2,1,0:T(8,128)(2,1)}, bf16[4,2,32,5120]{3,2,1,0:T(8,128)(2,1)}, u32[]{:S(2)}, u32[]{:S(2)}) collective-permute-start(bf16[4,2,32,5120]{3,2,1,0:T(8,128)(2,1)} %pad_maximum_fusion.7), channel_id=1, source_target_pairs={{0,16},{1,17},{2,18},{3,19},{4,20},{5,21},{6,22},{7,23},{8,9},{9,8... | collective-permute-start | bytes 7864328 | tf_op jit(solution)/shard_map/ppermute | solution.py:143
  111.9 26.0 %collective-permute-start.14 = (bf16[4,128,1024]{2,1,0:T(8,128)(2,1)S(1)}, bf16[4,128,1024]{2,1,0:T(8,128)(2,1)S(1)}, u32[]{:S(2)}, u32[]{:S(2)}) collective-permute-start(bf16[4,128,1024]{2,1,0:T(8,128)(2,1)S(1)} %bitcast.321), channel_id=1, source_target_pairs={{0,1},{1,0},{2,3},{3,2},{4,5},{5,4},{6,7},{7,6},{8,24},{9,25},{10,... | collective-permute-start | bytes 3145736 | tf_op jit(solution)/shard_map/ppermute | solution.py:143
  175.5 37.5 %collective-permute-start.15 = (bf16[4,4,32,5120]{3,2,1,0:T(8,128)(2,1)}, bf16[4,4,32,5120]{3,2,1,0:T(8,128)(2,1)}, u32[]{:S(2)}, u32[]{:S(2)}) collective-permute-start(bf16[4,4,32,5120]{3,2,1,0:T(8,128)(2,1)} %pad_maximum_fusion.1), channel_id=1, source_target_pairs={{0,8},{1,9},{2,10},{3,11},{4,12},{5,13},{6,14},{7,15},{8,0},{9,1},... | collective-permute-start | bytes 15728648 | tf_op jit(solution)/shard_map/ppermute | solution.py:143
  175.6 37.4 %collective-permute-start.16 = (bf16[4,2,128,1024]{3,2,1,0:T(8,128)(2,1)}, bf16[4,2,128,1024]{3,2,1,0:T(8,128)(2,1)}, u32[]{:S(2)}, u32[]{:S(2)}) collective-permute-start(bf16[4,2,128,1024]{3,2,1,0:T(8,128)(2,1)} %pad_maximum_fusion.9), channel_id=1, source_target_pairs={{0,16},{1,17},{2,18},{3,19},{4,20},{5,21},{6,22},{7,23},{8,9},{9,8... | collective-permute-start | bytes 6291464 | tf_op jit(solution)/shard_map/ppermute | solution.py:143
  226.0 14.5 %collective-permute-start.17 = (bf16[4,4,128,1024]{3,2,1,0:T(8,128)(2,1)}, bf16[4,4,128,1024]{3,2,1,0:T(8,128)(2,1)}, u32[]{:S(2)}, u32[]{:S(2)}) collective-permute-start(bf16[4,4,128,1024]{3,2,1,0:T(8,128)(2,1)} %pad_maximum_fusion.4), channel_id=1, source_target_pairs={{0,8},{1,9},{2,10},{3,11},{4,12},{5,13},{6,14},{7,15},{8,0},{9,1},... | collective-permute-start | bytes 12582920 | tf_op jit(solution)/shard_map/ppermute | solution.py:143
  266.6 24.0 %collective-permute-start.18 = (bf16[4,4,128,1024]{3,2,1,0:T(8,128)(2,1)}, bf16[4,4,128,1024]{3,2,1,0:T(8,128)(2,1)}, u32[]{:S(2)}, u32[]{:S(2)}) collective-permute-start(bf16[4,4,128,1024]{3,2,1,0:T(8,128)(2,1)} %dynamic-slice_bitcast_fusion.2), channel_id=1, source_target_pairs={{0,8},{1,9},{2,10},{3,11},{4,12},{5,13},{6,14},{7,15},{8,0},{9,1},... | collective-permute-start | bytes 12582920 | tf_op jit(solution)/shard_map/ppermute | solution.py:143
  268.9 21.7 %slice-start.4 = ((s8[8388608]{0:T(1024)(128)(4,1)}), s8[4194304]{0:T(1024)(128)(4,1)S(1)}, s32[]{:S(2)}) async-start(s8[8388608]{0:T(1024)(128)(4,1)} %bitcast.328), calls=%async_computation.4 | async-start | bytes 8388608
  298.1 26.4 %collective-permute-start.19 = (bf16[4,2,128,1024]{3,2,0,1:T(8,128)(2,1)}, bf16[4,2,128,1024]{3,2,0,1:T(8,128)(2,1)}, u32[]{:S(2)}, u32[]{:S(2)}) collective-permute-start(bf16[4,2,128,1024]{3,2,0,1:T(8,128)(2,1)} %pad_maximum_fusion.10), channel_id=1, source_target_pairs={{0,16},{1,17},{2,18},{3,19},{4,20},{5,21},{6,22},{7,23},{8,9},{9,8... | collective-permute-start | bytes 6291464 | tf_op jit(solution)/shard_map/ppermute | solution.py:143
  335.0 20.7 %collective-permute-start.21 = (bf16[4,4,32,5120]{3,2,1,0:T(8,128)(2,1)}, bf16[4,4,32,5120]{3,2,1,0:T(8,128)(2,1)}, u32[]{:S(2)}, u32[]{:S(2)}) collective-permute-start(bf16[4,4,32,5120]{3,2,1,0:T(8,128)(2,1)} %pad_maximum_fusion.2), channel_id=1, source_target_pairs={{0,8},{1,9},{2,10},{3,11},{4,12},{5,13},{6,14},{7,15},{8,0},{9,1},... | collective-permute-start | bytes 15728648 | tf_op jit(solution)/shard_map/ppermute | solution.py:143
  340.3 15.4 %collective-permute-start.20 = (bf16[4,128,1024]{2,1,0:T(8,128)(2,1)}, bf16[4,128,1024]{2,1,0:T(8,128)(2,1)S(1)}, u32[]{:S(2)}, u32[]{:S(2)}) collective-permute-start(bf16[4,128,1024]{2,1,0:T(8,128)(2,1)} %fusion.38), channel_id=1, source_target_pairs={{0,1},{1,0},{2,3},{3,2},{4,5},{5,4},{6,7},{7,6},{8,24},{9,25},{10,... | collective-permute-start | bytes 3145736 | tf_op jit(solution)/shard_map/ppermute | solution.py:143
  373.3 31.9 %collective-permute-start.23 = (bf16[4,2,32,5120]{3,2,0,1:T(8,128)(2,1)}, bf16[4,2,32,5120]{3,2,0,1:T(8,128)(2,1)S(1)}, u32[]{:S(2)}, u32[]{:S(2)}) collective-permute-start(bf16[4,2,32,5120]{3,2,0,1:T(8,128)(2,1)} %pad_maximum_fusion.8), channel_id=1, source_target_pairs={{0,16},{1,17},{2,18},{3,19},{4,20},{5,21},{6,22},{7,23},{8,9},{9,8... | collective-permute-start | bytes 7864328 | tf_op jit(solution)/shard_map/ppermute | solution.py:143
  374.6 13.9 %collective-permute-start.22 = (bf16[2,128,1024]{2,1,0:T(8,128)(2,1)}, bf16[2,128,1024]{2,1,0:T(8,128)(2,1)S(1)}, u32[]{:S(2)}, u32[]{:S(2)}) collective-permute-start(bf16[2,128,1024]{2,1,0:T(8,128)(2,1)} %dynamic-slice_bitcast_fusion.13), channel_id=1, source_target_pairs={{0,2},{1,3},{2,0},{3,1},{4,6},{5,7},{6,4},{7,5},{8,10},{9,11},{10,... | collective-permute-start | bytes 1572872 | tf_op jit(solution)/shard_map/ppermute | solution.py:143
  407.4 17.7 %collective-permute-start.25 = (bf16[4,32,5120]{2,1,0:T(8,128)(2,1)S(1)}, bf16[4,32,5120]{2,1,0:T(8,128)(2,1)S(1)}, u32[]{:S(2)}, u32[]{:S(2)}) collective-permute-start(bf16[4,32,5120]{2,1,0:T(8,128)(2,1)S(1)} %fusion.26), channel_id=1, source_target_pairs={{0,1},{1,0},{2,3},{3,2},{4,5},{5,4},{6,7},{7,6},{8,24},{9,25},{10,... | collective-permute-start | bytes 3932168 | tf_op jit(solution)/shard_map/ppermute | solution.py:143
  408.3 13.7 %collective-permute-start.24 = (bf16[1,128,1024]{2,1,0:T(8,128)(2,1)S(1)}, bf16[1,128,1024]{2,1,0:T(8,128)(2,1)S(1)}, u32[]{:S(2)}, u32[]{:S(2)}) collective-permute-start(bf16[1,128,1024]{2,1,0:T(8,128)(2,1)S(1)} %constant_dynamic-slice_fusion.2), channel_id=1, source_target_pairs={{0,4},{1,5},{2,6},{3,7},{4,0},{5,1},{6,2},{7,3},{8,12},{9,13},{10,... | collective-permute-start | bytes 786440 | tf_op jit(solution)/shard_map/ppermute | solution.py:143
  428.6 17.2 %collective-permute-start.28 = (bf16[4,4,32,3072]{3,2,1,0:T(8,128)(2,1)}, bf16[4,4,32,3072]{3,2,1,0:T(8,128)(2,1)}, u32[]{:S(2)}, u32[]{:S(2)}) collective-permute-start(bf16[4,4,32,3072]{3,2,1,0:T(8,128)(2,1)} %dynamic-slice_bitcast_fusion.3), channel_id=1, source_target_pairs={{0,8},{1,9},{2,10},{3,11},{4,12},{5,13},{6,14},{7,15},{8,0},{9,1},... | collective-permute-start | bytes 9437192 | tf_op jit(solution)/shard_map/ppermute | solution.py:143
  428.6 17.1 %collective-permute-start.27 = (bf16[2,32,5120]{2,1,0:T(8,128)(2,1)S(1)}, bf16[2,32,5120]{2,1,0:T(8,128)(2,1)S(1)}, u32[]{:S(2)}, u32[]{:S(2)}) collective-permute-start(bf16[2,32,5120]{2,1,0:T(8,128)(2,1)S(1)} %dynamic-slice_bitcast_fusion.12), channel_id=1, source_target_pairs={{0,2},{1,3},{2,0},{3,1},{4,6},{5,7},{6,4},{7,5},{8,10},{9,11},{10,... | collective-permute-start | bytes 1966088 | tf_op jit(solution)/shard_map/ppermute | solution.py:143
  430.0 10.0 %collective-permute-start.26 = (bf16[128,1024]{1,0:T(8,128)(2,1)S(1)}, bf16[128,1024]{1,0:T(8,128)(2,1)S(1)}, u32[]{:S(2)}, u32[]{:S(2)}) collective-permute-start(bf16[128,1024]{1,0:T(8,128)(2,1)S(1)} %bitcast.374), channel_id=1, source_target_pairs={{0,16},{1,17},{2,18},{3,19},{4,20},{5,21},{6,22},{7,23},{8,24},{9,... | collective-permute-start | bytes 786440 | tf_op jit(solution)/shard_map/ppermute | solution.py:143
  431.2 8.8 %collective-permute-start.29 = (f32[12288]{0:T(1024)S(1)}, f32[12288]{0:T(1024)S(1)}, u32[]{:S(2)}, u32[]{:S(2)}) collective-permute-start(f32[12288]{0:T(1024)S(1)} %constant_dynamic-update-slice_fusion.9), channel_id=1, source_target_pairs={{0,8},{1,9},{2,10},{3,11},{4,12},{5,13},{6,14},{7,15},{8,0},{9,1},... | collective-permute-start | bytes 147464 | tf_op jit(solution)/shard_map/ppermute | solution.py:143
  448.9 22.8 %copy-start.5 = (bf16[4,4,32,3072]{3,2,1,0:T(8,128)(2,1)}, bf16[4,4,32,3072]{3,2,1,0:T(8,128)(2,1)S(1)}, u32[]{:S(2)}) copy-start(bf16[4,4,32,3072]{3,2,1,0:T(8,128)(2,1)S(1)} %fusion.4) | copy-start | bytes 9437188
  449.5 21.5 %collective-permute-start.32 = (bf16[4,2,32,3072]{3,2,0,1:T(8,128)(2,1)S(1)}, bf16[4,2,32,3072]{3,2,0,1:T(8,128)(2,1)S(1)}, u32[]{:S(2)}, u32[]{:S(2)}) collective-permute-start(bf16[4,2,32,3072]{3,2,0,1:T(8,128)(2,1)S(1)} %pad_maximum_fusion.12), channel_id=1, source_target_pairs={{0,16},{1,17},{2,18},{3,19},{4,20},{5,21},{6,22},{7,23},{8,9},{9,8... | collective-permute-start | bytes 4718600 | tf_op jit(solution)/shard_map/ppermute | solution.py:143
  450.9 20.2 %collective-permute-start.30 = (bf16[2,128,1024]{2,1,0:T(8,128)(2,1)S(1)}, bf16[2,128,1024]{2,1,0:T(8,128)(2,1)S(1)}, u32[]{:S(2)}, u32[]{:S(2)}) collective-permute-start(bf16[2,128,1024]{2,1,0:T(8,128)(2,1)S(1)} %maximum_select_fusion.12), channel_id=1, source_target_pairs={{0,8},{1,9},{2,10},{3,11},{4,12},{5,13},{6,14},{7,15},{8,0},{9,1},... | collective-permute-start | bytes 1572872 | tf_op jit(solution)/shard_map/ppermute | solution.py:143
  450.9 20.2 %collective-permute-start.31 = (bf16[1,32,5120]{2,1,0:T(8,128)(2,1)S(1)}, bf16[1,32,5120]{2,1,0:T(8,128)(2,1)S(1)}, u32[]{:S(2)}, u32[]{:S(2)}) collective-permute-start(bf16[1,32,5120]{2,1,0:T(8,128)(2,1)S(1)} %constant_dynamic-slice_fusion.1), channel_id=1, source_target_pairs={{0,4},{1,5},{2,6},{3,7},{4,0},{5,1},{6,2},{7,3},{8,12},{9,13},{10,... | collective-permute-start | bytes 983048 | tf_op jit(solution)/shard_map/ppermute | solution.py:143
  453.2 17.9 %collective-permute-start.33 = (f32[12288]{0:T(1024)S(1)}, f32[12288]{0:T(1024)S(1)}, u32[]{:S(2)}, u32[]{:S(2)}) collective-permute-start(f32[12288]{0:T(1024)S(1)} %add.555), channel_id=1, source_target_pairs={{0,16},{1,17},{2,18},{3,19},{4,20},{5,21},{6,22},{7,23},{8,24},{9,... | collective-permute-start | bytes 147464 | tf_op jit(solution)/shard_map/ppermute | solution.py:143
  472.9 12.8 %collective-permute-start.35 = (bf16[4,32,3072]{2,1,0:T(8,128)(2,1)}, bf16[4,32,3072]{2,1,0:T(8,128)(2,1)}, u32[]{:S(2)}, u32[]{:S(2)}) collective-permute-start(bf16[4,32,3072]{2,1,0:T(8,128)(2,1)} %fusion.41), channel_id=1, source_target_pairs={{0,1},{1,0},{2,3},{3,2},{4,5},{5,4},{6,7},{7,6},{8,24},{9,25},{10,... | collective-permute-start | bytes 2359304 | tf_op jit(solution)/shard_map/ppermute | solution.py:143
  473.9 11.8 %collective-permute-start.34 = (bf16[32,5120]{1,0:T(8,128)(2,1)S(1)}, bf16[32,5120]{1,0:T(8,128)(2,1)S(1)}, u32[]{:S(2)}, u32[]{:S(2)}) collective-permute-start(bf16[32,5120]{1,0:T(8,128)(2,1)S(1)} %bitcast.372), channel_id=1, source_target_pairs={{0,16},{1,17},{2,18},{3,19},{4,20},{5,21},{6,22},{7,23},{8,24},{9,... | collective-permute-start | bytes 983048 | tf_op jit(solution)/shard_map/ppermute | solution.py:143
  475.4 10.3 %collective-permute-start.36 = (f32[12288]{0:T(1024)}, f32[12288]{0:T(1024)S(1)}, u32[]{:S(2)}, u32[]{:S(2)}) collective-permute-start(f32[12288]{0:T(1024)} %add.560), channel_id=1, source_target_pairs={{0,1},{1,0},{2,3},{3,2},{4,5},{5,4},{6,7},{7,6},{8,9},{9,8},{10,11... | collective-permute-start | bytes 147464 | tf_op jit(solution)/shard_map/ppermute | solution.py:143
  488.4 16.9 %collective-permute-start.37 = (bf16[2,32,5120]{2,1,0:T(8,128)(2,1)S(1)}, bf16[2,32,5120]{2,1,0:T(8,128)(2,1)S(1)}, u32[]{:S(2)}, u32[]{:S(2)}) collective-permute-start(bf16[2,32,5120]{2,1,0:T(8,128)(2,1)S(1)} %maximum_select_fusion.8), channel_id=1, source_target_pairs={{0,8},{1,9},{2,10},{3,11},{4,12},{5,13},{6,14},{7,15},{8,0},{9,1},... | collective-permute-start | bytes 1966088 | tf_op jit(solution)/shard_map/ppermute | solution.py:143
  493.2 12.1 %collective-permute-start.38 = (bf16[2,32,3072]{2,1,0:T(8,128)(2,1)S(1)}, bf16[2,32,3072]{2,1,0:T(8,128)(2,1)S(1)}, u32[]{:S(2)}, u32[]{:S(2)}) collective-permute-start(bf16[2,32,3072]{2,1,0:T(8,128)(2,1)S(1)} %dynamic-slice_bitcast_fusion.14), channel_id=1, source_target_pairs={{0,2},{1,3},{2,0},{3,1},{4,6},{5,7},{6,4},{7,5},{8,10},{9,11},{10,... | collective-permute-start | bytes 1179656 | tf_op jit(solution)/shard_map/ppermute | solution.py:143
  494.6 10.7 %collective-permute-start.39 = (f32[12288]{0:T(1024)S(1)}, f32[12288]{0:T(1024)S(1)}, u32[]{:S(2)}, u32[]{:S(2)}) collective-permute-start(f32[12288]{0:T(1024)S(1)} %add.562), channel_id=1, source_target_pairs={{0,2},{1,3},{2,0},{3,1},{4,6},{5,7},{6,4},{7,5},{8,10},{9,11},{10,... | collective-permute-start | bytes 147464 | tf_op jit(solution)/shard_map/ppermute | solution.py:143
  505.4 13.3 %collective-permute-start.40 = (bf16[1,32,3072]{2,1,0:T(8,128)(2,1)S(1)}, bf16[1,32,3072]{2,1,0:T(8,128)(2,1)S(1)}, u32[]{:S(2)}, u32[]{:S(2)}) collective-permute-start(bf16[1,32,3072]{2,1,0:T(8,128)(2,1)S(1)} %constant_dynamic-slice_fusion), channel_id=1, source_target_pairs={{0,4},{1,5},{2,6},{3,7},{4,0},{5,1},{6,2},{7,3},{8,12},{9,13},{10,... | collective-permute-start | bytes 589832 | tf_op jit(solution)/shard_map/ppermute | solution.py:143
  507.9 10.8 %collective-permute-start.41 = (f32[12288]{0:T(1024)S(1)}, f32[12288]{0:T(1024)S(1)}, u32[]{:S(2)}, u32[]{:S(2)}) collective-permute-start(f32[12288]{0:T(1024)S(1)} %add.564), channel_id=1, source_target_pairs={{0,4},{1,5},{2,6},{3,7},{4,0},{5,1},{6,2},{7,3},{8,12},{9,13},{10,... | collective-permute-start | bytes 147464 | tf_op jit(solution)/shard_map/ppermute | solution.py:143
  518.8 6.0 %collective-permute-start.42 = (bf16[32,3072]{1,0:T(8,128)(2,1)S(1)}, bf16[32,3072]{1,0:T(8,128)(2,1)S(1)}, u32[]{:S(2)}, u32[]{:S(2)}) collective-permute-start(bf16[32,3072]{1,0:T(8,128)(2,1)S(1)} %bitcast.389), channel_id=1, source_target_pairs={{0,16},{1,17},{2,18},{3,19},{4,20},{5,21},{6,22},{7,23},{8,24},{9,... | collective-permute-start | bytes 589832 | tf_op jit(solution)/shard_map/ppermute | solution.py:143
  524.9 1.8 collective-permute-start.43
  (66 other events, 414.7 us)

commit v3 on v2

--- a/solution.py
+++ b/solution.py
@@ -193,14 +193,13 @@
         blocks.append(take(four, jnp.where(core == 0, swapped, apart), 1))
     near = jnp.stack(blocks, axis=1)
     far = yield (near, links.core)
-    zero = jnp.int32(0)
     wholes = []
     start = 0
     for size in widths:
-        whole = jnp.zeros((lead, 4, 2, quarter, size), part.dtype)
-        for block, side in ((near, core), (far, 1 - core)):
-            block = block[:, :, None, :, start : start + size]
-            whole = lax.dynamic_update_slice(whole, block, (zero, zero, side, zero, zero))
+        columns = slice(start, start + size)
+        first = jnp.where(core == 0, near[..., columns], far[..., columns])
+        second = jnp.where(core == 0, far[..., columns], near[..., columns])
+        whole = jnp.stack([first, second], axis=2)
         wholes.append(whole.reshape(rows * links.shard_count, size))
         start += size
     return wholes
@@ -338,7 +337,9 @@
     ticks.begin("joint", gather_chunk(links, [joint_weight]))
     ticks.begin("small", gather_small(links, jnp.concatenate([p for p in owned if p.ndim == 1])))
     ticks.tick()
+    ticks.tick()
     ticks.begin("wide", gather_chunk(links, [expand_weight, output_weight]))
+    ticks.tick()
     ticks.tick()
     ticks.begin("reduce", gather_chunk(links, [reduce_weight]))
     (joint_full,), small = ticks.finish("joint", "small")
@@ -357,15 +358,38 @@
     segment = segment_of(lengths[0], row_count)
     live_rows = (segment < lengths.shape[1]).astype(jnp.float32)[:, None]
 
+    groups = 2
+    group_width = model_width // groups
+    group_heads = HEADS // groups
+
+    def columns_of(array, group):
+        return array[:, group * group_width : (group + 1) * group_width]
+
+    def attend_group(queries, key_rows, values, group):
+        return attend_forward(
+            columns_of(queries, group),
+            columns_of(key_rows, group),
+            columns_of(values, group),
+            segment,
+            group_heads,
+        )
+
     def attend(tokens, weight):
         joint = jnp.dot(tokens, weight, preferred_element_type=jnp.float32)
         queries = (joint[:, :model_width] + query_add).astype(jnp.bfloat16)
         key_rows = joint[:, model_width : 2 * model_width].astype(jnp.bfloat16)
         values = (joint[:, 2 * model_width :] + value_add).astype(jnp.bfloat16)
-        context, log_total = attend_forward(queries, key_rows, values, segment, HEADS)
-        return queries, key_rows, values, context, log_total
-
-    queries, key_rows, values, context, log_total = ticks.tick(attend, (tokens, joint_full))
+        return queries, key_rows, values, attend_group(queries, key_rows, values, 0)
+
+    queries, key_rows, values, attended = ticks.tick(attend, (tokens, joint_full))
+    contexts, log_totals = [attended[0]], [attended[1]]
+    for group in range(1, groups):
+        more_context, more_log = ticks.tick(
+            lambda *rows, group=group: attend_group(*rows, group), (queries, key_rows, values)
+        )
+        contexts.append(more_context)
+        log_totals.append(more_log)
+    context = jnp.concatenate(contexts, axis=1)
     ((expand_full, output_full),) = ticks.finish("wide")
 
     def to_active(context, expand_full, output_full):
@@ -429,45 +453,44 @@
         "te,de->td", grad_branch, output_full, preferred_element_type=jnp.float32
     ).astype(jnp.bfloat16)
     parts = []
-    groups = 2
-    group_width = model_width // groups
-    group_heads = HEADS // groups
-    for group in range(groups):
-        columns = slice(group * group_width, (group + 1) * group_width)
-
-        def heads_back(queries, key_rows, values, grad_context, log_total):
-            grads = attend_backward(
-                queries, key_rows, values, segment, log_total, grad_context, group_heads
-            )
-            return tuple(grad.astype(jnp.bfloat16) for grad in grads)
-
-        if parts:
-            grad_context = after(grad_context, parts[-1])
-        parts.append(
-            ticks.tick(
-                heads_back,
-                (
-                    queries[:, columns],
-                    key_rows[:, columns],
-                    values[:, columns],
-                    grad_context[:, columns],
-                    log_total[:, group * group_heads : (group + 1) * group_heads],
-                ),
-            )
-        )
-    grad_joint = jnp.concatenate(
-        [parts[group][which] for which in range(3) for group in range(groups)], axis=1
-    )
-    grad_query_bias = jnp.sum(grad_joint[:, :model_width].astype(jnp.float32), axis=0)
-    grad_value_bias = jnp.sum(grad_joint[:, 2 * model_width :].astype(jnp.float32), axis=0)
+    joint_parts = []
 
     def joint_back(tokens, grad_joint):
         return jnp.einsum(
             "td,te->de", tokens, grad_joint, preferred_element_type=jnp.float32
         ).astype(jnp.bfloat16)
 
-    grad_joint_weight = ticks.tick(joint_back, (tokens, grad_joint))
-    ticks.begin("grad_joint", reduce_chunk(links, [grad_joint_weight]))
+    for group in range(groups):
+
+        def heads_back(queries, key_rows, values, grad_context, log_total, *before):
+            grads = attend_backward(
+                queries, key_rows, values, segment, log_total, grad_context, group_heads
+            )
+            grads = tuple(grad.astype(jnp.bfloat16) for grad in grads)
+            return grads, [joint_back(tokens, grad_joint) for grad_joint in before]
+
+        part, weight_grad = ticks.tick(
+            heads_back,
+            (
+                columns_of(queries, group),
+                columns_of(key_rows, group),
+                columns_of(values, group),
+                columns_of(grad_context, group),
+                log_totals[group],
+                *joint_parts[-1:],
+            ),
+        )
+        if weight_grad:
+            ticks.begin("grad_joint%d" % (group - 1), reduce_chunk(links, weight_grad))
+        parts.append(part)
+        joint_parts.append(jnp.concatenate(part, axis=1))
+    grad_joint = jnp.concatenate(
+        [parts[group][which] for which in range(3) for group in range(groups)], axis=1
+    )
+    grad_query_bias = jnp.sum(grad_joint[:, :model_width].astype(jnp.float32), axis=0)
+    grad_value_bias = jnp.sum(grad_joint[:, 2 * model_width :].astype(jnp.float32), axis=0)
+    weight_grad = ticks.tick(joint_back, (tokens, joint_parts[-1]))
+    ticks.begin("grad_joint%d" % (groups - 1), reduce_chunk(links, [weight_grad]))
     vectors = [
         grad_query_bias,
         grad_value_bias,
@@ -488,8 +511,12 @@
         ).astype(jnp.bfloat16)
 
     grad_tokens = ticks.tick(tokens_back, (grad_one, grad_joint))
-    (sum_joint,), (sum_expand, sum_output), (sum_reduce,), summed = ticks.finish(
-        "grad_joint", "grad_wide", "grad_reduce", "grad_small"
+    joint_names = ["grad_joint%d" % group for group in range(groups)]
+    (sum_expand, sum_output), (sum_reduce,), summed, *joint_sums = ticks.finish(
+        "grad_wide", "grad_reduce", "grad_small", *joint_names
+    )
+    sum_joint = jnp.concatenate(
+        [columns_of(joint_sum, which) for which in range(3) for (joint_sum,) in joint_sums], axis=1
     )
     shard = lax.axis_index("shard")
     small_sums = []

time: 538 us -> 551 us (1.024)
  other arithmetic: 90 us -> 126 us
  starting transfers between devices: 52 us -> 45.7 us
  waiting for transfers between devices: 190 us -> 184 us
    another operation x1 -> x9, other arithmetic: 0.18 us -> 31.4 us  [the longest x8 31.2 us: gather_chunk(): whole = jnp.stack([first, second], axis=2)]
    dynamic_update_slice x6 -> x0, local copies, waits for them, and re-layouts: 18.4 us -> none  [gather_chunk(): lax.dynamic_update_slice(whole, block, (zero, zero, side, zero, zero))]
    slice x6 -> x16, local copies, waits for them, and re-layouts: 6.21 us -> 20.9 us  [columns_of(): return array[:, group * group_width:(group + 1) * group_width]]
    broadcast_in_dim x4 -> x0, local copies, waits for them, and re-layouts: 7.39 us -> none  [gather_chunk(): whole = jnp.zeros((lead, 4, 2, quarter, size), part.dtype)]
    ppermute x44 -> x51, starting transfers between devices: 52 us -> 45.7 us  [send(): return lax.ppermute(array, ('rep', 'shard'), pairs)]
    ppermute x44 -> x51, waiting for transfers between devices: 190 us -> 184 us  [send(): return lax.ppermute(array, ('rep', 'shard'), pairs)]
    reduce_sum x1 -> x2, other arithmetic: 9.16 us -> 3.46 us  [one_block(): row_total = jnp.sum(powers, axis=-1, keepdims=True)]
    dot_general x3 -> x4, matrix products: 12.5 us -> 7.64 us  [block_scores(): jnp.einsum('qhd,khd->hqk', query_block, key_heads, preferred_element_type...]
  transfers between devices with their start and end apart: 44 -> 51, of which waited for: 21 -> 27; matrix products, arithmetic and copies ran while one was open for 29% -> 25% of each run, Pallas kernels for 0% -> 0%
where the time goes in v3:
time: 551 us; the launch traced here: 545 us
  waiting for transfers between devices  184 us (33%)
  other arithmetic  126 us (23%)
  matrix products  105 us (19%)
  local copies, waits for them, and re-layouts  81.9 us (15%)
  starting transfers between devices  45.7 us (8%)
    ppermute x51, waiting for transfers between devices, send(): return lax.ppermute(array, ('rep', 'shard'), pairs)  184 us
    ppermute x51, starting transfers between devices, send(): return lax.ppermute(array, ('rep', 'shard'), pairs)  45.7 us
    another operation x8, other arithmetic, gather_chunk(): whole = jnp.stack([first, second], axis=2)  31.2 us
    unnamed x217, local copies, waits for them, and re-layouts  26.3 us
    slice x16, local copies, waits for them, and re-layouts, columns_of(): return array[:, group * group_width:(group + 1) * group_width]  20.9 us
    convert_element_type x16, other arithmetic, add_low(): (mine.astype(jnp.float32) + got.astype(jnp.float32)).astype(jnp.bfloat16)  20.2 us
    squeeze x15, local copies, waits for them, and re-layouts, take(): return lax.dynamic_index_in_dim(array, index, axis, keepdims=False)  13.7 us
    dot_general x1, matrix products, hidden_back(): jnp.einsum('td,fd->tf', grad_second, reduce_full, preferred_element_type=...  11.2 us
  transfers between devices with their start and end apart: 51, of which 27 were waited for; matrix products, arithmetic and copies ran while one was open for 25% of the time, Pallas kernels for 0%

profile of v3, /device:TPU:0, one launch (start us, length us, event | category | flops | bytes accessed | tf_op | source)
XLA Modules:
  0.0 545.0 jit_solution(1881158209466654100)
XLA Ops:
  9.3 4.1 collective-permute-start
  17.5 5.0 collective-permute-done
  25.8 7.3 %collective-permute-done.3 = bf16[2,1536]{1,0:T(2,128)(2,1)S(1)} collective-permute-done((bf16[2,1536]{1,0:T(2,128)(2,1)S(1)}, bf16[2,1536]{1,0:T(2,128)(2,1)S(1)}, u32[]{:S(2)}, u32[]{:S(2)}) %collective-permute-start.3) | collective-permute-done | bytes 6176 | tf_op jit(solution)/shard_map/ppermute | solution.py:143
  34.6 3.3 collective-permute-start.6
  37.9 14.8 %collective-permute-done.5 = bf16[4,1536]{1,0:T(4,128)(2,1)S(1)} collective-permute-done((bf16[4,1536]{1,0:T(4,128)(2,1)S(1)}, bf16[4,1536]{1,0:T(4,128)(2,1)S(1)}, u32[]{:S(2)}, u32[]{:S(2)}) %collective-permute-start.5) | collective-permute-done | bytes 12320 | tf_op jit(solution)/shard_map/ppermute | solution.py:143
  57.4 16.4 %collective-permute-done.8 = bf16[2,32,5120]{2,1,0:T(8,128)(2,1)S(1)} collective-permute-done((bf16[2,32,5120]{2,1,0:T(8,128)(2,1)}, bf16[2,32,5120]{2,1,0:T(8,128)(2,1)S(1)}, u32[]{:S(2)}, u32[]{:S(2)}) %collective-permute-start.8) | collective-permute-done | bytes 655392 | tf_op jit(solution)/shard_map/ppermute | solution.py:143
  73.8 3.0 collective-permute-done.7
  84.9 13.3 %collective-permute-done.11 = bf16[1,128,1024]{2,1,0:T(8,128)(2,1)S(1)} collective-permute-done((bf16[1,128,1024]{2,1,0:T(8,128)(2,1)S(1)}, bf16[1,128,1024]{2,1,0:T(8,128)(2,1)S(1)}, u32[]{:S(2)}, u32[]{:S(2)}) %collective-permute-start.11) | collective-permute-done | bytes 262176 | tf_op jit(solution)/shard_map/ppermute | solution.py:143
  99.1 3.3 select_bitcast_fusion.5
  103.9 4.1 pad_maximum_fusion.10
  108.1 5.1 fusion.84
  129.1 3.2 fusion.30
  135.3 3.2 collective-permute-done.13
  138.5 16.9 %collective-permute-done.12 = bf16[4,2,32,5120]{3,2,1,0:T(8,128)(2,1)S(1)} collective-permute-done((bf16[4,2,32,5120]{3,2,1,0:T(8,128)(2,1)}, bf16[4,2,32,5120]{3,2,1,0:T(8,128)(2,1)S(1)}, u32[]{:S(2)}, u32[]{:S(2)}) %collective-permute-start.12) | collective-permute-done | bytes 2621472 | tf_op jit(solution)/shard_map/ppermute | solution.py:143
  157.8 3.1 pad_maximum_fusion.4
  178.6 4.0 collective-permute-done.15
  184.7 5.1 select_bitcast_fusion.3
  191.4 6.4 %pad_maximum_fusion = bf16[4,4,2,32,4096]{4,3,2,1,0:T(8,128)(2,1)} fusion(bf16[4,4,1,32,4096]{4,3,2,1,0:T(8,128)(2,1)} %get-tuple-element.451, bf16[4,4,1,32,4096]{4,3,2,1,0:T(8,128)(2,1)S(1)} %get-tuple-element.450), kind=kLoop, calls=%fused_computation.1 | loop fusion | flops 4194304 | bytes 16777216 | tf_op jit(solution)/shard_map/stack | solution.py:202
  204.9 7.8 %multiply_convert_fusion.2 = (bf16[512,4096]{1,0:T(8,128)(2,1)}, f32[512,4096]{1,0:T(8,128)}) fusion(f32[4096]{0:T(1024)S(1)} %bitcast.476, bf16[512,1024]{1,0:T(8,128)(2,1)S(1)} %get-tuple-element.327, bf16[1024,4096]{1,0:T(8,128)(2,1)S(1)} %bitcast.366), kind=kOutput, calls=%fused_computation.13 | convolution fusion | flops 4307550208 | bytes 22036480 | tf_op jit(solution)/shard_map/dot_general | solution.py:400
  212.7 15.4 %collective-permute-done.16 = bf16[4,2,128,1024]{3,2,1,0:T(8,128)(2,1)S(1)} collective-permute-done((bf16[4,2,128,1024]{3,2,1,0:T(8,128)(2,1)S(1)}, bf16[4,2,128,1024]{3,2,1,0:T(8,128)(2,1)S(1)}, u32[]{:S(2)}, u32[]{:S(2)}) %collective-permute-start.16) | collective-permute-done | bytes 2097184 | tf_op jit(solution)/shard_map/ppermute | solution.py:143
  232.5 7.5 %collective-permute-done.17 = bf16[4,4,128,1024]{3,2,1,0:T(8,128)(2,1)} collective-permute-done((bf16[4,4,128,1024]{3,2,1,0:T(8,128)(2,1)}, bf16[4,4,128,1024]{3,2,1,0:T(8,128)(2,1)}, u32[]{:S(2)}, u32[]{:S(2)}) %collective-permute-start.17) | collective-permute-done | bytes 4194336 | tf_op jit(solution)/shard_map/ppermute | solution.py:143
  240.0 6.1 %select_bitcast_fusion.1 = (bf16[4,4,1,128,1024]{4,3,2,1,0:T(8,128)(2,1)}, bf16[4,4,1,128,1024]{4,3,2,1,0:T(8,128)(2,1)}) fusion(bf16[4,4,128,1024]{3,2,1,0:T(8,128)(2,1)} %collective-permute-done.17, pred[]{:T(512)S(6)} %eq.168, bf16[4,1,128,1024]{3,2,1,0:T(8,128)(2,1)} %copy-done.9, bf16[4,1,128,1024]{3,2,1,0:T(8,128)(2,1)} %copy-done.10, ...), kind=kLoop, calls=%fused_computation.39 | loop fusion | flops 10485760 | bytes 16777216 | tf_op jit(solution)/shard_map/stack | solution.py:202
  246.1 7.6 %pad_maximum_fusion.1 = bf16[4,4,2,128,1024]{4,3,2,1,0:T(8,128)(2,1)} fusion(bf16[4,4,1,128,1024]{4,3,2,1,0:T(8,128)(2,1)} %get-tuple-element.455, bf16[4,4,1,128,1024]{4,3,2,1,0:T(8,128)(2,1)} %get-tuple-element.454), kind=kLoop, calls=%fused_computation.2 | loop fusion | flops 4194304 | bytes 16777216 | tf_op jit(solution)/shard_map/stack | solution.py:202
  253.6 8.3 %fusion.86 = f32[512,1024]{1,0:T(8,128)S(1)} fusion(bf16[512,4096]{1,0:T(8,128)(2,1)} %get-tuple-element.320, bf16[4096,1024]{1,0:T(8,128)(2,1)} %bitcast.367), kind=kOutput, calls=%fused_computation.293 | convolution fusion | flops 4294967296 | bytes 14680064 | tf_op jit(solution)/shard_map/dot_general | solution.py:407
  269.5 4.8 convolution_convert_fusion.1
  274.3 3.1 dynamic-slice_bitcast_fusion.2
  284.2 11.2 %add_convert_fusion.1 = bf16[512,4096]{1,0:T(8,128)(2,1)S(1)} fusion(f32[512,4096]{1,0:T(8,128)} %get-tuple-element.325, bf16[512,1024]{1,0:T(8,128)(2,1)S(1)} %copy-done.66, bf16[4096,1024]{1,0:T(8,128)(2,1)} %bitcast.368), kind=kOutput, calls=%fused_computation.12 | convolution fusion | flops 4322230272 | bytes 22020096 | tf_op jit(solution)/shard_map/td,fd->tf/dot_general | solution.py:422
  295.5 7.1 %convolution_convert_fusion = bf16[1024,4096]{1,0:T(8,128)(2,1)} fusion(bf16[512,1024]{1,0:T(8,128)(2,1)S(1)} %copy-done.64, bf16[512,4096]{1,0:T(8,128)(2,1)S(1)} %add_convert_fusion.1), kind=kOutput, calls=%fused_computation.20 | convolution fusion | flops 4299161600 | bytes 13631488 | tf_op jit(solution)/shard_map/td,tf->df/dot_general | solution.py:427
  302.6 4.3 fusion
  310.8 10.2 %multiply_reduce_fusion.3 = (f32[1024]{0:T(1024)S(1)}, f32[512]{0:T(512)S(1)}, f32[1024]{0:T(1024)S(1)}, f32[512,1024]{1,0:T(8,128)S(1)}) fusion(f32[512,1024]{1,0:T(8,128)S(1)} %get-tuple-element.334, f32[512]{0:T(512)S(1)} %fusion.65, f32[512]{0:T(512)S(1)} %broadcast_multiply_fusion, f32[1024]{0:T(1024)S(1)} %get-tuple-element.505, ...), kind=kOutput, calls=%fused_computation.85 | convolution fusion | flops 4299683328 | bytes 18892800 | tf_op jit(solution)/shard_map/tf,df->td/dot_general | solution.py:436
  329.4 7.1 %collective-permute-done.19 = bf16[4,2,128,1024]{3,2,0,1:T(8,128)(2,1)} collective-permute-done((bf16[4,2,128,1024]{3,2,0,1:T(8,128)(2,1)}, bf16[4,2,128,1024]{3,2,0,1:T(8,128)(2,1)}, u32[]{:S(2)}, u32[]{:S(2)}) %collective-permute-start.19) | collective-permute-done | bytes 2097184 | tf_op jit(solution)/shard_map/ppermute | solution.py:143
  336.5 3.2 convolution_convert_fusion.5
  348.6 3.2 convert_reduce_fusion
  355.6 3.0 multiply_reduce_fusion.1
  364.4 3.1 fusion.31
  368.8 5.9 %add_convert_fusion = bf16[4,4,32,5120]{3,2,1,0:T(8,128)(2,1)S(1)} fusion(bf16[4,4,32,5120]{3,2,1,0:T(8,128)(2,1)} %collective-permute-done.21, bf16[4,4,32,1024]{3,2,1,0:T(8,128)(2,1)} %get-tuple-element.477, bf16[4,4,32,4096]{3,2,1,0:T(8,128)(2,1)} %get-tuple-element.452), kind=kLoop, calls=%fused_computation | loop fusion | flops 18350080 | bytes 15728640 | tf_op jit(solution)/shard_map/convert_element_type | solution.py:166
  390.9 3.1 multiply_convert_fusion
  399.6 3.5 fusion.15
  403.1 14.1 %collective-permute-done.23 = bf16[4,2,32,5120]{3,2,0,1:T(8,128)(2,1)S(1)} collective-permute-done((bf16[4,2,32,5120]{3,2,0,1:T(8,128)(2,1)}, bf16[4,2,32,5120]{3,2,0,1:T(8,128)(2,1)S(1)}, u32[]{:S(2)}, u32[]{:S(2)}) %collective-permute-start.23) | collective-permute-done | bytes 2621472 | tf_op jit(solution)/shard_map/ppermute | solution.py:143
  420.0 4.8 copy.167
  434.2 11.8 %collective-permute-done.24 = bf16[1,128,1024]{2,1,0:T(8,128)(2,1)S(1)} collective-permute-done((bf16[1,128,1024]{2,1,0:T(8,128)(2,1)S(1)}, bf16[1,128,1024]{2,1,0:T(8,128)(2,1)S(1)}, u32[]{:S(2)}, u32[]{:S(2)}) %collective-permute-start.24) | collective-permute-done | bytes 262176 | tf_op jit(solution)/shard_map/ppermute | solution.py:143
  457.8 8.2 %add_convert_fusion.3 = bf16[512,1024]{1,0:T(8,128)(2,1)} fusion(f32[512,1024]{1,0:T(8,128)S(1)} %copy-done.44, bf16[512,3072]{0,1:T(8,128)(2,1)} %copy-done.78, bf16[1024,3072]{1,0:T(8,128)(2,1)} %bitcast.388), kind=kOutput, calls=%fused_computation.79 | convolution fusion | flops 3222274048 | bytes 12582912 | tf_op jit(solution)/shard_map/te,de->td/dot_general | solution.py:510
  466.0 6.9 %collective-permute-done.27 = bf16[128,1024]{1,0:T(8,128)(2,1)S(1)} collective-permute-done((bf16[128,1024]{1,0:T(8,128)(2,1)S(1)}, bf16[128,1024]{1,0:T(8,128)(2,1)S(1)}, u32[]{:S(2)}, u32[]{:S(2)}) %collective-permute-start.27) | collective-permute-done | bytes 262176 | tf_op jit(solution)/shard_map/ppermute | solution.py:143
  481.2 12.3 %collective-permute-done.36 = f32[12288]{0:T(1024)S(1)} collective-permute-done((f32[12288]{0:T(1024)S(1)}, f32[12288]{0:T(1024)S(1)}, u32[]{:S(2)}, u32[]{:S(2)}) %collective-permute-start.36) | collective-permute-done | bytes 49184 | tf_op jit(solution)/shard_map/ppermute | solution.py:143
  503.9 3.5 collective-permute-done.40
  517.0 3.4 collective-permute-start.42
  521.5 5.3 collective-permute-done.44
  533.1 3.4 collective-permute-done.47
  (478 shorter events, 221.3 us)
Async XLA Ops:
  9.3 13.2 %collective-permute-start = (bf16[1,32,3072]{2,1,0:T(8,128)(2,1)S(1)}, bf16[1,32,3072]{2,1,0:T(8,128)(2,1)S(1)}, u32[]{:S(2)}, u32[]{:S(2)}) collective-permute-start(bf16[1,32,3072]{2,1,0:T(8,128)(2,1)S(1)} %fusion.140), channel_id=1, source_target_pairs={{0,4},{1,5},{2,6},{3,7},{4,0},{5,1},{6,2},{7,3},{8,12},{9,13},{10,... | collective-permute-start | bytes 589832 | tf_op jit(solution)/shard_map/ppermute | solution.py:143
  22.6 10.5 %collective-permute-start.2 = (bf16[2,32,3072]{2,1,0:T(8,128)(2,1)S(1)}, bf16[2,32,3072]{2,1,0:T(8,128)(2,1)S(1)}, u32[]{:S(2)}, u32[]{:S(2)}) collective-permute-start(bf16[2,32,3072]{2,1,0:T(8,128)(2,1)S(1)} %maximum_select_fusion.14), channel_id=1, source_target_pairs={{0,2},{1,3},{2,0},{3,1},{4,6},{5,7},{6,4},{7,5},{8,10},{9,11},{10,... | collective-permute-start | bytes 1179656 | tf_op jit(solution)/shard_map/ppermute | solution.py:143
  24.3 8.8 %collective-permute-start.3 = (bf16[2,1536]{1,0:T(2,128)(2,1)S(1)}, bf16[2,1536]{1,0:T(2,128)(2,1)S(1)}, u32[]{:S(2)}, u32[]{:S(2)}) collective-permute-start(bf16[2,1536]{1,0:T(2,128)(2,1)S(1)} %broadcast_select_fusion), channel_id=1, source_target_pairs={{0,2},{1,3},{2,0},{3,1},{4,6},{5,7},{6,4},{7,5},{8,10},{9,11},{10,... | collective-permute-start | bytes 18440 | tf_op jit(solution)/shard_map/ppermute | solution.py:143
  33.2 19.5 %collective-permute-start.4 = (bf16[4,32,3072]{2,1,0:T(8,128)(2,1)S(1)}, bf16[4,32,3072]{2,1,0:T(8,128)(2,1)S(1)}, u32[]{:S(2)}, u32[]{:S(2)}) collective-permute-start(bf16[4,32,3072]{2,1,0:T(8,128)(2,1)S(1)} %bitcast.384), channel_id=1, source_target_pairs={{0,1},{1,0},{2,3},{3,2},{4,5},{5,4},{6,7},{7,6},{8,24},{9,25},{10,... | collective-permute-start | bytes 2359304 | tf_op jit(solution)/shard_map/ppermute | solution.py:143
  34.6 18.2 %collective-permute-start.6 = (bf16[1,32,5120]{2,1,0:T(8,128)(2,1)}, bf16[1,32,5120]{2,1,0:T(8,128)(2,1)S(1)}, u32[]{:S(2)}, u32[]{:S(2)}) collective-permute-start(bf16[1,32,5120]{2,1,0:T(8,128)(2,1)} %get-tuple-element.283), channel_id=1, source_target_pairs={{0,4},{1,5},{2,6},{3,7},{4,0},{5,1},{6,2},{7,3},{8,12},{9,13},{10,... | collective-permute-start | bytes 983048 | tf_op jit(solution)/shard_map/ppermute | solution.py:143
  37.9 14.8 %collective-permute-start.5 = (bf16[4,1536]{1,0:T(4,128)(2,1)S(1)}, bf16[4,1536]{1,0:T(4,128)(2,1)S(1)}, u32[]{:S(2)}, u32[]{:S(2)}) collective-permute-start(bf16[4,1536]{1,0:T(4,128)(2,1)S(1)} %maximum_select_fusion.21), channel_id=1, source_target_pairs={{0,4},{1,5},{2,6},{3,7},{4,0},{5,1},{6,2},{7,3},{8,12},{9,13},{10,... | collective-permute-start | bytes 36872 | tf_op jit(solution)/shard_map/ppermute | solution.py:143
  56.1 20.7 %collective-permute-start.7 = (bf16[4,2,32,3072]{3,2,1,0:T(8,128)(2,1)}, bf16[4,2,32,3072]{3,2,1,0:T(8,128)(2,1)}, u32[]{:S(2)}, u32[]{:S(2)}) collective-permute-start(bf16[4,2,32,3072]{3,2,1,0:T(8,128)(2,1)} %pad_maximum_fusion.15), channel_id=1, source_target_pairs={{0,16},{1,17},{2,18},{3,19},{4,20},{5,21},{6,22},{7,23},{8,9},{9,8... | collective-permute-start | bytes 4718600 | tf_op jit(solution)/shard_map/ppermute | solution.py:143
  56.6 17.2 %collective-permute-start.8 = (bf16[2,32,5120]{2,1,0:T(8,128)(2,1)}, bf16[2,32,5120]{2,1,0:T(8,128)(2,1)S(1)}, u32[]{:S(2)}, u32[]{:S(2)}) collective-permute-start(bf16[2,32,5120]{2,1,0:T(8,128)(2,1)} %maximum_select_fusion.5), channel_id=1, source_target_pairs={{0,2},{1,3},{2,0},{3,1},{4,6},{5,7},{6,4},{7,5},{8,10},{9,11},{10,... | collective-permute-start | bytes 1966088 | tf_op jit(solution)/shard_map/ppermute | solution.py:143
  81.4 17.7 %collective-permute-start.9 = (bf16[4,4,32,3072]{3,2,1,0:T(8,128)(2,1)}, bf16[4,4,32,3072]{3,2,1,0:T(8,128)(2,1)}, u32[]{:S(2)}, u32[]{:S(2)}) collective-permute-start(bf16[4,4,32,3072]{3,2,1,0:T(8,128)(2,1)} %pad_maximum_fusion.9), channel_id=1, source_target_pairs={{0,8},{1,9},{2,10},{3,11},{4,12},{5,13},{6,14},{7,15},{8,0},{9,1},... | collective-permute-start | bytes 9437192 | tf_op jit(solution)/shard_map/ppermute | solution.py:143
  81.4 17.7 %collective-permute-start.10 = (bf16[4,32,5120]{2,1,0:T(8,128)(2,1)S(1)}, bf16[4,32,5120]{2,1,0:T(8,128)(2,1)}, u32[]{:S(2)}, u32[]{:S(2)}) collective-permute-start(bf16[4,32,5120]{2,1,0:T(8,128)(2,1)S(1)} %bitcast.357), channel_id=1, source_target_pairs={{0,1},{1,0},{2,3},{3,2},{4,5},{5,4},{6,7},{7,6},{8,24},{9,25},{10,... | collective-permute-start | bytes 3932168 | tf_op jit(solution)/shard_map/ppermute | solution.py:143
  84.1 14.0 %collective-permute-start.11 = (bf16[1,128,1024]{2,1,0:T(8,128)(2,1)S(1)}, bf16[1,128,1024]{2,1,0:T(8,128)(2,1)S(1)}, u32[]{:S(2)}, u32[]{:S(2)}) collective-permute-start(bf16[1,128,1024]{2,1,0:T(8,128)(2,1)S(1)} %fusion.139), channel_id=1, source_target_pairs={{0,4},{1,5},{2,6},{3,7},{4,0},{5,1},{6,2},{7,3},{8,12},{9,13},{10,... | collective-permute-start | bytes 786440 | tf_op jit(solution)/shard_map/ppermute | solution.py:143
  123.6 31.9 %collective-permute-start.12 = (bf16[4,2,32,5120]{3,2,1,0:T(8,128)(2,1)}, bf16[4,2,32,5120]{3,2,1,0:T(8,128)(2,1)S(1)}, u32[]{:S(2)}, u32[]{:S(2)}) collective-permute-start(bf16[4,2,32,5120]{3,2,1,0:T(8,128)(2,1)} %pad_maximum_fusion.10), channel_id=1, source_target_pairs={{0,16},{1,17},{2,18},{3,19},{4,20},{5,21},{6,22},{7,23},{8,9},{9,8... | collective-permute-start | bytes 7864328 | tf_op jit(solution)/shard_map/ppermute | solution.py:143
  124.2 14.3 %collective-permute-start.13 = (bf16[2,128,1024]{2,1,0:T(8,128)(2,1)}, bf16[2,128,1024]{2,1,0:T(8,128)(2,1)S(1)}, u32[]{:S(2)}, u32[]{:S(2)}) collective-permute-start(bf16[2,128,1024]{2,1,0:T(8,128)(2,1)} %maximum_select_fusion.10), channel_id=1, source_target_pairs={{0,2},{1,3},{2,0},{3,1},{4,6},{5,7},{6,4},{7,5},{8,10},{9,11},{10,... | collective-permute-start | bytes 1572872 | tf_op jit(solution)/shard_map/ppermute | solution.py:143
  160.9 21.7 %collective-permute-start.14 = (bf16[4,4,32,5120]{3,2,1,0:T(8,128)(2,1)}, bf16[4,4,32,5120]{3,2,1,0:T(8,128)(2,1)}, u32[]{:S(2)}, u32[]{:S(2)}) collective-permute-start(bf16[4,4,32,5120]{3,2,1,0:T(8,128)(2,1)} %pad_maximum_fusion.4), channel_id=1, source_target_pairs={{0,8},{1,9},{2,10},{3,11},{4,12},{5,13},{6,14},{7,15},{8,0},{9,1},... | collective-permute-start | bytes 15728648 | tf_op jit(solution)/shard_map/ppermute | solution.py:143
  167.7 14.9 %collective-permute-start.15 = (bf16[4,128,1024]{2,1,0:T(8,128)(2,1)S(1)}, bf16[4,128,1024]{2,1,0:T(8,128)(2,1)S(1)}, u32[]{:S(2)}, u32[]{:S(2)}) collective-permute-start(bf16[4,128,1024]{2,1,0:T(8,128)(2,1)S(1)} %bitcast.360), channel_id=1, source_target_pairs={{0,1},{1,0},{2,3},{3,2},{4,5},{5,4},{6,7},{7,6},{8,24},{9,25},{10,... | collective-permute-start | bytes 3145736 | tf_op jit(solution)/shard_map/ppermute | solution.py:143
  202.0 26.1 %collective-permute-start.16 = (bf16[4,2,128,1024]{3,2,1,0:T(8,128)(2,1)S(1)}, bf16[4,2,128,1024]{3,2,1,0:T(8,128)(2,1)S(1)}, u32[]{:S(2)}, u32[]{:S(2)}) collective-permute-start(bf16[4,2,128,1024]{3,2,1,0:T(8,128)(2,1)S(1)} %pad_maximum_fusion.12), channel_id=1, source_target_pairs={{0,16},{1,17},{2,18},{3,19},{4,20},{5,21},{6,22},{7,23},{8,9},{9,8... | collective-permute-start | bytes 6291464 | tf_op jit(solution)/shard_map/ppermute | solution.py:143
  232.5 7.5 %collective-permute-start.17 = (bf16[4,4,128,1024]{3,2,1,0:T(8,128)(2,1)}, bf16[4,4,128,1024]{3,2,1,0:T(8,128)(2,1)}, u32[]{:S(2)}, u32[]{:S(2)}) collective-permute-start(bf16[4,4,128,1024]{3,2,1,0:T(8,128)(2,1)} %pad_maximum_fusion.7), channel_id=1, source_target_pairs={{0,8},{1,9},{2,10},{3,11},{4,12},{5,13},{6,14},{7,15},{8,0},{9,1},... | collective-permute-start | bytes 12582920 | tf_op jit(solution)/shard_map/ppermute | solution.py:143
  278.9 23.7 %collective-permute-start.18 = (bf16[4,4,128,1024]{3,2,1,0:T(8,128)(2,1)}, bf16[4,4,128,1024]{3,2,1,0:T(8,128)(2,1)}, u32[]{:S(2)}, u32[]{:S(2)}) collective-permute-start(bf16[4,4,128,1024]{3,2,1,0:T(8,128)(2,1)} %dynamic-slice_bitcast_fusion.2), channel_id=1, source_target_pairs={{0,8},{1,9},{2,10},{3,11},{4,12},{5,13},{6,14},{7,15},{8,0},{9,1},... | collective-permute-start | bytes 12582920 | tf_op jit(solution)/shard_map/ppermute | solution.py:143
  310.1 26.4 %collective-permute-start.19 = (bf16[4,2,128,1024]{3,2,0,1:T(8,128)(2,1)}, bf16[4,2,128,1024]{3,2,0,1:T(8,128)(2,1)}, u32[]{:S(2)}, u32[]{:S(2)}) collective-permute-start(bf16[4,2,128,1024]{3,2,0,1:T(8,128)(2,1)} %pad_maximum_fusion.14), channel_id=1, source_target_pairs={{0,16},{1,17},{2,18},{3,19},{4,20},{5,21},{6,22},{7,23},{8,9},{9,8... | collective-permute-start | bytes 6291464 | tf_op jit(solution)/shard_map/ppermute | solution.py:143
  348.3 19.5 %collective-permute-start.21 = (bf16[4,4,32,5120]{3,2,1,0:T(8,128)(2,1)}, bf16[4,4,32,5120]{3,2,1,0:T(8,128)(2,1)}, u32[]{:S(2)}, u32[]{:S(2)}) collective-permute-start(bf16[4,4,32,5120]{3,2,1,0:T(8,128)(2,1)} %pad_maximum_fusion.5), channel_id=1, source_target_pairs={{0,8},{1,9},{2,10},{3,11},{4,12},{5,13},{6,14},{7,15},{8,0},{9,1},... | collective-permute-start | bytes 15728648 | tf_op jit(solution)/shard_map/ppermute | solution.py:143
  352.7 15.1 %collective-permute-start.20 = (bf16[4,128,1024]{2,1,0:T(8,128)(2,1)}, bf16[4,128,1024]{2,1,0:T(8,128)(2,1)S(1)}, u32[]{:S(2)}, u32[]{:S(2)}) collective-permute-start(bf16[4,128,1024]{2,1,0:T(8,128)(2,1)} %fusion.41), channel_id=1, source_target_pairs={{0,1},{1,0},{2,3},{3,2},{4,5},{5,4},{6,7},{7,6},{8,24},{9,25},{10,... | collective-permute-start | bytes 3145736 | tf_op jit(solution)/shard_map/ppermute | solution.py:143
  385.3 31.9 %collective-permute-start.23 = (bf16[4,2,32,5120]{3,2,0,1:T(8,128)(2,1)}, bf16[4,2,32,5120]{3,2,0,1:T(8,128)(2,1)S(1)}, u32[]{:S(2)}, u32[]{:S(2)}) collective-permute-start(bf16[4,2,32,5120]{3,2,0,1:T(8,128)(2,1)} %pad_maximum_fusion.11), channel_id=1, source_target_pairs={{0,16},{1,17},{2,18},{3,19},{4,20},{5,21},{6,22},{7,23},{8,9},{9,8... | collective-permute-start | bytes 7864328 | tf_op jit(solution)/shard_map/ppermute | solution.py:143
  386.1 17.1 %collective-permute-start.22 = (bf16[2,128,1024]{2,1,0:T(8,128)(2,1)}, bf16[2,128,1024]{2,1,0:T(8,128)(2,1)}, u32[]{:S(2)}, u32[]{:S(2)}) collective-permute-start(bf16[2,128,1024]{2,1,0:T(8,128)(2,1)} %dynamic-slice_bitcast_fusion.12), channel_id=1, source_target_pairs={{0,2},{1,3},{2,0},{3,1},{4,6},{5,7},{6,4},{7,5},{8,10},{9,11},{10,... | collective-permute-start | bytes 1572872 | tf_op jit(solution)/shard_map/ppermute | solution.py:143
  430.3 17.8 %collective-permute-start.26 = (bf16[4,4,32,1536]{3,2,1,0:T(8,128)(2,1)S(1)}, bf16[4,4,32,1536]{3,2,1,0:T(8,128)(2,1)S(1)}, u32[]{:S(2)}, u32[]{:S(2)}) collective-permute-start(bf16[4,4,32,1536]{3,2,1,0:T(8,128)(2,1)S(1)} %dynamic-slice_bitcast_fusion.4), channel_id=1, source_target_pairs={{0,8},{1,9},{2,10},{3,11},{4,12},{5,13},{6,14},{7,15},{8,0},{9,1},... | collective-permute-start | bytes 4718600 | tf_op jit(solution)/shard_map/ppermute | solution.py:143
  430.4 17.7 %collective-permute-start.25 = (bf16[4,32,5120]{2,1,0:T(8,128)(2,1)S(1)}, bf16[4,32,5120]{2,1,0:T(8,128)(2,1)S(1)}, u32[]{:S(2)}, u32[]{:S(2)}) collective-permute-start(bf16[4,32,5120]{2,1,0:T(8,128)(2,1)S(1)} %fusion.27), channel_id=1, source_target_pairs={{0,1},{1,0},{2,3},{3,2},{4,5},{5,4},{6,7},{7,6},{8,24},{9,25},{10,... | collective-permute-start | bytes 3932168 | tf_op jit(solution)/shard_map/ppermute | solution.py:143
  432.0 14.0 %collective-permute-start.24 = (bf16[1,128,1024]{2,1,0:T(8,128)(2,1)S(1)}, bf16[1,128,1024]{2,1,0:T(8,128)(2,1)S(1)}, u32[]{:S(2)}, u32[]{:S(2)}) collective-permute-start(bf16[1,128,1024]{2,1,0:T(8,128)(2,1)S(1)} %constant_dynamic-slice_fusion.5), channel_id=1, source_target_pairs={{0,4},{1,5},{2,6},{3,7},{4,0},{5,1},{6,2},{7,3},{8,12},{9,13},{10,... | collective-permute-start | bytes 786440 | tf_op jit(solution)/shard_map/ppermute | solution.py:143
  455.0 18.6 %collective-permute-start.30 = (bf16[4,4,32,1536]{3,2,1,0:T(8,128)(2,1)}, bf16[4,4,32,1536]{3,2,1,0:T(8,128)(2,1)}, u32[]{:S(2)}, u32[]{:S(2)}) collective-permute-start(bf16[4,4,32,1536]{3,2,1,0:T(8,128)(2,1)} %dynamic-slice_bitcast_fusion.3), channel_id=1, source_target_pairs={{0,8},{1,9},{2,10},{3,11},{4,12},{5,13},{6,14},{7,15},{8,0},{9,1},... | collective-permute-start | bytes 4718600 | tf_op jit(solution)/shard_map/ppermute | solution.py:143
  455.0 18.5 %collective-permute-start.29 = (bf16[4,2,32,1536]{3,2,1,0:T(8,128)(2,1)}, bf16[4,2,32,1536]{3,2,1,0:T(8,128)(2,1)S(1)}, u32[]{:S(2)}, u32[]{:S(2)}) collective-permute-start(bf16[4,2,32,1536]{3,2,1,0:T(8,128)(2,1)} %pad_maximum_fusion.18), channel_id=1, source_target_pairs={{0,16},{1,17},{2,18},{3,19},{4,20},{5,21},{6,22},{7,23},{8,9},{9,8... | collective-permute-start | bytes 2359304 | tf_op jit(solution)/shard_map/ppermute | solution.py:143
  455.8 17.8 %collective-permute-start.28 = (bf16[2,32,5120]{2,1,0:T(8,128)(2,1)}, bf16[2,32,5120]{2,1,0:T(8,128)(2,1)S(1)}, u32[]{:S(2)}, u32[]{:S(2)}) collective-permute-start(bf16[2,32,5120]{2,1,0:T(8,128)(2,1)} %dynamic-slice_bitcast_fusion.11), channel_id=1, source_target_pairs={{0,2},{1,3},{2,0},{3,1},{4,6},{5,7},{6,4},{7,5},{8,10},{9,11},{10,... | collective-permute-start | bytes 1966088 | tf_op jit(solution)/shard_map/ppermute | solution.py:143
  456.3 16.6 %collective-permute-start.27 = (bf16[128,1024]{1,0:T(8,128)(2,1)S(1)}, bf16[128,1024]{1,0:T(8,128)(2,1)S(1)}, u32[]{:S(2)}, u32[]{:S(2)}) collective-permute-start(bf16[128,1024]{1,0:T(8,128)(2,1)S(1)} %bitcast.425), channel_id=1, source_target_pairs={{0,16},{1,17},{2,18},{3,19},{4,20},{5,21},{6,22},{7,23},{8,24},{9,... | collective-permute-start | bytes 786440 | tf_op jit(solution)/shard_map/ppermute | solution.py:143
  457.8 8.2 %collective-permute-start.31 = (f32[12288]{0:T(1024)S(1)}, f32[12288]{0:T(1024)S(1)}, u32[]{:S(2)}, u32[]{:S(2)}) collective-permute-start(f32[12288]{0:T(1024)S(1)} %constant_dynamic-update-slice_fusion.11), channel_id=1, source_target_pairs={{0,8},{1,9},{2,10},{3,11},{4,12},{5,13},{6,14},{7,15},{8,0},{9,1},... | collective-permute-start | bytes 147464 | tf_op jit(solution)/shard_map/ppermute | solution.py:143
  476.2 19.9 %collective-permute-start.35 = (bf16[4,2,32,1536]{3,2,0,1:T(8,128)(2,1)S(1)}, bf16[4,2,32,1536]{3,2,0,1:T(8,128)(2,1)S(1)}, u32[]{:S(2)}, u32[]{:S(2)}) collective-permute-start(bf16[4,2,32,1536]{3,2,0,1:T(8,128)(2,1)S(1)} %pad_maximum_fusion.19), channel_id=1, source_target_pairs={{0,16},{1,17},{2,18},{3,19},{4,20},{5,21},{6,22},{7,23},{8,9},{9,8... | collective-permute-start | bytes 2359304 | tf_op jit(solution)/shard_map/ppermute | solution.py:143
  476.9 19.2 %collective-permute-start.32 = (bf16[2,128,1024]{2,1,0:T(8,128)(2,1)S(1)}, bf16[2,128,1024]{2,1,0:T(8,128)(2,1)S(1)}, u32[]{:S(2)}, u32[]{:S(2)}) collective-permute-start(bf16[2,128,1024]{2,1,0:T(8,128)(2,1)S(1)} %maximum_select_fusion.11), channel_id=1, source_target_pairs={{0,8},{1,9},{2,10},{3,11},{4,12},{5,13},{6,14},{7,15},{8,0},{9,1},... | collective-permute-start | bytes 1572872 | tf_op jit(solution)/shard_map/ppermute | solution.py:143
  476.9 19.2 %collective-permute-start.34 = (bf16[4,32,1536]{2,1,0:T(8,128)(2,1)S(1)}, bf16[4,32,1536]{2,1,0:T(8,128)(2,1)S(1)}, u32[]{:S(2)}, u32[]{:S(2)}) collective-permute-start(bf16[4,32,1536]{2,1,0:T(8,128)(2,1)S(1)} %fusion.47), channel_id=1, source_target_pairs={{0,1},{1,0},{2,3},{3,2},{4,5},{5,4},{6,7},{7,6},{8,24},{9,25},{10,... | collective-permute-start | bytes 1179656 | tf_op jit(solution)/shard_map/ppermute | solution.py:143
  478.2 17.9 %collective-permute-start.33 = (bf16[1,32,5120]{2,1,0:T(8,128)(2,1)S(1)}, bf16[1,32,5120]{2,1,0:T(8,128)(2,1)S(1)}, u32[]{:S(2)}, u32[]{:S(2)}) collective-permute-start(bf16[1,32,5120]{2,1,0:T(8,128)(2,1)S(1)} %constant_dynamic-slice_fusion.2), channel_id=1, source_target_pairs={{0,4},{1,5},{2,6},{3,7},{4,0},{5,1},{6,2},{7,3},{8,12},{9,13},{10,... | collective-permute-start | bytes 983048 | tf_op jit(solution)/shard_map/ppermute | solution.py:143
  479.8 13.8 %collective-permute-start.36 = (f32[12288]{0:T(1024)S(1)}, f32[12288]{0:T(1024)S(1)}, u32[]{:S(2)}, u32[]{:S(2)}) collective-permute-start(f32[12288]{0:T(1024)S(1)} %add.600), channel_id=1, source_target_pairs={{0,16},{1,17},{2,18},{3,19},{4,20},{5,21},{6,22},{7,23},{8,24},{9,... | collective-permute-start | bytes 147464 | tf_op jit(solution)/shard_map/ppermute | solution.py:143
  498.3 11.7 %collective-permute-start.39 = (bf16[4,32,1536]{2,1,0:T(8,128)(2,1)}, bf16[4,32,1536]{2,1,0:T(8,128)(2,1)}, u32[]{:S(2)}, u32[]{:S(2)}) collective-permute-start(bf16[4,32,1536]{2,1,0:T(8,128)(2,1)} %fusion.48), channel_id=1, source_target_pairs={{0,1},{1,0},{2,3},{3,2},{4,5},{5,4},{6,7},{7,6},{8,24},{9,25},{10,... | collective-permute-start | bytes 1179656 | tf_op jit(solution)/shard_map/ppermute | solution.py:143
  499.2 10.8 %collective-permute-start.37 = (bf16[32,5120]{1,0:T(8,128)(2,1)S(1)}, bf16[32,5120]{1,0:T(8,128)(2,1)}, u32[]{:S(2)}, u32[]{:S(2)}) collective-permute-start(bf16[32,5120]{1,0:T(8,128)(2,1)S(1)} %bitcast.423), channel_id=1, source_target_pairs={{0,16},{1,17},{2,18},{3,19},{4,20},{5,21},{6,22},{7,23},{8,24},{9,... | collective-permute-start | bytes 983048 | tf_op jit(solution)/shard_map/ppermute | solution.py:143
  499.7 7.7 %collective-permute-start.38 = (bf16[2,32,1536]{2,1,0:T(8,128)(2,1)S(1)}, bf16[2,32,1536]{2,1,0:T(8,128)(2,1)S(1)}, u32[]{:S(2)}, u32[]{:S(2)}) collective-permute-start(bf16[2,32,1536]{2,1,0:T(8,128)(2,1)S(1)} %dynamic-slice_bitcast_fusion.17), channel_id=1, source_target_pairs={{0,2},{1,3},{2,0},{3,1},{4,6},{5,7},{6,4},{7,5},{8,10},{9,11},{10,... | collective-permute-start | bytes 589832 | tf_op jit(solution)/shard_map/ppermute | solution.py:143
  501.0 6.4 %collective-permute-start.40 = (f32[12288]{0:T(1024)}, f32[12288]{0:T(1024)S(1)}, u32[]{:S(2)}, u32[]{:S(2)}) collective-permute-start(f32[12288]{0:T(1024)} %add.604), channel_id=1, source_target_pairs={{0,1},{1,0},{2,3},{3,2},{4,5},{5,4},{6,7},{7,6},{8,9},{9,8},{10,11... | collective-permute-start | bytes 147464 | tf_op jit(solution)/shard_map/ppermute | solution.py:143
  513.2 13.6 %collective-permute-start.41 = (bf16[2,32,5120]{2,1,0:T(8,128)(2,1)S(1)}, bf16[2,32,5120]{2,1,0:T(8,128)(2,1)S(1)}, u32[]{:S(2)}, u32[]{:S(2)}) collective-permute-start(bf16[2,32,5120]{2,1,0:T(8,128)(2,1)S(1)} %maximum_select_fusion.7), channel_id=1, source_target_pairs={{0,8},{1,9},{2,10},{3,11},{4,12},{5,13},{6,14},{7,15},{8,0},{9,1},... | collective-permute-start | bytes 1966088 | tf_op jit(solution)/shard_map/ppermute | solution.py:143
  516.9 10.0 %collective-permute-start.43 = (bf16[2,32,1536]{2,1,0:T(8,128)(2,1)S(1)}, bf16[2,32,1536]{2,1,0:T(8,128)(2,1)S(1)}, u32[]{:S(2)}, u32[]{:S(2)}) collective-permute-start(bf16[2,32,1536]{2,1,0:T(8,128)(2,1)S(1)} %dynamic-slice_bitcast_fusion.16), channel_id=1, source_target_pairs={{0,2},{1,3},{2,0},{3,1},{4,6},{5,7},{6,4},{7,5},{8,10},{9,11},{10,... | collective-permute-start | bytes 589832 | tf_op jit(solution)/shard_map/ppermute | solution.py:143
  517.0 9.9 %collective-permute-start.42 = (bf16[1,32,1536]{2,1,0:T(8,128)(2,1)S(1)}, bf16[1,32,1536]{2,1,0:T(8,128)(2,1)S(1)}, u32[]{:S(2)}, u32[]{:S(2)}) collective-permute-start(bf16[1,32,1536]{2,1,0:T(8,128)(2,1)S(1)} %constant_dynamic-slice_fusion.1), channel_id=1, source_target_pairs={{0,4},{1,5},{2,6},{3,7},{4,0},{5,1},{6,2},{7,3},{8,12},{9,13},{10,... | collective-permute-start | bytes 294920 | tf_op jit(solution)/shard_map/ppermute | solution.py:143
  520.3 6.5 %collective-permute-start.44 = (f32[12288]{0:T(1024)S(1)}, f32[12288]{0:T(1024)S(1)}, u32[]{:S(2)}, u32[]{:S(2)}) collective-permute-start(f32[12288]{0:T(1024)S(1)} %add.609), channel_id=1, source_target_pairs={{0,2},{1,3},{2,0},{3,1},{4,6},{5,7},{6,4},{7,5},{8,10},{9,11},{10,... | collective-permute-start | bytes 147464 | tf_op jit(solution)/shard_map/ppermute | solution.py:143
  527.0 9.5 %collective-permute-start.45 = (bf16[32,1536]{1,0:T(8,128)(2,1)S(1)}, bf16[32,1536]{1,0:T(8,128)(2,1)S(1)}, u32[]{:S(2)}, u32[]{:S(2)}) collective-permute-start(bf16[32,1536]{1,0:T(8,128)(2,1)S(1)} %bitcast.448), channel_id=1, source_target_pairs={{0,16},{1,17},{2,18},{3,19},{4,20},{5,21},{6,22},{7,23},{8,24},{9,... | collective-permute-start | bytes 294920 | tf_op jit(solution)/shard_map/ppermute | solution.py:143
  527.3 9.1 %collective-permute-start.46 = (bf16[1,32,1536]{2,1,0:T(8,128)(2,1)S(1)}, bf16[1,32,1536]{2,1,0:T(8,128)(2,1)S(1)}, u32[]{:S(2)}, u32[]{:S(2)}) collective-permute-start(bf16[1,32,1536]{2,1,0:T(8,128)(2,1)S(1)} %constant_dynamic-slice_fusion), channel_id=1, source_target_pairs={{0,4},{1,5},{2,6},{3,7},{4,0},{5,1},{6,2},{7,3},{8,12},{9,13},{10,... | collective-permute-start | bytes 294920 | tf_op jit(solution)/shard_map/ppermute | solution.py:143
  530.1 6.3 %collective-permute-start.47 = (f32[12288]{0:T(1024)S(1)}, f32[12288]{0:T(1024)S(1)}, u32[]{:S(2)}, u32[]{:S(2)}) collective-permute-start(f32[12288]{0:T(1024)S(1)} %add.612), channel_id=1, source_target_pairs={{0,4},{1,5},{2,6},{3,7},{4,0},{5,1},{6,2},{7,3},{8,12},{9,13},{10,... | collective-permute-start | bytes 147464 | tf_op jit(solution)/shard_map/ppermute | solution.py:143
  536.5 5.3 collective-permute-start.48
  (97 other events, 624.7 us)
